TPU v7x, 128 devices: a whole 4x4x4 slice. The times are simulated.
128 devices in a mesh: dp: 2 (over y_hi), head: 8 (over z, y_lo), blk: 8 (over x, core).
Axes of the slice: x: 4, y: 4 (y_hi: 2, y_lo: 2; y = y_hi * 2 + y_lo), z: 4, core: 2. Of those that a mesh axis runs over, the one named last changes fastest.
Arguments:
- queries: bfloat16 [2048, 24576], P(('dp', 'blk', 'head')), may hold values from -60 to 60, as said below
- latent: bfloat16 [2048, 576], P(('dp', 'blk', 'head')), may hold values from -8 to 8
- key_up: bfloat16 [128, 512, 128], P('head'), may hold values from -0.25 to 0.25
- value_up: bfloat16 [128, 512, 128], P('head'), may hold values from -0.25 to 0.25
- out_grad: bfloat16 [2048, 16384], P(('dp', 'blk'), 'head'), may hold values from -6 to 6
- block_docs: int32 [2, 8], P('dp'), may hold values from 0 to 2, never falling along the last dimension, each value on 1 to 6 neighbouring positions
Outputs:
- attended: bfloat16 [2048, 16384], P(('dp', 'blk'), 'head')
- query_grad: bfloat16 [2048, 24576], P(('dp', 'blk'), 'head')
- latent_grad: float32 [2048, 576], P(('dp', 'blk', 'head'))
- key_up_grad: float32 [128, 512, 128], P('head')
- value_up_grad: float32 [128, 512, 128], P('head')
Inputs may be any that keep to these rules, and one draw needn't show every extreme that they name: `queries`: query features, heads side by side. `block_docs`: document numbers never fall along a pack; each document covers 1 to 6 blocks, one exactly 6.
All inputs are finite; a program needn't handle non-finite values.
Results may differ from a plain program's by a relative error of at most 0.033.
Values may be sent and summed in bfloat16 or wider, within the bound.
No kernel may reach another device: no remote copies, remote signals or barrier semaphores. Data moves between devices by JAX's collectives and lax.ppermute only.
A program may use at most 192 MiB of HBM per device.

v0:
```python
import jax
import jax.numpy as jnp
from jax import lax
from jax.sharding import PartitionSpec as P

NOPE = 128
ROPE = 64
LATENT = 512
VHEAD = 128
BLOCK = 128


def shifted(value, axis, steps):
    count = lax.axis_size(axis)
    initial, last = (max(0, -steps), min(count, count - steps))
    return lax.ppermute(value, axis, [(source, source + steps) for source in range(initial, last)])


def shifted_2(value, axis, steps):
    count = lax.axis_size(axis)
    pairs = [(source, (source + steps) % count) for source in range(count)]
    return lax.ppermute(value, axis, pairs)


def doc_lookup(pack_docs, positions):
    blocks = positions // BLOCK
    table = jnp.arange(pack_docs.shape[0], dtype=jnp.int32)
    return jnp.sum(jnp.where(blocks[:, None] == table[None, :], pack_docs[None, :], 0), axis=1)


def tile_mask(pack_docs, query_docs, positions, first_row, key_count):
    key_positions = first_row + jnp.arange(key_count, dtype=jnp.int32)
    key_docs = doc_lookup(pack_docs, key_positions)
    return (key_docs[None, :] == query_docs[:, None]) & (
        key_positions[None, :] <= positions[:, None]
    )


def tile_scores(query_lat, query_rotary, key_rows):
    score_scale = (NOPE + ROPE) ** (-0.5)
    partial_scores = jnp.einsum(
        "thj,kj->htk", query_lat, key_rows[:, :LATENT], preferred_element_type=jnp.float32
    )
    partial_scores = partial_scores + jnp.einsum(
        "thr,kr->htk", query_rotary, key_rows[:, LATENT:], preferred_element_type=jnp.float32
    )
    return partial_scores * score_scale


def absorb_tile(carried, query_lat, query_rotary, key_rows, allowed):
    row_top, row_total, weighted = carried
    masked = jnp.where(
        allowed[None], tile_scores(query_lat, query_rotary, key_rows), jnp.float32(-1e30)
    )
    new_top = jnp.maximum(row_top, jnp.max(masked, axis=-1))
    expo_tile = jnp.where(allowed[None], jnp.exp(masked - new_top[..., None]), jnp.float32(0.0))
    new_total = jnp.sum(expo_tile, axis=-1)
    new_weighted = jnp.einsum(
        "htk,kj->htj",
        expo_tile.astype(jnp.bfloat16),
        key_rows[:, :LATENT],
        preferred_element_type=jnp.float32,
    )
    return (new_top, new_total, new_weighted)


def tile_terms(query_lat, query_rotary, context_grad, delta, row_top, row_total, key_rows, allowed):
    score_scale = (NOPE + ROPE) ** (-0.5)
    probs = jnp.where(
        allowed[None],
        jnp.exp(tile_scores(query_lat, query_rotary, key_rows) - row_top[..., None])
        / row_total[..., None],
        jnp.float32(0.0),
    )
    prob_grad = jnp.einsum(
        "thj,kj->htk", context_grad, key_rows[:, :LATENT], preferred_element_type=jnp.float32
    )
    score_grad = (probs * (prob_grad - delta[..., None]) * score_scale).astype(jnp.bfloat16)
    latent_part = jnp.einsum(
        "htk,kj->thj", score_grad, key_rows[:, :LATENT], preferred_element_type=jnp.float32
    )
    rotary_part = jnp.einsum(
        "htk,kr->thr", score_grad, key_rows[:, LATENT:], preferred_element_type=jnp.float32
    )
    key_nope = jnp.einsum("htk,thj->kj", score_grad, query_lat, preferred_element_type=jnp.float32)
    key_nope = key_nope + jnp.einsum(
        "htk,thj->kj", probs.astype(jnp.bfloat16), context_grad, preferred_element_type=jnp.float32
    )
    key_rotary = jnp.einsum(
        "htk,thr->kr", score_grad, query_rotary, preferred_element_type=jnp.float32
    )
    return (latent_part, rotary_part, jnp.concatenate([key_nope, key_rotary], axis=1))


def start_running(heads_here, row_count):
    return (
        jnp.full((heads_here, row_count), -1e30, jnp.float32),
        jnp.zeros((heads_here, row_count), jnp.float32),
        jnp.zeros((heads_here, row_count, LATENT), jnp.float32),
    )


def forward_tail(running, value_weights, grad_heads):
    row_top, row_total, weighted = running
    context = jnp.transpose(weighted / row_total[..., None], (1, 0, 2)).astype(jnp.bfloat16)
    attended = jnp.einsum(
        "thj,hjv->thv", context, value_weights, preferred_element_type=jnp.float32
    ).astype(jnp.bfloat16)
    context_grad = jnp.einsum(
        "thv,hjv->thj", grad_heads, value_weights, preferred_element_type=jnp.float32
    ).astype(jnp.bfloat16)
    value_grad = jnp.einsum("thj,thv->hjv", context, grad_heads, preferred_element_type=jnp.float32)
    delta = jnp.transpose(
        jnp.sum(context_grad.astype(jnp.float32) * context.astype(jnp.float32), axis=-1)
    )
    return (attended, context_grad, value_grad, delta)


def backward_tail(latent_sum, rotary_sum, key_weights, query_nope):
    lat_grad = latent_sum.astype(jnp.bfloat16)
    nope_grad = jnp.einsum(
        "thj,hjn->thn", lat_grad, key_weights, preferred_element_type=jnp.float32
    )
    query_grad = jnp.concatenate([nope_grad, rotary_sum], axis=-1).astype(jnp.bfloat16)
    key_grad = jnp.einsum("thj,thn->hjn", lat_grad, query_nope, preferred_element_type=jnp.float32)
    return (query_grad, key_grad)


def on_device(queries, latent, key_up, value_up, out_grad, block_docs):
    heads_here = key_up.shape[0]
    query_dim = NOPE + ROPE
    own_keys = lax.all_gather(latent, "head", axis=0, tiled=True)
    cycle_size = lax.axis_size("blk")
    cycle_place = lax.axis_index("blk")
    pack_docs = block_docs[0]
    arrived = lax.all_to_all(queries, "head", split_axis=1, concat_axis=0, tiled=True)
    row_count = arrived.shape[0]
    arrived = arrived.reshape(row_count, heads_here, query_dim)
    query_nope = arrived[:, :, :NOPE]
    query_rotary = arrived[:, :, NOPE:]
    positions = cycle_place * row_count + jnp.arange(row_count, dtype=jnp.int32)
    query_docs = doc_lookup(pack_docs, positions)
    query_lat = jnp.einsum(
        "thn,hjn->thj", query_nope, key_up, preferred_element_type=jnp.float32
    ).astype(jnp.bfloat16)
    running = start_running(heads_here, row_count)
    key_rows = lax.all_gather(own_keys, "blk", axis=0, tiled=True)
    allowed = tile_mask(pack_docs, query_docs, positions, jnp.int32(0), key_rows.shape[0])
    running = absorb_tile(running, query_lat, query_rotary, key_rows, allowed)
    row_top, row_total = (running[0], running[1])
    grad_heads = out_grad.reshape(row_count, heads_here, VHEAD)
    attended, context_grad, value_grad, delta = forward_tail(running, value_up, grad_heads)
    attended = attended.reshape(row_count, heads_here * VHEAD)
    latent_sum = jnp.zeros((row_count, heads_here, LATENT), jnp.float32)
    rotary_sum = jnp.zeros((row_count, heads_here, ROPE), jnp.float32)
    key_rows = own_keys
    partial_sum = jnp.zeros((row_count, LATENT + ROPE), jnp.float32)
    for hop_index in range(cycle_size):
        first_row = (cycle_place - hop_index) % cycle_size * row_count
        guarded_allowed = tile_mask(pack_docs, query_docs, positions, first_row, key_rows.shape[0])
        latent_part, rotary_part, key_term = tile_terms(
            query_lat,
            query_rotary,
            context_grad,
            delta,
            row_top,
            row_total,
            key_rows,
            guarded_allowed,
        )
        latent_sum = latent_sum + latent_part
        rotary_sum = rotary_sum + rotary_part
        partial_sum = partial_sum + key_term
        if hop_index + 1 < cycle_size:
            key_rows = shifted(key_rows, "blk", 1)
        partial_sum = shifted_2(partial_sum.astype(jnp.bfloat16), "blk", 1).astype(
            partial_sum.dtype
        )
    latent_grad = lax.psum_scatter(
        partial_sum.astype(jnp.bfloat16), "head", scatter_dimension=0, tiled=True
    ).astype(jnp.float32)
    query_grad, key_grad = backward_tail(latent_sum, rotary_sum, key_up, query_nope)
    query_grad = query_grad.reshape(row_count, heads_here * query_dim)
    key_up_grad, value_up_grad = (
        lax.psum(key_grad.astype(jnp.bfloat16), ("dp", "blk")).astype(jnp.float32),
        lax.psum(value_grad.astype(jnp.bfloat16), ("dp", "blk")).astype(jnp.float32),
    )
    return (attended, query_grad, latent_grad, key_up_grad, value_up_grad)


def solution(mesh):
    return jax.shard_map(
        on_device,
        mesh=mesh,
        in_specs=(
            P(("dp", "blk", "head"), None),
            P(("dp", "blk", "head"), None),
            P("head", None, None),
            P("head", None, None),
            P(("dp", "blk"), "head"),
            P("dp", None),
        ),
        out_specs=(
            P(("dp", "blk"), "head"),
            P(("dp", "blk"), "head"),
            P(("dp", "blk", "head"), None),
            P("head", None, None),
            P("head", None, None),
        ),
        check_vma=False,
    )
```

profile of v0, /device:TPU:1, one launch (start us, length us, event | category | flops | bytes accessed | tf_op | source)
XLA Modules:
  0.0 433.7 jit_solution(4930715633861113022)
XLA Ops:
  7.2 26.7 %all_gather.6 = bf16[128,576]{1,0:T(8,128)(2,1)} all-gather(bf16[16,576]{1,0:T(8,128)(2,1)} %param.7), channel_id=1, replica_groups=mesh['dp'=2,'head'=8,'blk'=8] {'head'}, dimensions={0}, use_global_device_ids=true | all-gather | bytes 165888 | tf_op jit(solution)/shard_map/all_gather | solution.py:132
  34.0 10.0 %collective-permute-start = (bf16[128,576]{1,0:T(8,128)(2,1)}, bf16[128,576]{1,0:T(8,128)(2,1)}, u32[]{:S(2)}, u32[]{:S(2)}) collective-permute-start(bf16[128,576]{1,0:T(8,128)(2,1)} %all_gather.6), channel_id=1, source_target_pairs={{0,1},{1,2},{2,3},{3,4},{4,5},{5,6},{6,7},{8,9},{9,10},{10,11},{11... | collective-permute-start | bytes 442376 | tf_op jit(solution)/shard_map/ppermute | solution.py:16
  44.0 2.1 copy.453
  46.0 4.6 %all-to-all-start = ((bf16[16,8,3072]{2,0,1:T(8,128)(2,1)}), bf16[16,8,3072]{2,0,1:T(8,128)(2,1)S(1)}, u32[]{:S(2)}, u32[]{:S(2)}) async-start(bf16[16,8,3072]{2,0,1:T(8,128)(2,1)} %bitcast.785), calls=%async_computation | async-start | bytes 1572864 | tf_op jit(solution)/shard_map/all_to_all | solution.py:136
  53.2 2.2 collective-permute-start.1
  56.2 4.5 %collective-permute-done.1 = bf16[128,576]{1,0:T(8,128)(2,1)S(1)} collective-permute-done((bf16[128,576]{1,0:T(8,128)(2,1)}, bf16[128,576]{1,0:T(8,128)(2,1)S(1)}, u32[]{:S(2)}, u32[]{:S(2)}) %collective-permute-start.1) | collective-permute-done | bytes 147488 | tf_op jit(solution)/shard_map/ppermute | solution.py:16
  60.7 4.3 collective-permute-start.2
  65.1 2.1 collective-permute-done.2
  67.2 4.4 %collective-permute-start.3 = (bf16[128,576]{1,0:T(8,128)(2,1)S(1)}, bf16[128,576]{1,0:T(8,128)(2,1)}, u32[]{:S(2)}, u32[]{:S(2)}) collective-permute-start(bf16[128,576]{1,0:T(8,128)(2,1)S(1)} %collective-permute-done.2), channel_id=1, source_target_pairs={{0,1},{1,2},{2,3},{3,4},{4,5},{5,6},{6,7},{8,9},{9,10},{10,11},{11... | collective-permute-start | bytes 442376 | tf_op jit(solution)/shard_map/ppermute | solution.py:16
  71.8 2.0 collective-permute-done.3
  73.9 4.5 %collective-permute-start.4 = (bf16[128,576]{1,0:T(8,128)(2,1)}, bf16[128,576]{1,0:T(8,128)(2,1)}, u32[]{:S(2)}, u32[]{:S(2)}) collective-permute-start(bf16[128,576]{1,0:T(8,128)(2,1)} %collective-permute-done.3), channel_id=1, source_target_pairs={{0,1},{1,2},{2,3},{3,4},{4,5},{5,6},{6,7},{8,9},{9,10},{10,11},{11... | collective-permute-start | bytes 442376 | tf_op jit(solution)/shard_map/ppermute | solution.py:16
  78.4 2.1 reshape.720
  81.6 2.1 slice.108
  86.4 2.2 convolution_bitcast_fusion.3
  91.3 2.0 convolution_convert_fusion.2
  93.4 2.1 convolution_bitcast_fusion.6
  97.4 2.2 convolution_bitcast_fusion.2
  99.9 4.8 %collective-permute-start.6 = (bf16[128,576]{1,0:T(8,128)(2,1)S(1)}, bf16[128,576]{1,0:T(8,128)(2,1)S(1)}, u32[]{:S(2)}, u32[]{:S(2)}) collective-permute-start(bf16[128,576]{1,0:T(8,128)(2,1)S(1)} %collective-permute-done.5), channel_id=1, source_target_pairs={{0,1},{1,2},{2,3},{3,4},{4,5},{5,6},{6,7},{8,9},{9,10},{10,11},{11... | collective-permute-start | bytes 442376 | tf_op jit(solution)/shard_map/ppermute | solution.py:16
  107.8 4.4 %fusion.78 = f32[128,16,1024]{2,0,1:T(8,128)S(1)} fusion(bf16[16,512,128]{2,1,0:T(8,128)(2,1)} %convolution_convert_fusion.2, bf16[1024,576]{1,0:T(8,128)(2,1)} %all-gather.2.cloned.1.call-done), kind=kOutput, calls=%fused_computation.82 | convolution fusion | flops 2147483648 | bytes 11534336 | tf_op jit(solution)/shard_map/thj,kj->htk/dot_general | solution.py:41
  112.2 2.4 fusion.491
  114.6 2.1 fusion.2
  118.4 4.1 multiply_reduce_fusion
  124.3 2.7 fusion.479
  127.0 2.1 fusion.370
  140.8 2.1 fusion.361
  146.8 2.1 fusion.358
  163.1 2.5 collective-permute-start.7
  169.0 3.7 fusion.483
  172.7 2.7 fusion.482
  175.4 2.7 fusion.481
  178.1 3.8 fusion.480
  181.9 9.6 %add_convert_fusion = bf16[16,128,512]{2,1,0:T(8,128)(2,1)} fusion(f32[16,128,512]{2,1,0:T(8,128)S(1)} %fusion.485, f32[16,128,512]{2,1,0:T(8,128)S(1)} %fusion.484, f32[16,128,512]{2,1,0:T(8,128)} %fusion.483, f32[16,128,512]{2,1,0:T(8,128)} %fusion.482, f32[16,128,512]{2,1,0:T(8,128)} %fusion.481, f32[16,128,512]{2,1,0:T(8,128)S(1)} %copy-done.4, ...), kind=kOutput, calls=%fused_computation.9 | convolution fusion | flops 276824064 | bytes 32112640 | tf_op jit(solution)/shard_map/htk,kj->thj/dot_general | solution.py:79
  194.4 2.5 collective-permute-start.9
  199.2 2.5 collective-permute-start.10
  204.0 2.5 collective-permute-start.11
  206.8 2.1 collective-permute-done.11
  209.0 2.3 collective-permute-start.12
  211.6 3.3 collective-permute-done.12
  216.4 4.6 %collective-permute-done.13 = bf16[128,576]{1,0:T(8,128)(2,1)S(1)} collective-permute-done((bf16[128,576]{1,0:T(8,128)(2,1)S(1)}, bf16[128,576]{1,0:T(8,128)(2,1)S(1)}, u32[]{:S(2)}, u32[]{:S(2)}) %collective-permute-start.13) | collective-permute-done | bytes 147488 | tf_op jit(solution)/shard_map/ppermute | solution.py:22
  221.1 2.1 convolution_convert_fusion
  223.2 3.8 collective-permute-done.14
  227.7 3.8 fusion.80
  231.5 3.2 convolution_convert_fusion.3
  234.7 2.0 copy.339
  248.3 15.0 %reduce-scatter.2.cloned.1.call-done = bf16[16,576]{1,0:T(8,128)(2,1)} async-done(((bf16[128,576]{1,0:T(8,128)(2,1)}), bf16[16,576]{1,0:T(8,128)(2,1)}) %reduce-scatter.2.cloned.1.call-update) | async-done | bytes 18448 | tf_op jit(solution)/shard_map/reduce_scatter | solution.py:179
  264.6 155.6 %all-reduce.3.cloned.1.call-done = (bf16[16,512,128]{2,1,0:T(8,128)(2,1)}, bf16[16,512,128]{2,1,0:T(8,128)(2,1)}) async-done(((bf16[16,512,128]{2,1,0:T(8,128)(2,1)}, bf16[16,512,128]{2,1,0:T(8,128)(2,1)}), (bf16[16,512,128]{2,1,0:T(8,128)(2,1)}, bf16[16,512,128]{2,1,0:T(8,128)(2,1)})) %all-reduce.3.cloned.1.call-update) | async-done | bytes 4194320 | tf_op jit(solution)/shard_map/psum | solution.py:185
  420.1 4.2 convert_element_type.190
  424.3 2.4 convert_element_type.192
  (234 shorter events, 74.7 us)
Async XLA Ops:
  7.2 43.8 %copy-start = (bf16[16,512,128]{2,1,0:T(8,128)(2,1)S(1)}, bf16[16,512,128]{2,1,0:T(8,128)(2,1)}, u32[]{:S(2)}) copy-start(bf16[16,512,128]{2,1,0:T(8,128)(2,1)} %param.9) | copy-start | bytes 6291460
  7.2 43.8 %copy-start.29 = (bf16[128,2048]{1,0:T(8,128)(2,1)S(1)}, bf16[128,2048]{1,0:T(8,128)(2,1)}, u32[]{:S(2)}) copy-start(bf16[128,2048]{1,0:T(8,128)(2,1)} %param.10) | copy-start | bytes 1572868
  7.2 100.6 %all-gather.2.cloned.1.call-start = ((), (), s32[]{:S(2)}) async-start(), calls=%async_computation.2 | async-start | bytes 1474560 | tf_op jit(solution)/shard_map/all_gather | solution.py:147
  34.0 19.2 %collective-permute-start = (bf16[128,576]{1,0:T(8,128)(2,1)}, bf16[128,576]{1,0:T(8,128)(2,1)}, u32[]{:S(2)}, u32[]{:S(2)}) collective-permute-start(bf16[128,576]{1,0:T(8,128)(2,1)} %all_gather.6), channel_id=1, source_target_pairs={{0,1},{1,2},{2,3},{3,4},{4,5},{5,6},{6,7},{8,9},{9,10},{10,11},{11... | collective-permute-start | bytes 442376 | tf_op jit(solution)/shard_map/ppermute | solution.py:16
  46.0 32.3 %all-to-all-start = ((bf16[16,8,3072]{2,0,1:T(8,128)(2,1)}), bf16[16,8,3072]{2,0,1:T(8,128)(2,1)S(1)}, u32[]{:S(2)}, u32[]{:S(2)}) async-start(bf16[16,8,3072]{2,0,1:T(8,128)(2,1)} %bitcast.785), calls=%async_computation | async-start | bytes 1572864 | tf_op jit(solution)/shard_map/all_to_all | solution.py:136
  50.7 212.6 %reduce-scatter.2.cloned.1.call-start = ((), (), s32[]{:S(2)}) async-start(), calls=%async_computation.3 | async-start | bytes 184320 | tf_op jit(solution)/shard_map/reduce_scatter | solution.py:179
  53.2 7.5 %collective-permute-start.1 = (bf16[128,576]{1,0:T(8,128)(2,1)}, bf16[128,576]{1,0:T(8,128)(2,1)S(1)}, u32[]{:S(2)}, u32[]{:S(2)}) collective-permute-start(bf16[128,576]{1,0:T(8,128)(2,1)} %collective-permute-done), channel_id=1, source_target_pairs={{0,1},{1,2},{2,3},{3,4},{4,5},{5,6},{6,7},{8,9},{9,10},{10,11},{11... | collective-permute-start | bytes 442376 | tf_op jit(solution)/shard_map/ppermute | solution.py:16
  60.7 29.3 %copy-start.49 = (bf16[128,576]{1,0:T(8,128)(2,1)}, bf16[128,576]{1,0:T(8,128)(2,1)S(1)}, u32[]{:S(2)}) copy-start(bf16[128,576]{1,0:T(8,128)(2,1)S(1)} %collective-permute-done.1) | copy-start | bytes 442372
  60.7 6.5 %collective-permute-start.2 = (bf16[128,576]{1,0:T(8,128)(2,1)S(1)}, bf16[128,576]{1,0:T(8,128)(2,1)S(1)}, u32[]{:S(2)}, u32[]{:S(2)}) collective-permute-start(bf16[128,576]{1,0:T(8,128)(2,1)S(1)} %collective-permute-done.1), channel_id=1, source_target_pairs={{0,1},{1,2},{2,3},{3,4},{4,5},{5,6},{6,7},{8,9},{9,10},{10,11},{11... | collective-permute-start | bytes 442376 | tf_op jit(solution)/shard_map/ppermute | solution.py:16
  67.2 21.5 %copy-start.52 = (bf16[128,576]{1,0:T(8,128)(2,1)}, bf16[128,576]{1,0:T(8,128)(2,1)S(1)}, u32[]{:S(2)}) copy-start(bf16[128,576]{1,0:T(8,128)(2,1)S(1)} %collective-permute-done.2) | copy-start | bytes 442372
  67.2 6.6 %collective-permute-start.3 = (bf16[128,576]{1,0:T(8,128)(2,1)S(1)}, bf16[128,576]{1,0:T(8,128)(2,1)}, u32[]{:S(2)}, u32[]{:S(2)}) collective-permute-start(bf16[128,576]{1,0:T(8,128)(2,1)S(1)} %collective-permute-done.2), channel_id=1, source_target_pairs={{0,1},{1,2},{2,3},{3,4},{4,5},{5,6},{6,7},{8,9},{9,10},{10,11},{11... | collective-permute-start | bytes 442376 | tf_op jit(solution)/shard_map/ppermute | solution.py:16
  73.9 21.6 %collective-permute-start.4 = (bf16[128,576]{1,0:T(8,128)(2,1)}, bf16[128,576]{1,0:T(8,128)(2,1)}, u32[]{:S(2)}, u32[]{:S(2)}) collective-permute-start(bf16[128,576]{1,0:T(8,128)(2,1)} %collective-permute-done.3), channel_id=1, source_target_pairs={{0,1},{1,2},{2,3},{3,4},{4,5},{5,6},{6,7},{8,9},{9,10},{10,11},{11... | collective-permute-start | bytes 442376 | tf_op jit(solution)/shard_map/ppermute | solution.py:16
  78.4 6.7 %copy-start.26 = (bf16[128,576]{1,0:T(8,128)(2,1)S(1)}, bf16[128,576]{1,0:T(8,128)(2,1)}, u32[]{:S(2)}) copy-start(bf16[128,576]{1,0:T(8,128)(2,1)} %all_gather.6) | copy-start | bytes 442372
  81.6 9.8 %copy-start.25 = (bf16[128,16,128]{2,1,0:T(8,128)(2,1)}, bf16[128,16,128]{2,1,0:T(8,128)(2,1)S(1)}, u32[]{:S(2)}) copy-start(bf16[128,16,128]{2,1,0:T(8,128)(2,1)S(1)} %slice.105) | copy-start | bytes 1572868
  86.4 4.9 %copy-start.22 = (bf16[16,512,128]{2,1,0:T(8,128)(2,1)S(1)}, bf16[16,512,128]{2,1,0:T(8,128)(2,1)}, u32[]{:S(2)}) copy-start(bf16[16,512,128]{2,1,0:T(8,128)(2,1)} %param.8) | copy-start | bytes 6291460
  95.4 4.5 %collective-permute-start.5 = (bf16[128,576]{1,0:T(8,128)(2,1)}, bf16[128,576]{1,0:T(8,128)(2,1)S(1)}, u32[]{:S(2)}, u32[]{:S(2)}) collective-permute-start(bf16[128,576]{1,0:T(8,128)(2,1)} %collective-permute-done.4), channel_id=1, source_target_pairs={{0,1},{1,2},{2,3},{3,4},{4,5},{5,6},{6,7},{8,9},{9,10},{10,11},{11... | collective-permute-start | bytes 442376 | tf_op jit(solution)/shard_map/ppermute | solution.py:16
  99.9 12.3 %copy-start.55 = (bf16[128,576]{1,0:T(8,128)(2,1)}, bf16[128,576]{1,0:T(8,128)(2,1)S(1)}, u32[]{:S(2)}) copy-start(bf16[128,576]{1,0:T(8,128)(2,1)S(1)} %collective-permute-done.5) | copy-start | bytes 442372
  99.9 6.5 %collective-permute-start.6 = (bf16[128,576]{1,0:T(8,128)(2,1)S(1)}, bf16[128,576]{1,0:T(8,128)(2,1)S(1)}, u32[]{:S(2)}, u32[]{:S(2)}) collective-permute-start(bf16[128,576]{1,0:T(8,128)(2,1)S(1)} %collective-permute-done.5), channel_id=1, source_target_pairs={{0,1},{1,2},{2,3},{3,4},{4,5},{5,6},{6,7},{8,9},{9,10},{10,11},{11... | collective-permute-start | bytes 442376 | tf_op jit(solution)/shard_map/ppermute | solution.py:16
  106.4 5.8 %copy-start.46 = (bf16[128,576]{1,0:T(8,128)(2,1)}, bf16[128,576]{1,0:T(8,128)(2,1)S(1)}, u32[]{:S(2)}) copy-start(bf16[128,576]{1,0:T(8,128)(2,1)S(1)} %collective-permute-done.6) | copy-start | bytes 442372
  107.8 4.4 %copy-start.58 = (bf16[1024,576]{1,0:T(8,128)(2,1)S(1)}, bf16[1024,576]{1,0:T(8,128)(2,1)}, u32[]{:S(2)}) copy-start(bf16[1024,576]{1,0:T(8,128)(2,1)} %all-gather.2.cloned.1.call-done) | copy-start | bytes 3538948
  118.4 4.1 copy-start.27
  163.1 4.2 copy-start.17
  163.1 28.8 %collective-permute-start.7 = (bf16[128,576]{1,0:T(8,128)(2,1)}, bf16[128,576]{1,0:T(8,128)(2,1)S(1)}, u32[]{:S(2)}, u32[]{:S(2)}) collective-permute-start(bf16[128,576]{1,0:T(8,128)(2,1)} %pad_maximum_fusion.1), channel_id=1, source_target_pairs={{0,1},{1,2},{2,3},{3,4},{4,5},{5,6},{6,7},{7,0},{8,9},{9,10},{10,1... | collective-permute-start | bytes 442376 | tf_op jit(solution)/shard_map/ppermute | solution.py:22
  169.0 3.7 copy-start.11
  169.0 3.7 copy-start.54
  178.1 3.8 copy-start.4
  178.1 3.8 copy-start.48
  181.9 10.0 %copy-start.37 = (f32[128,512]{1,0:T(8,128)S(1)}, f32[128,512]{1,0:T(8,128)}, u32[]{:S(2)}) copy-start(f32[128,512]{1,0:T(8,128)} %fusion.447) | copy-start | bytes 786436
  191.5 7.6 %copy-start.35 = (f32[128,512]{1,0:T(8,128)S(1)}, f32[128,512]{1,0:T(8,128)}, u32[]{:S(2)}) copy-start(f32[128,512]{1,0:T(8,128)} %fusion.441) | copy-start | bytes 786436
  191.9 12.0 %copy-start.34 = (f32[128,512]{1,0:T(8,128)S(1)}, f32[128,512]{1,0:T(8,128)}, u32[]{:S(2)}) copy-start(f32[128,512]{1,0:T(8,128)} %fusion.438) | copy-start | bytes 786436
  192.0 2.3 collective-permute-start.8
  192.4 16.6 %copy-start.33 = (f32[128,512]{1,0:T(8,128)S(1)}, f32[128,512]{1,0:T(8,128)}, u32[]{:S(2)}) copy-start(f32[128,512]{1,0:T(8,128)} %fusion.435) | copy-start | bytes 786436
  194.3 16.9 %copy-start.20 = (bf16[16,128,128]{2,1,0:T(8,128)(2,1)S(1)}, bf16[16,128,128]{2,1,0:T(8,128)(2,1)}, u32[]{:S(2)}) copy-start(bf16[16,128,128]{2,1,0:T(8,128)(2,1)} %copy-done.19) | copy-start | bytes 1572868
  194.4 4.8 %collective-permute-start.9 = (bf16[128,576]{1,0:T(8,128)(2,1)S(1)}, bf16[128,576]{1,0:T(8,128)(2,1)S(1)}, u32[]{:S(2)}, u32[]{:S(2)}) collective-permute-start(bf16[128,576]{1,0:T(8,128)(2,1)S(1)} %fusion.473), channel_id=1, source_target_pairs={{0,1},{1,2},{2,3},{3,4},{4,5},{5,6},{6,7},{7,0},{8,9},{9,10},{10,1... | collective-permute-start | bytes 442376 | tf_op jit(solution)/shard_map/ppermute | solution.py:22
  197.2 17.8 %copy-start.32 = (f32[128,512]{1,0:T(8,128)S(1)}, f32[128,512]{1,0:T(8,128)}, u32[]{:S(2)}) copy-start(f32[128,512]{1,0:T(8,128)} %fusion.432) | copy-start | bytes 786436
  199.2 4.8 %collective-permute-start.10 = (bf16[128,576]{1,0:T(8,128)(2,1)S(1)}, bf16[128,576]{1,0:T(8,128)(2,1)S(1)}, u32[]{:S(2)}, u32[]{:S(2)}) collective-permute-start(bf16[128,576]{1,0:T(8,128)(2,1)S(1)} %fusion.474), channel_id=1, source_target_pairs={{0,1},{1,2},{2,3},{3,4},{4,5},{5,6},{6,7},{7,0},{8,9},{9,10},{10,1... | collective-permute-start | bytes 442376 | tf_op jit(solution)/shard_map/ppermute | solution.py:22
  202.0 19.0 %copy-start.31 = (f32[128,512]{1,0:T(8,128)S(1)}, f32[128,512]{1,0:T(8,128)}, u32[]{:S(2)}) copy-start(f32[128,512]{1,0:T(8,128)} %fusion.429) | copy-start | bytes 786436
  204.0 17.1 %copy-start.24 = (bf16[128,16,512]{2,0,1:T(8,128)(2,1)S(1)}, bf16[128,16,512]{2,0,1:T(8,128)(2,1)}, u32[]{:S(2)}) copy-start(bf16[128,16,512]{2,0,1:T(8,128)(2,1)} %get-tuple-element.47) | copy-start | bytes 6291460
  204.0 17.1 %copy-start.30 = (bf16[128,2048]{1,0:T(8,128)(2,1)S(1)}, bf16[128,2048]{1,0:T(8,128)(2,1)}, u32[]{:S(2)}) copy-start(bf16[128,2048]{1,0:T(8,128)(2,1)} %param.10) | copy-start | bytes 1572868
  204.0 5.0 %collective-permute-start.11 = (bf16[128,576]{1,0:T(8,128)(2,1)S(1)}, bf16[128,576]{1,0:T(8,128)(2,1)S(1)}, u32[]{:S(2)}, u32[]{:S(2)}) collective-permute-start(bf16[128,576]{1,0:T(8,128)(2,1)S(1)} %fusion.475), channel_id=1, source_target_pairs={{0,1},{1,2},{2,3},{3,4},{4,5},{5,6},{6,7},{7,0},{8,9},{9,10},{10,1... | collective-permute-start | bytes 442376 | tf_op jit(solution)/shard_map/ppermute | solution.py:22
  209.0 6.0 %collective-permute-start.12 = (bf16[128,576]{1,0:T(8,128)(2,1)S(1)}, bf16[128,576]{1,0:T(8,128)(2,1)S(1)}, u32[]{:S(2)}, u32[]{:S(2)}) collective-permute-start(bf16[128,576]{1,0:T(8,128)(2,1)S(1)} %fusion.476), channel_id=1, source_target_pairs={{0,1},{1,2},{2,3},{3,4},{4,5},{5,6},{6,7},{7,0},{8,9},{9,10},{10,1... | collective-permute-start | bytes 442376 | tf_op jit(solution)/shard_map/ppermute | solution.py:22
  215.0 6.0 %collective-permute-start.13 = (bf16[128,576]{1,0:T(8,128)(2,1)S(1)}, bf16[128,576]{1,0:T(8,128)(2,1)S(1)}, u32[]{:S(2)}, u32[]{:S(2)}) collective-permute-start(bf16[128,576]{1,0:T(8,128)(2,1)S(1)} %fusion.477), channel_id=1, source_target_pairs={{0,1},{1,2},{2,3},{3,4},{4,5},{5,6},{6,7},{7,0},{8,9},{9,10},{10,1... | collective-permute-start | bytes 442376 | tf_op jit(solution)/shard_map/ppermute | solution.py:22
  221.0 6.0 %collective-permute-start.14 = (bf16[128,576]{1,0:T(8,128)(2,1)S(1)}, bf16[128,576]{1,0:T(8,128)(2,1)S(1)}, u32[]{:S(2)}, u32[]{:S(2)}) collective-permute-start(bf16[128,576]{1,0:T(8,128)(2,1)S(1)} %fusion.478), channel_id=1, source_target_pairs={{0,1},{1,2},{2,3},{3,4},{4,5},{5,6},{6,7},{7,0},{8,9},{9,10},{10,1... | collective-permute-start | bytes 442376 | tf_op jit(solution)/shard_map/ppermute | solution.py:22
  227.7 192.5 %all-reduce.3.cloned.1.call-start = ((), (), s32[]{:S(2)}) async-start(), calls=%async_computation.4 | async-start | bytes 8388608 | tf_op jit(solution)/shard_map/psum | solution.py:185
  236.7 3.8 copy-start.12
  237.9 3.8 copy-start.15
  240.5 3.5 copy-start.21
  420.1 4.2 copy-start.28
  (36 other events, 69.7 us)
Sparse Core Ops, SparseCore 0:
  34.1 31.4 all-gather.1
  227.8 35.4 reduce-scatter.1
  266.5 153.5 all-reduce.2
where the time goes:
time: 440 us; the launch traced here: 434 us
  waiting for transfers between devices  200 us (45%)
  matrix products  115 us (26%)
  starting transfers between devices  50.2 us (11%)
  blocking collectives  26.7 us (6%)
  between operations  15.4 us (4%)
  local copies, waits for them, and re-layouts  14.1 us (3%)
  other arithmetic  13.2 us (3%)
    psum x1, waiting for transfers between devices, on_device(): lax.psum(key_grad.astype(jnp.bfloat16), ('dp', 'blk')).astype(jnp.float32)  156 us
    ppermute x7, starting transfers between devices, shifted(): lax.ppermute(value, axis, [(source, source + steps) for source in range(i...  32 us
    dot_general x8, matrix products, tile_terms(): jnp.einsum('htk,kj->thj', score_grad, key_rows[:, :LATENT], preferred_ele...  28.6 us
    all_gather x1, blocking collectives, on_device(): own_keys = lax.all_gather(latent, 'head', axis=0, tiled=True)  26.7 us
    ppermute x8, waiting for transfers between devices, shifted_2(): return lax.ppermute(value, axis, pairs)  19.6 us
    dot_general x9, matrix products, tile_scores(): jnp.einsum('thj,kj->htk', query_lat, key_rows[:, :LATENT], preferred_elem...  16.5 us
    dot_general x9, matrix products, tile_scores(): jnp.einsum('thr,kr->htk', query_rotary, key_rows[:, LATENT:], preferred_e...  15.5 us
    reduce_scatter x1, waiting for transfers between devices, on_device(): lax.psum_scatter(partial_sum.astype(jnp.bfloat16), 'head', scatter_dimens...  15 us
  transfers between devices with their start and end apart: 19, of which 14 were waited for; matrix products, arithmetic and copies ran while one was open for 18% of the time, Pallas kernels for 0%

commit v1 on v0

v1 whole, which is shorter than its diff:
```python
import functools

import jax
import jax.numpy as jnp
from jax import lax
from jax.experimental import pallas as pl
from jax.experimental.pallas import tpu as pltpu
from jax.sharding import Mesh
from jax.sharding import PartitionSpec as P

NOPE = 128
ROPE = 64
LATENT = 512
VHEAD = 128
BLOCK = 128
QUERY = NOPE + ROPE
KEY = LATENT + ROPE
DOC_MOST = 6
WINDOW = DOC_MOST * BLOCK
PAIR = 2
ROWS = PAIR * BLOCK
SCALE = QUERY ** -0.5

bf16 = jnp.bfloat16
f32 = jnp.float32


def mul(a, b, dims=((1,), (0,))):
    return lax.dot_general(a, b, (dims, ((), ())), preferred_element_type=f32)


NT = ((1,), (1,))
TN = ((0,), (0,))


def attention_kernel(
    place, query_ref, own_ref, other_ref, key_ref, value_ref, grad_ref,
    attended_ref, query_grad_ref, kv_ref, keep_ref, send_ref,
    keys, flipped, bias, total,
):
    step = pl.program_id(0)
    core, first, doc_first, block = place[0], place[1], place[2], place[3]
    n_x = own_ref.shape[0]

    @pl.when(step == 0)
    def _():
        for x in range(n_x):
            keys[pl.ds(pl.multiple_of((2 * x + core) * BLOCK, BLOCK), BLOCK), :] = own_ref[x]
            keys[pl.ds(pl.multiple_of((2 * x + 1 - core) * BLOCK, BLOCK), BLOCK), :] = other_ref[x]
        window = keys[pl.ds(pl.multiple_of(first * BLOCK, BLOCK), WINDOW), :]
        flipped[:LATENT, :] = jnp.transpose(window[:, :LATENT])
        flipped[LATENT:, :] = jnp.transpose(window[:, LATENT:])
        key_at = first * BLOCK + lax.broadcasted_iota(jnp.int32, (WINDOW, ROWS), 0)
        query_at = block * BLOCK + lax.broadcasted_iota(jnp.int32, (WINDOW, ROWS), 1) % BLOCK
        seen = (key_at >= doc_first * BLOCK) & (key_at <= query_at)
        bias[...] = jnp.where(seen, f32(0.0), f32(-1e30))
        total[...] = jnp.zeros_like(total)

    window = keys.at[pl.ds(pl.multiple_of(first * BLOCK, BLOCK), WINDOW), :]
    latents = window[:, :LATENT]
    rotary = window[:, LATENT:]
    queries = query_ref[...].reshape(BLOCK, PAIR * QUERY)
    nope = [queries[:, e * QUERY:e * QUERY + NOPE] for e in range(PAIR)]
    turned = jnp.concatenate([queries[:, e * QUERY + NOPE:(e + 1) * QUERY] for e in range(PAIR)], axis=0)
    grads = [grad_ref[:, e * VHEAD:(e + 1) * VHEAD] for e in range(PAIR)]
    query_lat = jnp.concatenate([mul(key_ref[e], nope[e], NT) for e in range(PAIR)], axis=1).astype(bf16)
    context_grad = jnp.concatenate([mul(value_ref[e], grads[e], NT) for e in range(PAIR)], axis=1).astype(bf16)

    scores = (mul(latents, query_lat) + mul(rotary, turned, NT)) * SCALE + bias[...]
    top = jnp.max(scores, axis=0, keepdims=True)
    expo = jnp.exp(scores - top)
    inverse = 1.0 / jnp.sum(expo, axis=0, keepdims=True)
    context = (mul(flipped[:LATENT, :], expo.astype(bf16)) * inverse).astype(bf16)
    delta = jnp.sum(context.astype(f32) * context_grad.astype(f32), axis=0, keepdims=True)
    probs = expo * inverse
    score_grad = (probs * (mul(latents, context_grad) - delta) * SCALE).astype(bf16)
    low = probs.astype(bf16)
    lat_grad = mul(flipped[...], score_grad)
    turned_grad = lat_grad[LATENT:, :]
    lat_grad = lat_grad[:LATENT, :].astype(bf16)

    out = total.at[pl.ds(pl.multiple_of(first * BLOCK, BLOCK), WINDOW), :]
    out[:, :LATENT] += mul(score_grad, query_lat, NT) + mul(low, context_grad, NT)
    out[:, LATENT:] += mul(score_grad, turned)

    pieces = []
    for e in range(PAIR):
        at = slice(e * BLOCK, (e + 1) * BLOCK)
        attended_ref[:, e * VHEAD:(e + 1) * VHEAD] = mul(context[:, at], value_ref[e], TN).astype(bf16)
        pieces.append(mul(lat_grad[:, at], key_ref[e], TN))
        pieces.append(jnp.transpose(turned_grad[:, at]))
        kv_ref[e, :, :NOPE] = mul(lat_grad[:, at], nope[e]).astype(bf16)
        kv_ref[e, :, NOPE:] = mul(context[:, at], grads[e]).astype(bf16)
    query_grad_ref[...] = jnp.concatenate(pieces, axis=1).astype(bf16)

    @pl.when(step == pl.num_programs(0) - 1)
    def _():
        for x in range(n_x):
            keep_ref[x] = total[pl.ds(pl.multiple_of((2 * x + core) * BLOCK, BLOCK), BLOCK), :].astype(bf16)
            send_ref[x] = total[pl.ds(pl.multiple_of((2 * x + 1 - core) * BLOCK, BLOCK), BLOCK), :].astype(bf16)


def attention(place, arrived, own, other, key_up, value_up, out_grad):
    heads = key_up.shape[0]
    steps = heads // PAIR
    n_x = own.shape[0]
    tokens = 2 * n_x * BLOCK

    def turn(i, place):
        return lax.rem(i + (1 - place[0]) * (steps // 2), steps)

    whole = lambda shape: pl.BlockSpec(shape, lambda i, place: (0,) * len(shape))
    return pl.pallas_call(
        attention_kernel,
        grid_spec=pltpu.PrefetchScalarGridSpec(
            num_scalar_prefetch=1,
            grid=(steps,),
            in_specs=[
                pl.BlockSpec((BLOCK, PAIR * QUERY), lambda i, place: (0, turn(i, place))),
                whole(own.shape),
                whole(other.shape),
                pl.BlockSpec((PAIR, LATENT, NOPE), lambda i, place: (turn(i, place), 0, 0)),
                pl.BlockSpec((PAIR, LATENT, VHEAD), lambda i, place: (turn(i, place), 0, 0)),
                pl.BlockSpec((BLOCK, PAIR * VHEAD), lambda i, place: (0, turn(i, place))),
            ],
            out_specs=[
                pl.BlockSpec((BLOCK, PAIR * VHEAD), lambda i, place: (0, turn(i, place))),
                pl.BlockSpec((BLOCK, PAIR * QUERY), lambda i, place: (0, turn(i, place))),
                pl.BlockSpec((PAIR, LATENT, NOPE + VHEAD), lambda i, place: (i, 0, 0)),
                whole(own.shape),
                whole(own.shape),
            ],
            scratch_shapes=[
                pltpu.VMEM((tokens, KEY), bf16),
                pltpu.VMEM((KEY, WINDOW), bf16),
                pltpu.VMEM((WINDOW, ROWS), f32),
                pltpu.VMEM((tokens, KEY), f32),
            ],
        ),
        out_shape=[
            jax.ShapeDtypeStruct((BLOCK, heads * VHEAD), bf16),
            jax.ShapeDtypeStruct((BLOCK, heads * QUERY), bf16),
            jax.ShapeDtypeStruct((heads, LATENT, NOPE + VHEAD), bf16),
            jax.ShapeDtypeStruct(own.shape, bf16),
            jax.ShapeDtypeStruct(own.shape, bf16),
        ],
        compiler_params=pltpu.CompilerParams(
            dimension_semantics=("arbitrary",), vmem_limit_bytes=48 * 1024 * 1024
        ),
        cost_estimate=pl.CostEstimate(
            flops=12_000_000_000, bytes_accessed=15_000_000, transcendentals=2_000_000
        ),
    )(place, arrived, own, other, key_up, value_up, out_grad)


def swapped(value):
    return lax.ppermute(value, "core", [(0, 1), (1, 0)])


def spread(value, axes):
    count = lax.axis_size(axes)
    return lax.all_to_all(
        jnp.broadcast_to(value[None], (count,) + value.shape), axes, 0, 0, tiled=True
    )


def on_device(queries, latent, key_up, value_up, out_grad, block_docs):
    heads = key_up.shape[0]
    n_head = lax.axis_size(("z", "y"))
    n_x = lax.axis_size("x")
    core = lax.axis_index("core")
    block = lax.axis_index("x") * 2 + core
    docs = block_docs[0]
    doc_first = jnp.sum((docs < docs[block]).astype(jnp.int32))
    first = jnp.maximum(block - (DOC_MOST - 1), 0)
    place = jnp.stack([core, first, doc_first, block]).astype(jnp.int32)

    rows = queries.shape[0]
    packed = jnp.concatenate(
        [
            queries.reshape(rows, n_head, heads * QUERY),
            jnp.broadcast_to(latent[:, None, :], (rows, n_head, KEY)),
        ],
        axis=2,
    )
    arrived = lax.all_to_all(packed, ("z", "y"), split_axis=1, concat_axis=0, tiled=False)
    arrived = arrived.reshape(rows * n_head, heads * QUERY + KEY)
    own = spread(arrived[:, heads * QUERY:], "x")
    other = swapped(own)

    attended, query_grad, kv, keep, send = attention(
        place, arrived, own, other, key_up, value_up, out_grad
    )

    half = heads // 2
    kv = (kv[half:].astype(f32) + swapped(kv[:half]).astype(f32)).astype(bf16)
    keep = (keep.astype(f32) + swapped(send).astype(f32)).astype(bf16)
    keep = lax.all_to_all(
        keep.reshape(n_x * n_head, rows, KEY), ("x", "z", "y"), 0, 0, tiled=True
    )
    latent_grad = jnp.sum(keep.astype(f32), axis=0)
    kv = lax.all_to_all(kv, ("dp", "x"), 0, 0, tiled=True)
    kv = jnp.sum(kv.astype(f32), axis=0).astype(bf16)
    mine = spread(kv, ("dp", "x"))
    others = swapped(mine)
    low = jnp.where(core == 0, mine, others)
    high = jnp.where(core == 0, others, mine)
    kv = jnp.concatenate([low, high], axis=0).astype(f32)
    return (attended, query_grad, latent_grad, kv[:, :, :NOPE], kv[:, :, NOPE:])


def solution(mesh):
    n_dp, n_head, n_blk = mesh.devices.shape
    fine = Mesh(
        mesh.devices.reshape(n_dp, n_head // 2, 2, n_blk // 2, 2), ("dp", "z", "y", "x", "core")
    )
    head, blk = ("z", "y"), ("x", "core")
    return jax.shard_map(
        on_device,
        mesh=fine,
        in_specs=(
            P(("dp",) + blk + head, None),
            P(("dp",) + blk + head, None),
            P(head, None, None),
            P(head, None, None),
            P(("dp",) + blk, head),
            P("dp", None),
        ),
        out_specs=(
            P(("dp",) + blk, head),
            P(("dp",) + blk, head),
            P(("dp",) + blk + head, None),
            P(head, None, None),
            P(head, None, None),
        ),
        check_vma=False,
    )
```

time: 440 us -> 179 us (0.41); the launches traced: 434 us -> 178 us
  waiting for transfers between devices: 200 us -> 21.1 us
  matrix products: 115 us -> 0 us
  blocking collectives: 26.7 us -> 96.3 us
  starting transfers between devices: 50.2 us -> 8.91 us
  Pallas kernels: 0 us -> 28.2 us
  between operations: 15.4 us -> 0.81 us
    psum x1 -> x0, waiting for transfers between devices: 156 us -> none  [on_device(): lax.psum(key_grad.astype(jnp.bfloat16), ('dp', 'blk')).astype(jnp.float32)]
    dot_general x73 -> x0, matrix products: 115 us -> none  [the longest x8 28.6 us: tile_terms(): jnp.einsum('htk,kj->thj', score_grad, key_rows[:, :LATENT], preferred_ele...]
    all_to_all x0 -> x4, blocking collectives: none -> 96.3 us  [the longest x2 42.8 us: spread(): lax.all_to_all(jnp.broadcast_to(value[None], (count,) + value.shape), axe...]
    ppermute x15 -> x4, starting transfers between devices: 45.4 us -> 5.01 us  [swapped(): return lax.ppermute(value, 'core', [(0, 1), (1, 0)])]
    pallas_call x0 -> x1, Pallas kernels: none -> 28.2 us  [attention(): pl.pallas_call(attention_kernel, grid_spec=pltpu.PrefetchScalarGridSpec(n...]
    all_gather x1 -> x0, blocking collectives: 26.7 us -> none  [on_device(): own_keys = lax.all_gather(latent, 'head', axis=0, tiled=True)]
    ppermute x15 -> x4, waiting for transfers between devices: 29 us -> 8.37 us  [swapped(): return lax.ppermute(value, 'core', [(0, 1), (1, 0)])]
    reduce_scatter x1 -> x0, waiting for transfers between devices: 15 us -> none  [on_device(): lax.psum_scatter(partial_sum.astype(jnp.bfloat16), 'head', scatter_dimens...]
  transfers between devices with their start and end apart: 19 -> 5, of which waited for: 14 -> 3; matrix products, arithmetic and copies ran while one was open for 18% -> 3% of each run, Pallas kernels for 0% -> 0%
where the time goes in v1:
time: 179 us; the launch traced here: 178 us
  blocking collectives  96.3 us (54%)
  Pallas kernels  28.2 us (16%)
  waiting for transfers between devices  21.1 us (12%)
  local copies, waits for them, and re-layouts  13.7 us (8%)
  other arithmetic  9.31 us (5%)
  starting transfers between devices  8.91 us (5%)
    all_to_all x2, blocking collectives, spread(): lax.all_to_all(jnp.broadcast_to(value[None], (count,) + value.shape), axe...  42.8 us
    all_to_all x1, blocking collectives, on_device(): kv = lax.all_to_all(kv, ('dp', 'x'), 0, 0, tiled=True)  33 us
    pallas_call x1, Pallas kernels, attention(): pl.pallas_call(attention_kernel, grid_spec=pltpu.PrefetchScalarGridSpec(n...  28.2 us
    all_to_all x1, blocking collectives, on_device(): lax.all_to_all(packed, ('z', 'y'), split_axis=1, concat_axis=0, tiled=False)  20.5 us
    all_to_all x1, waiting for transfers between devices, on_device(): lax.all_to_all(keep.reshape(n_x * n_head, rows, KEY), ('x', 'z', 'y'), 0,...  12.8 us
    ppermute x4, waiting for transfers between devices, swapped(): return lax.ppermute(value, 'core', [(0, 1), (1, 0)])  8.37 us
    ppermute x4, starting transfers between devices, swapped(): return lax.ppermute(value, 'core', [(0, 1), (1, 0)])  5.01 us
    slice x1, local copies, waits for them, and re-layouts, on_device(): return (attended, query_grad, latent_grad, kv[:, :, :NOPE], kv[:, :, NOPE:])  4.45 us
  transfers between devices with their start and end apart: 5, of which 3 were waited for; matrix products, arithmetic and copies ran while one was open for 3% of the time, Pallas kernels for 0%

profile of v1, /device:TPU:1, one launch (start us, length us, event | category | flops | bytes accessed | tf_op | source)
XLA Modules:
  0.0 178.4 jit_solution(10940444142994243132)
XLA Ops:
  0.6 1.6 copy.23
  2.2 0.7 broadcast_in_dim.8
  3.0 0.1 maximum_bitcast_fusion
  3.0 0.1 copy.17
  3.1 0.0 copy-start.5
  3.1 20.5 %all_to_all.35 = bf16[1,16,8,3648]{3,1,0,2:T(8,128)(2,1)S(1)} all-to-all(bf16[1,16,8,3648]{3,1,0,2:T(8,128)(2,1)S(1)} %copy.17), channel_id=1, replica_groups=mesh['dp'=2,'z'=4,'y'=2,'x'=4,'core'=2] {'z','y'}, dimensions={2} | all-to-all | bytes 1867776 | tf_op jit(solution)/shard_map/all_to_all | solution.py:186
  23.6 0.1 copy.18
  23.8 0.0 copy-start.3
  23.8 0.1 broadcast_in_dim.10
  23.9 12.0 %all_to_all.36 = bf16[4,128,576]{1,2,0:T(8,128)(2,1)S(1)} all-to-all(bf16[4,128,576]{1,2,0:T(8,128)(2,1)S(1)} %broadcast_in_dim.10), channel_id=1, replica_groups=mesh['dp'=2,'z'=4,'y'=2,'x'=4,'core'=2] {'x'}, dimensions={0} | all-to-all | bytes 1179648 | tf_op jit(solution)/shard_map/all_to_all | solution.py:162
  35.9 3.1 %collective-permute-start = (bf16[4,128,576]{1,2,0:T(8,128)(2,1)S(1)}, bf16[4,128,576]{1,2,0:T(8,128)(2,1)}, u32[]{:S(2)}, u32[]{:S(2)}) collective-permute-start(bf16[4,128,576]{1,2,0:T(8,128)(2,1)S(1)} %all_to_all.36), channel_id=1, source_target_pairs={{0,1},{1,0},{2,3},{3,2},{4,5},{5,4},{6,7},{7,6},{8,9},{9,8},{10,11... | collective-permute-start | bytes 1769480 | tf_op jit(solution)/shard_map/ppermute | solution.py:157
  39.0 0.0 copy-done.5
  39.0 0.6 constant_dynamic-slice_fusion
  39.5 1.3 fusion
  40.8 0.7 pad_add_fusion.place
  41.5 0.3 copy.19.own_ref
  41.9 0.0 collective-permute-done
  41.9 1.4 copy.20.other_ref
  43.2 0.0 copy-done.3
  43.2 0.0 copy-start.2
  43.3 1.6 copy-done.2
  44.8 28.2 %shard_map.101 = (bf16[128,2048]{1,0:T(8,128)(2,1)}, bf16[128,3072]{1,0:T(8,128)(2,1)}, bf16[16,512,256]{2,1,0:T(8,128)(2,1)}, bf16[4,128,576]{2,1,0:T(8,128)(2,1)S(1)}, bf16[4,128,576]{2,1,0:T(8,128)(2,1)S(1)}) custom-call(s32[4]{0:T(128)S(1)} %pad_add_fusion.place, bf16[128,3648]{1,0:T(8,128)(2,1)S(1)} %bitcast.16, bf16[4,128,576]{2,1,0:T(8,128)(2,1)S(1)} %copy.19.own_ref, ...), custom_call_target="tpu_custom_call" | custom-call | flops 12000000000 | bytes 15000000 | tf_op jit(solution)/shard_map/pallas_call | solution.py:113
  73.0 0.0 copy-start
  73.0 0.0 copy-start.4
  73.0 2.0 %slice.17 = bf16[8,512,256]{2,1,0:T(8,128)(2,1)S(1)} slice(bf16[16,512,256]{2,1,0:T(8,128)(2,1)} %get-tuple-element.14), slice={[0:8], [0:512], [0:256]} | slice | bytes 4194304 | tf_op jit(solution)/shard_map/slice | solution.py:196
  75.1 0.0 copy-done
  75.1 0.1 collective-permute-start.2
  75.2 4.1 %collective-permute-done.2 = bf16[8,512,256]{2,1,0:T(8,128)(2,1)S(1)} collective-permute-done((bf16[8,512,256]{2,1,0:T(8,128)(2,1)S(1)}, bf16[8,512,256]{2,1,0:T(8,128)(2,1)S(1)}, u32[]{:S(2)}, u32[]{:S(2)}) %collective-permute-start.2) | collective-permute-done | bytes 2097184 | tf_op jit(solution)/shard_map/ppermute | solution.py:157
  79.3 0.0 copy-done.4
  79.3 0.5 add_convert_fusion
  79.8 33.0 %all_to_all.37 = bf16[8,512,256]{2,1,0:T(8,128)(2,1)} all-to-all(bf16[8,512,256]{2,1,0:T(8,128)(2,1)S(1)} %add_convert_fusion), channel_id=1, replica_groups=mesh['dp'=2,'z'=4,'y'=2,'x'=4,'core'=2] {'dp','x'}, dimensions={0} | all-to-all | bytes 4194304 | tf_op jit(solution)/shard_map/all_to_all | solution.py:202
  112.8 2.0 %reduce_sum.32 = bf16[512,256]{1,0:T(8,128)(2,1)S(1)} reduce(bf16[8,512,256]{2,1,0:T(8,128)(2,1)} %all_to_all.37, bf16[]{:T(256)} %constant.21.clone.1), dimensions={0}, to_apply=%region_2.0 | reduce | flops 917504 | bytes 2359298 | tf_op jit(solution)/shard_map/reduce_sum | solution.py:203
  114.8 0.1 broadcast_in_dim.11
  115.0 30.8 %all_to_all.38 = bf16[8,512,256]{2,1,0:T(8,128)(2,1)} all-to-all(bf16[8,512,256]{2,1,0:T(8,128)(2,1)S(1)} %broadcast_in_dim.11), channel_id=1, replica_groups=mesh['dp'=2,'z'=4,'y'=2,'x'=4,'core'=2] {'dp','x'}, dimensions={0} | all-to-all | bytes 4194304 | tf_op jit(solution)/shard_map/all_to_all | solution.py:162
  145.8 1.7 collective-permute-start.3
  147.5 0.3 copy.21
  147.8 0.1 collective-permute-start.1
  147.9 4.2 %collective-permute-done.1 = bf16[4,128,576]{1,2,0:T(8,128)(2,1)S(1)} collective-permute-done((bf16[4,128,576]{1,2,0:T(8,128)(2,1)S(1)}, bf16[4,128,576]{1,2,0:T(8,128)(2,1)S(1)}, u32[]{:S(2)}, u32[]{:S(2)}) %collective-permute-start.1) | collective-permute-done | bytes 589856 | tf_op jit(solution)/shard_map/ppermute | solution.py:157
  152.1 0.3 copy.22
  152.4 0.0 copy-done.1
  152.5 1.0 add_convert_fusion.1
  153.5 3.9 %all-to-all-start.2 = ((bf16[32,16,576]{2,1,0:T(8,128)(2,1)}), bf16[32,16,576]{2,1,0:T(8,128)(2,1)S(1)}, u32[]{:S(2)}, u32[]{:S(2)}) async-start(bf16[32,16,576]{2,1,0:T(8,128)(2,1)} %bitcast.11), calls=%async_computation.2 | async-start | bytes 1310720 | tf_op jit(solution)/shard_map/all_to_all | solution.py:198
  157.4 12.8 %all-to-all-done.2 = bf16[32,16,576]{2,1,0:T(8,128)(2,1)S(1)} async-done(((bf16[32,16,576]{2,1,0:T(8,128)(2,1)}), bf16[32,16,576]{2,1,0:T(8,128)(2,1)S(1)}, u32[]{:S(2)}, u32[]{:S(2)}) %all-to-all-start.2) | async-done | bytes 589856 | tf_op jit(solution)/shard_map/all_to_all | solution.py:198
  170.2 0.7 convert_reduce_fusion
  170.9 0.0 collective-permute-done.3
  170.9 2.5 %broadcast_select_fusion.1 = (bf16[8,512,256]{2,1,0:T(8,128)(2,1)S(1)}, bf16[8,512,256]{2,1,0:T(8,128)(2,1)S(1)}) fusion(bf16[8,512,256]{2,1,0:T(8,128)(2,1)} %all_to_all.38, bf16[8,512,256]{2,1,0:T(8,128)(2,1)} %collective-permute-done.3, pred[]{:T(512)S(6)} %eq.4), kind=kLoop, calls=%fused_computation.3 | loop fusion | flops 2097152 | bytes 8388609 | tf_op jit(solution)/shard_map/jit(_where)/select_n | solution.py:206
  173.4 0.5 maximum_convert_fusion
  173.9 4.5 %fusion.1 = (f32[16,512,128]{2,1,0:T(8,128)}, f32[16,512,128]{2,1,0:T(8,128)}) fusion(f32[16,512,256]{2,1,0:T(8,128)S(1)} %maximum_convert_fusion), kind=kLoop, calls=%fused_computation.11 | loop fusion | bytes 16777216 | tf_op jit(solution)/shard_map/slice | solution.py:209
  (2 shorter events, 0.0 us)
Async XLA Ops:
  3.1 35.8 %copy-start.5 = (s32[1,8]{1,0:T(1,128)S(1)}, s32[1,8]{1,0:T(1,128)}, u32[]{:S(2)}) copy-start(s32[1,8]{1,0:T(1,128)} %param.11) | copy-start | bytes 100
  23.8 19.5 %copy-start.3 = (bf16[128,2048]{1,0:T(8,128)(2,1)S(1)}, bf16[128,2048]{1,0:T(8,128)(2,1)}, u32[]{:S(2)}) copy-start(bf16[128,2048]{1,0:T(8,128)(2,1)} %grad_ref.1) | copy-start | bytes 1572868
  35.9 6.0 %collective-permute-start = (bf16[4,128,576]{1,2,0:T(8,128)(2,1)S(1)}, bf16[4,128,576]{1,2,0:T(8,128)(2,1)}, u32[]{:S(2)}, u32[]{:S(2)}) collective-permute-start(bf16[4,128,576]{1,2,0:T(8,128)(2,1)S(1)} %all_to_all.36), channel_id=1, source_target_pairs={{0,1},{1,0},{2,3},{3,2},{4,5},{5,4},{6,7},{7,6},{8,9},{9,8},{10,11... | collective-permute-start | bytes 1769480 | tf_op jit(solution)/shard_map/ppermute | solution.py:157
  43.2 1.6 copy-start.2
  73.0 2.0 %copy-start = (bf16[4,128,576]{2,1,0:T(8,128)(2,1)}, bf16[4,128,576]{2,1,0:T(8,128)(2,1)S(1)}, u32[]{:S(2)}) copy-start(bf16[4,128,576]{2,1,0:T(8,128)(2,1)S(1)} %get-tuple-element.12) | copy-start | bytes 1769476
  73.0 6.3 %copy-start.4 = (bf16[16,512,256]{2,1,0:T(8,128)(2,1)S(1)}, bf16[16,512,256]{2,1,0:T(8,128)(2,1)}, u32[]{:S(2)}) copy-start(bf16[16,512,256]{2,1,0:T(8,128)(2,1)} %get-tuple-element.14) | copy-start | bytes 12582916
  75.1 4.2 %collective-permute-start.2 = (bf16[8,512,256]{2,1,0:T(8,128)(2,1)S(1)}, bf16[8,512,256]{2,1,0:T(8,128)(2,1)S(1)}, u32[]{:S(2)}, u32[]{:S(2)}) collective-permute-start(bf16[8,512,256]{2,1,0:T(8,128)(2,1)S(1)} %slice.17), channel_id=1, source_target_pairs={{0,1},{1,0},{2,3},{3,2},{4,5},{5,4},{6,7},{7,6},{8,9},{9,8},{10,11... | collective-permute-start | bytes 6291464 | tf_op jit(solution)/shard_map/ppermute | solution.py:157
  145.8 6.7 %copy-start.1 = (bf16[4,128,576]{2,1,0:T(8,128)(2,1)S(1)}, bf16[4,128,576]{2,1,0:T(8,128)(2,1)}, u32[]{:S(2)}) copy-start(bf16[4,128,576]{2,1,0:T(8,128)(2,1)} %copy-done) | copy-start | bytes 1769476
  145.8 25.1 %collective-permute-start.3 = (bf16[8,512,256]{2,1,0:T(8,128)(2,1)}, bf16[8,512,256]{2,1,0:T(8,128)(2,1)}, u32[]{:S(2)}, u32[]{:S(2)}) collective-permute-start(bf16[8,512,256]{2,1,0:T(8,128)(2,1)} %all_to_all.38), channel_id=1, source_target_pairs={{0,1},{1,0},{2,3},{3,2},{4,5},{5,4},{6,7},{7,6},{8,9},{9,8},{10,11... | collective-permute-start | bytes 6291464 | tf_op jit(solution)/shard_map/ppermute | solution.py:157
  147.8 4.3 %collective-permute-start.1 = (bf16[4,128,576]{1,2,0:T(8,128)(2,1)S(1)}, bf16[4,128,576]{1,2,0:T(8,128)(2,1)S(1)}, u32[]{:S(2)}, u32[]{:S(2)}) collective-permute-start(bf16[4,128,576]{1,2,0:T(8,128)(2,1)S(1)} %copy.21), channel_id=1, source_target_pairs={{0,1},{1,0},{2,3},{3,2},{4,5},{5,4},{6,7},{7,6},{8,9},{9,8},{10,11... | collective-permute-start | bytes 1769480 | tf_op jit(solution)/shard_map/ppermute | solution.py:157
  153.5 16.7 %all-to-all-start.2 = ((bf16[32,16,576]{2,1,0:T(8,128)(2,1)}), bf16[32,16,576]{2,1,0:T(8,128)(2,1)S(1)}, u32[]{:S(2)}, u32[]{:S(2)}) async-start(bf16[32,16,576]{2,1,0:T(8,128)(2,1)} %bitcast.11), calls=%async_computation.2 | async-start | bytes 1310720 | tf_op jit(solution)/shard_map/all_to_all | solution.py:198

commit v2 on v1

v2 whole, which is shorter than its diff:
```python
import jax
import jax.numpy as jnp
from jax import lax
from jax.experimental import pallas as pl
from jax.experimental.pallas import tpu as pltpu
from jax.sharding import Mesh
from jax.sharding import PartitionSpec as P

NOPE = 128
ROPE = 64
LATENT = 512
VHEAD = 128
BLOCK = 128
QUERY = NOPE + ROPE
KEY = LATENT + ROPE
KEY_PAD = 640
DOC_MOST = 6
WINDOW = DOC_MOST * BLOCK
GROUP = 4
ROWS = GROUP * BLOCK
HALF = LATENT // 2
SCALE = QUERY ** -0.5
MIB = 1024 * 1024

bf16 = jnp.bfloat16
f32 = jnp.float32
NT = ((1,), (1,))
TN = ((0,), (0,))
HEAD_AXES = ("z", "y")
SUM_AXES = ("dp", "x")


def mul(a, b, dims=((1,), (0,))):
    return lax.dot_general(a, b, (dims, ((), ())), preferred_element_type=f32)


def at_block(block):
    return pl.ds(pl.multiple_of(block * BLOCK, BLOCK), BLOCK)


def attention_kernel(
    place, query_ref, own_ref, other_ref, key_ref, value_ref, grad_ref,
    attended_ref, query_grad_ref, kv_keep_ref, kv_send_ref, keep_ref, send_ref,
    keys, flipped, bias, total,
):
    step = pl.program_id(0)
    core, first, doc_first, x_here = place[0], place[1], place[2], place[3]
    z_here, y_here = place[4], place[5]
    n_x = own_ref.shape[0]
    block = x_here * 2 + core

    @pl.when(step == 0)
    def _():
        for s in range(n_x):
            x = lax.rem(x_here + n_x - s, n_x)
            keys[at_block(2 * x + core), :] = own_ref[s]
            keys[at_block(2 * x + 1 - core), :] = other_ref[s]
        window = keys[pl.ds(pl.multiple_of(first * BLOCK, BLOCK), WINDOW), :]
        flipped[:LATENT, :] = jnp.transpose(window[:, :LATENT])
        flipped[LATENT:, :] = jnp.transpose(window[:, LATENT:])
        key_at = first * BLOCK + lax.broadcasted_iota(jnp.int32, (WINDOW, BLOCK), 0)
        query_at = block * BLOCK + lax.broadcasted_iota(jnp.int32, (WINDOW, BLOCK), 1)
        seen = (key_at >= doc_first * BLOCK) & (key_at <= query_at)
        bias[...] = jnp.where(seen, f32(0.0), f32(-1e30))
        total[...] = jnp.zeros_like(total)

    window = keys.at[pl.ds(pl.multiple_of(first * BLOCK, BLOCK), WINDOW), :]
    latents = window[:, :LATENT]
    rotary = window[:, LATENT:]
    queries = query_ref[...]
    nope = [queries[:, e * QUERY:e * QUERY + NOPE] for e in range(GROUP)]
    turned = jnp.concatenate(
        [queries[:, e * QUERY + NOPE:(e + 1) * QUERY] for e in range(GROUP)], axis=0
    )
    grads = [grad_ref[:, e * VHEAD:(e + 1) * VHEAD] for e in range(GROUP)]
    query_lat = jnp.concatenate(
        [mul(key_ref[e], nope[e], NT).astype(bf16) for e in range(GROUP)], axis=1
    )
    context_grad = jnp.concatenate(
        [mul(value_ref[e], grads[e], NT).astype(bf16) for e in range(GROUP)], axis=1
    )

    hidden = jnp.concatenate([bias[...]] * GROUP, axis=1)
    scores = (mul(latents, query_lat) + mul(rotary, turned, NT)) * SCALE + hidden
    top = jnp.max(scores, axis=0, keepdims=True)
    expo = jnp.exp(scores - top)
    inverse = 1.0 / jnp.sum(expo, axis=0, keepdims=True)
    context = (mul(flipped[:LATENT, :], expo.astype(bf16)) * inverse).astype(bf16)
    delta = jnp.sum(context.astype(f32) * context_grad.astype(f32), axis=0, keepdims=True)
    probs = expo * inverse
    score_grad = (probs * (mul(latents, context_grad) - delta) * SCALE).astype(bf16)
    low = probs.astype(bf16)
    lat_grad = mul(flipped[...], score_grad)
    turned_grad = lat_grad[LATENT:, :]
    lat_grad = lat_grad[:LATENT, :].astype(bf16)

    out = total.at[pl.ds(pl.multiple_of(first * BLOCK, BLOCK), WINDOW), :]
    out[:, :LATENT] += mul(score_grad, query_lat, NT) + mul(low, context_grad, NT)
    out[:, LATENT:] += mul(score_grad, turned)

    pieces = []
    for e in range(GROUP):
        at = slice(e * BLOCK, (e + 1) * BLOCK)
        attended_ref[:, e * VHEAD:(e + 1) * VHEAD] = mul(context[:, at], value_ref[e], TN).astype(bf16)
        pieces.append(mul(lat_grad[:, at], key_ref[e], TN))
        pieces.append(jnp.transpose(turned_grad[:, at]))
        pair = jnp.concatenate([mul(lat_grad[:, at], nope[e]), mul(context[:, at], grads[e])], axis=1)
        upper, lower = pair[:HALF], pair[HALF:]
        kv_keep_ref[e] = jnp.where(core == 0, upper, lower).astype(bf16)
        kv_send_ref[e] = jnp.where(core == 0, lower, upper).astype(bf16)
    query_grad_ref[...] = jnp.concatenate(pieces, axis=1).astype(bf16)

    @pl.when(step == pl.num_programs(0) - 1)
    def _():
        n_z, n_y, _, rows = keep_ref.shape[:4]
        empty = jnp.zeros((rows, KEY_PAD - KEY), bf16)
        for dz in range(n_z):
            for dy in range(n_y):
                head = lax.rem(z_here + dz, n_z) * n_y + lax.rem(y_here + dy, n_y)
                for dx in range(n_x):
                    x = lax.rem(x_here + dx, n_x)
                    for ref, parity in ((keep_ref, core), (send_ref, 1 - core)):
                        start = pl.multiple_of((2 * x + parity) * BLOCK + head * rows, rows)
                        ref[dz, dy, dx, :, :KEY] = total[pl.ds(start, rows), :].astype(bf16)
                        ref[dz, dy, dx, :, KEY:] = empty


def attention(place, queries, own, other, key_up, value_up, out_grad, n_z, n_y):
    heads = key_up.shape[0]
    n_x = own.shape[0]
    tokens = 2 * n_x * BLOCK
    whole = lambda shape: pl.BlockSpec(shape, lambda i, place: (0,) * len(shape))
    heads_at = lambda i, place: (i, 0, 0)
    lanes_at = lambda i, place: (0, i)
    kv_spec = pl.BlockSpec((GROUP, HALF, NOPE + VHEAD), heads_at)
    kv_shape = jax.ShapeDtypeStruct((heads, HALF, NOPE + VHEAD), bf16)
    rows_shape = jax.ShapeDtypeStruct((n_z, n_y, n_x, BLOCK // (n_z * n_y), KEY_PAD), bf16)
    return pl.pallas_call(
        attention_kernel,
        grid_spec=pltpu.PrefetchScalarGridSpec(
            num_scalar_prefetch=1,
            grid=(heads // GROUP,),
            in_specs=[
                pl.BlockSpec((BLOCK, GROUP * QUERY), lanes_at),
                whole(own.shape),
                whole(other.shape),
                pl.BlockSpec((GROUP, LATENT, NOPE), heads_at),
                pl.BlockSpec((GROUP, LATENT, VHEAD), heads_at),
                pl.BlockSpec((BLOCK, GROUP * VHEAD), lanes_at),
            ],
            out_specs=[
                pl.BlockSpec((BLOCK, GROUP * VHEAD), lanes_at),
                pl.BlockSpec((BLOCK, GROUP * QUERY), lanes_at),
                kv_spec,
                kv_spec,
                whole(rows_shape.shape),
                whole(rows_shape.shape),
            ],
            scratch_shapes=[
                pltpu.VMEM((tokens, KEY), bf16),
                pltpu.VMEM((KEY, WINDOW), bf16),
                pltpu.VMEM((WINDOW, BLOCK), f32),
                pltpu.VMEM((tokens, KEY), f32),
            ],
        ),
        out_shape=[
            jax.ShapeDtypeStruct((BLOCK, heads * VHEAD), bf16),
            jax.ShapeDtypeStruct((BLOCK, heads * QUERY), bf16),
            kv_shape,
            kv_shape,
            rows_shape,
            rows_shape,
        ],
        name="attention",
        compiler_params=pltpu.CompilerParams(
            dimension_semantics=("arbitrary",), vmem_limit_bytes=48 * MIB
        ),
        cost_estimate=pl.CostEstimate(
            flops=12_000_000_000, bytes_accessed=15_000_000, transcendentals=1_600_000
        ),
    )(place, queries, own, other, key_up, value_up, out_grad)


def unfold(place, rows, begun, which):
    heads = rows.shape[0]
    each = heads // 2
    shape = jax.ShapeDtypeStruct((heads, LATENT, NOPE), f32)

    def kernel(place, rows_ref, *refs):
        key_ref, value_ref = refs[-2:]
        key_ref[...] = rows_ref[:, :, :NOPE].astype(f32)
        value_ref[...] = rows_ref[:, :, NOPE:].astype(f32)

    def half_at(i, place):
        return (i, place[0] if which == 0 else 1 - place[0], 0)

    out_spec = pl.BlockSpec((each, HALF, NOPE), half_at)
    return pl.pallas_call(
        kernel,
        grid_spec=pltpu.PrefetchScalarGridSpec(
            num_scalar_prefetch=1,
            grid=(heads // each,),
            in_specs=[pl.BlockSpec((each, HALF, NOPE + VHEAD), lambda i, place: (i, 0, 0))]
            + [pl.BlockSpec(memory_space=pl.ANY)] * len(begun),
            out_specs=[out_spec, out_spec],
        ),
        out_shape=[shape, shape],
        input_output_aliases={2: 0, 3: 1} if begun else {},
        name=f"unfold_{which}",
        cost_estimate=pl.CostEstimate(flops=0, bytes_accessed=6_000_000, transcendentals=0),
    )(place, rows, *begun)


def swapped(value):
    return lax.ppermute(value, "core", [(0, 1), (1, 0)])


def shifted(value, axis, steps):
    count = lax.axis_size(axis)
    return lax.ppermute(value, axis, [(i, (i + steps) % count) for i in range(count)])


def exchanged(value, axes):
    return lax.all_to_all(value, axes, 0, 0, tiled=True)


def copies(value, count):
    return jnp.broadcast_to(value[None], (count,) + value.shape)


def added(*terms):
    return sum(term.astype(f32) for term in terms)


def folded(rows, axis):
    count = rows.shape[0]
    return added(rows[0], *[shifted(rows[s], axis, s) for s in range(1, count)])


def on_device(queries, latent, key_up, value_up, out_grad, block_docs):
    n_head = lax.axis_size(HEAD_AXES)
    n_x = lax.axis_size("x")
    n_sum = lax.axis_size(SUM_AXES)
    core = lax.axis_index("core")
    x_here = lax.axis_index("x")
    block = x_here * 2 + core
    n_z, n_y = [lax.axis_size(axis) for axis in HEAD_AXES]
    docs = block_docs[0]
    doc_first = jnp.sum((docs < docs[block]).astype(jnp.int32))
    first = jnp.maximum(block - (DOC_MOST - 1), 0)
    place = jnp.stack(
        [core, first, doc_first, x_here] + [lax.axis_index(axis) for axis in HEAD_AXES]
    ).astype(jnp.int32)

    rows = queries.shape[0]
    arrived = jnp.swapaxes(queries.reshape(rows, n_head, -1), 0, 1)
    own = exchanged(copies(latent, n_head), HEAD_AXES)
    own, arrived = lax.optimization_barrier((own, arrived))
    arrived = exchanged(arrived, HEAD_AXES).reshape(rows * n_head, -1)
    own = own.reshape(BLOCK, KEY)
    own = jnp.stack([own] + [shifted(own, "x", s) for s in range(1, n_x)])
    other = swapped(own)

    attended, query_grad, keep, send, rows_keep, rows_send = attention(
        place, arrived, own, other, key_up, value_up, out_grad, n_z, n_y
    )
    kv = exchanged(added(keep, swapped(send)).astype(bf16), SUM_AXES)
    rows = added(rows_keep, swapped(rows_send)).astype(bf16)
    for axis in HEAD_AXES:
        rows = folded(rows, axis).astype(bf16)
    kv = added(*kv.reshape((n_sum, -1) + kv.shape[1:])).astype(bf16)
    kv, rows = lax.optimization_barrier((kv, rows))
    rows = [rows[0]] + [shifted(rows[s], "x", s) for s in range(1, n_x)]
    kv = exchanged(copies(kv, n_sum), SUM_AXES).reshape((-1,) + kv.shape[1:])
    grads = unfold(place, kv, [], 0)
    grads = unfold(place, swapped(kv), grads, 1)
    rows, grads = lax.optimization_barrier((rows, grads))
    latent_grad = added(*rows)[:, :KEY]
    key_up_grad, value_up_grad = grads
    return (attended, query_grad, latent_grad, key_up_grad, value_up_grad)


def solution(mesh):
    n_dp, n_head, n_blk = mesh.devices.shape
    fine = Mesh(
        mesh.devices.reshape(n_dp, n_head // 2, 2, n_blk // 2, 2), ("dp", "z", "y", "x", "core")
    )
    head, blk = HEAD_AXES, ("x", "core")
    return jax.shard_map(
        on_device,
        mesh=fine,
        in_specs=(
            P(("dp",) + blk + head, None),
            P(("dp",) + blk + head, None),
            P(head, None, None),
            P(head, None, None),
            P(("dp",) + blk, head),
            P("dp", None),
        ),
        out_specs=(
            P(("dp",) + blk, head),
            P(("dp",) + blk, head),
            P(("dp",) + blk + head, None),
            P(head, None, None),
            P(head, None, None),
        ),
        check_vma=False,
    )
```

time: 179 us -> 147 us (0.82)
  blocking collectives: 96.3 us -> 32.9 us
  starting transfers between devices: 8.91 us -> 33 us
  waiting for transfers between devices: 21.1 us -> 38 us
  local copies, waits for them, and re-layouts: 13.7 us -> 6.63 us
  other arithmetic: 9.31 us -> 5.66 us
    all_to_all x4 -> x1, blocking collectives: 96.3 us -> 32.9 us  [exchanged(): return lax.all_to_all(value, axes, 0, 0, tiled=True)]
    ppermute x0 -> x10, waiting for transfers between devices: none -> 27.2 us  [shifted(): lax.ppermute(value, axis, [(i, (i + steps) % count) for i in range(count)])]
    all_to_all x1 -> x3, starting transfers between devices: 3.9 us -> 16.1 us  [exchanged(): return lax.all_to_all(value, axes, 0, 0, tiled=True)]
    ppermute x0 -> x10, starting transfers between devices: none -> 8.86 us  [shifted(): lax.ppermute(value, axis, [(i, (i + steps) % count) for i in range(count)])]
    pallas_call x0 -> x2, Pallas kernels: none -> 8.09 us  [unfold(): pl.pallas_call(kernel, grid_spec=pltpu.PrefetchScalarGridSpec(num_scalar_...]
    pallas_call x1, Pallas kernels: 28.2 us -> 20.8 us  [attention(): pl.pallas_call(attention_kernel, grid_spec=pltpu.PrefetchScalarGridSpec(n...]
    all_to_all x1 -> x3, waiting for transfers between devices: 12.8 us -> 5.94 us  [exchanged(): return lax.all_to_all(value, axes, 0, 0, tiled=True)]
    slice x4 -> x0, local copies, waits for them, and re-layouts: 6.63 us -> none  [the longest x1 4.45 us: on_device(): return (attended, query_grad, latent_grad, kv[:, :, :NOPE], kv[:, :, NOPE:])]
  transfers between devices with their start and end apart: 5 -> 17, of which waited for: 3 -> 8; matrix products, arithmetic and copies ran while one was open for 3% -> 6% of each run, Pallas kernels for 0% -> 6%
where the time goes in v2:
time: 147 us; the launch traced here: 146 us
  waiting for transfers between devices  38 us (26%)
  starting transfers between devices  33 us (22%)
  blocking collectives  32.9 us (22%)
  Pallas kernels  28.9 us (20%)
  local copies, waits for them, and re-layouts  6.63 us (5%)
  other arithmetic  5.66 us (4%)
    all_to_all x1, blocking collectives, exchanged(): return lax.all_to_all(value, axes, 0, 0, tiled=True)  32.9 us
    ppermute x10, waiting for transfers between devices, shifted(): lax.ppermute(value, axis, [(i, (i + steps) % count) for i in range(count)])  27.2 us
    pallas_call x1, Pallas kernels, attention(): pl.pallas_call(attention_kernel, grid_spec=pltpu.PrefetchScalarGridSpec(n...  20.8 us
    all_to_all x3, starting transfers between devices, exchanged(): return lax.all_to_all(value, axes, 0, 0, tiled=True)  16.1 us
    ppermute x10, starting transfers between devices, shifted(): lax.ppermute(value, axis, [(i, (i + steps) % count) for i in range(count)])  8.86 us
    pallas_call x2, Pallas kernels, unfold(): pl.pallas_call(kernel, grid_spec=pltpu.PrefetchScalarGridSpec(num_scalar_...  8.09 us
    ppermute x4, starting transfers between devices, swapped(): return lax.ppermute(value, 'core', [(0, 1), (1, 0)])  8.01 us
    all_to_all x3, waiting for transfers between devices, exchanged(): return lax.all_to_all(value, axes, 0, 0, tiled=True)  5.94 us
  transfers between devices with their start and end apart: 17, of which 8 were waited for; matrix products, arithmetic and copies ran while one was open for 6% of the time, Pallas kernels for 6%

profile of v2, /device:TPU:1, one launch (start us, length us, event | category | flops | bytes accessed | tf_op | source)
XLA Modules:
  0.0 145.9 jit_solution(16320005316931672172)
XLA Ops:
  0.6 1.4 broadcast_in_dim.4
  2.0 6.9 %all-to-all-start = ((bf16[8,16,576]{2,1,0:T(8,128)(2,1)}), bf16[8,16,576]{2,1,0:T(8,128)(2,1)S(1)}, u32[]{:S(2)}, u32[]{:S(2)}) async-start(bf16[8,16,576]{2,1,0:T(8,128)(2,1)} %broadcast_in_dim.4), calls=%async_computation | async-start | bytes 327680 | tf_op jit(solution)/shard_map/all_to_all | solution.py:224
  8.9 2.1 %copy.19 = bf16[2,8,8,3072]{3,2,0,1:T(8,128)(2,1)} copy(bf16[2,8,8,3072]{3,2,1,0:T(8,128)(2,1)} %bitcast.50) | data formatting | bytes 1572864 | tf_op jit(solution)/shard_map/reshape | solution.py:256
  11.0 3.7 %all-to-all-done = bf16[8,16,576]{2,1,0:T(8,128)(2,1)S(1)} async-done(((bf16[8,16,576]{2,1,0:T(8,128)(2,1)}), bf16[8,16,576]{2,1,0:T(8,128)(2,1)S(1)}, u32[]{:S(2)}, u32[]{:S(2)}) %all-to-all-start) | async-done | bytes 147488 | tf_op jit(solution)/shard_map/all_to_all | solution.py:224
  14.6 2.5 %collective-permute-start.2 = (bf16[128,576]{1,0:T(8,128)(2,1)S(1)}, bf16[128,576]{1,0:T(8,128)(2,1)S(1)}, u32[]{:S(2)}, u32[]{:S(2)}) collective-permute-start(bf16[128,576]{1,0:T(8,128)(2,1)S(1)} %bitcast.51), channel_id=1, source_target_pairs={{0,6},{2,0},{4,2},{6,4},{1,7},{3,1},{5,3},{7,5},{8,14},{10,8},{12,... | collective-permute-start | bytes 442376 | tf_op jit(solution)/shard_map/ppermute | solution.py:220
  17.1 0.5 collective-permute-start.1
  17.6 0.6 collective-permute-start
  18.2 3.5 %all-to-all-start.1 = ((bf16[8,16,3072]{2,1,0:T(8,128)(2,1)}), bf16[8,16,3072]{2,1,0:T(8,128)(2,1)S(1)}, u32[]{:S(2)}, u32[]{:S(2)}) async-start(bf16[8,16,3072]{2,1,0:T(8,128)(2,1)} %bitcast.46), calls=%async_computation.1 | async-start | bytes 1572864 | tf_op jit(solution)/shard_map/all_to_all | solution.py:224
  21.8 0.0 collective-permute-done.2
  21.8 1.1 collective-permute-done.1
  22.9 4.1 %collective-permute-done = bf16[128,576]{1,0:T(8,128)(2,1)S(1)} collective-permute-done((bf16[128,576]{1,0:T(8,128)(2,1)S(1)}, bf16[128,576]{1,0:T(8,128)(2,1)S(1)}, u32[]{:S(2)}, u32[]{:S(2)}) %collective-permute-start) | collective-permute-done | bytes 147488 | tf_op jit(solution)/shard_map/ppermute | solution.py:220
  27.0 0.1 pad_maximum_fusion.own_ref
  27.1 0.3 copy.15
  27.4 1.9 %collective-permute-start.3 = (bf16[4,128,576]{1,2,0:T(8,128)(2,1)S(1)}, bf16[4,128,576]{1,2,0:T(8,128)(2,1)S(1)}, u32[]{:S(2)}, u32[]{:S(2)}) collective-permute-start(bf16[4,128,576]{1,2,0:T(8,128)(2,1)S(1)} %copy.15), channel_id=1, source_target_pairs={{0,1},{1,0},{2,3},{3,2},{4,5},{5,4},{6,7},{7,6},{8,9},{9,8},{10,11... | collective-permute-start | bytes 1769480 | tf_op jit(solution)/shard_map/ppermute | solution.py:215
  29.3 0.6 constant_dynamic-slice_fusion
  29.9 1.3 fusion.4
  31.1 0.7 stack.39.place
  31.8 0.0 collective-permute-done.3
  31.8 0.3 copy.16.other_ref
  32.1 0.0 all-to-all-done.1
  32.1 0.0 copy-start.1
  32.1 1.0 copy-done.1
  33.2 20.8 %attention.1 = (bf16[128,2048]{1,0:T(8,128)(2,1)}, bf16[128,3072]{1,0:T(8,128)(2,1)}, bf16[16,256,256]{2,1,0:T(8,128)(2,1)S(1)}, bf16[16,256,256]{2,1,0:T(8,128)...) custom-call(s32[6]{0:T(128)S(1)} %stack.39.place, ...), custom_call_target="tpu_custom_call" | custom-call | flops 12000000000 | bytes 15000000 | tf_op jit(solution)/shard_map/attention/pallas_call | solution.py:138
  53.9 3.5 %collective-permute-start.4 = (bf16[16,256,256]{2,1,0:T(8,128)(2,1)}, bf16[16,256,256]{2,1,0:T(8,128)(2,1)S(1)}, u32[]{:S(2)}, u32[]{:S(2)}) collective-permute-start(bf16[16,256,256]{2,1,0:T(8,128)(2,1)} %get-tuple-element.30), channel_id=1, source_target_pairs={{0,1},{1,0},{2,3},{3,2},{4,5},{5,4},{6,7},{7,6},{8,9},{9,8},{10,11... | collective-permute-start | bytes 6291464 | tf_op jit(solution)/shard_map/ppermute | solution.py:215
  57.5 0.1 collective-permute-start.5
  57.6 4.8 %collective-permute-done.4 = bf16[16,256,256]{2,1,0:T(8,128)(2,1)S(1)} collective-permute-done((bf16[16,256,256]{2,1,0:T(8,128)(2,1)}, bf16[16,256,256]{2,1,0:T(8,128)(2,1)S(1)}, u32[]{:S(2)}, u32[]{:S(2)}) %collective-permute-start.4) | collective-permute-done | bytes 2097184 | tf_op jit(solution)/shard_map/ppermute | solution.py:215
  62.4 2.0 %add_convert_fusion = bf16[16,256,256]{2,1,0:T(8,128)(2,1)} fusion(bf16[16,256,256]{2,1,0:T(8,128)(2,1)S(1)} %collective-permute-done.4, bf16[16,256,256]{2,1,0:T(8,128)(2,1)S(1)} %get-tuple-element.29), kind=kLoop, calls=%fused_computation | loop fusion | flops 4194304 | bytes 6291456 | tf_op jit(solution)/shard_map/convert_element_type | solution.py:267
  64.4 5.7 %all-to-all-start.2 = ((bf16[16,256,256]{2,1,0:T(8,128)(2,1)}), bf16[16,256,256]{2,1,0:T(8,128)(2,1)S(1)}, u32[]{:S(2)}, u32[]{:S(2)}) async-start(bf16[16,256,256]{2,1,0:T(8,128)(2,1)} %add_convert_fusion), calls=%async_computation.2 | async-start | bytes 4194304 | tf_op jit(solution)/shard_map/all_to_all | solution.py:224
  70.1 1.2 add_convert_fusion.1
  71.4 0.1 collective-permute-start.6
  71.5 2.7 %collective-permute-start.8 = (bf16[2,4,16,640]{3,2,1,0:T(8,128)(2,1)S(1)}, bf16[2,4,16,640]{3,2,1,0:T(8,128)(2,1)S(1)}, u32[]{:S(2)}, u32[]{:S(2)}) collective-permute-start(bf16[2,4,16,640]{3,2,1,0:T(8,128)(2,1)S(1)} %get-tuple-element.46), channel_id=1, source_target_pairs={{0,48},{16,0},{32,16},{48,32},{1,49},{17,1},{33,17},{49,33},{2,50}... | collective-permute-start | bytes 491528 | tf_op jit(solution)/shard_map/ppermute | solution.py:220
  74.2 3.6 %collective-permute-done.6 = bf16[2,4,16,640]{3,2,1,0:T(8,128)(2,1)S(1)} collective-permute-done((bf16[2,4,16,640]{3,2,1,0:T(8,128)(2,1)S(1)}, bf16[2,4,16,640]{3,2,1,0:T(8,128)(2,1)S(1)}, u32[]{:S(2)}, u32[]{:S(2)}) %collective-permute-start.6) | collective-permute-done | bytes 163872 | tf_op jit(solution)/shard_map/ppermute | solution.py:220
  77.8 0.0 collective-permute-done.8
  77.8 2.4 %collective-permute-done.7 = bf16[2,4,16,640]{3,2,1,0:T(8,128)(2,1)S(1)} collective-permute-done((bf16[2,4,16,640]{3,2,1,0:T(8,128)(2,1)S(1)}, bf16[2,4,16,640]{3,2,1,0:T(8,128)(2,1)S(1)}, u32[]{:S(2)}, u32[]{:S(2)}) %collective-permute-start.7) | collective-permute-done | bytes 163872 | tf_op jit(solution)/shard_map/ppermute | solution.py:220
  80.2 0.1 fusion.2
  80.3 0.1 collective-permute-start.9
  80.4 16.0 %collective-permute-done.9 = bf16[4,16,640]{2,1,0:T(8,128)(2,1)S(1)} collective-permute-done((bf16[4,16,640]{2,1,0:T(8,128)(2,1)S(1)}, bf16[4,16,640]{2,1,0:T(8,128)(2,1)S(1)}, u32[]{:S(2)}, u32[]{:S(2)}) %collective-permute-start.9) | collective-permute-done | bytes 81952 | tf_op jit(solution)/shard_map/ppermute | solution.py:220
  96.5 2.3 %all-to-all-done.2 = bf16[16,256,256]{2,1,0:T(8,128)(2,1)S(1)} async-done(((bf16[16,256,256]{2,1,0:T(8,128)(2,1)}), bf16[16,256,256]{2,1,0:T(8,128)(2,1)S(1)}, u32[]{:S(2)}, u32[]{:S(2)}) %all-to-all-start.2) | async-done | bytes 2097184 | tf_op jit(solution)/shard_map/all_to_all | solution.py:224
  98.7 0.3 add_convert_fusion.2
  99.0 0.2 broadcast_in_dim.5
  99.2 32.9 %all_to_all.20 = bf16[8,2,256,256]{3,2,1,0:T(8,128)(2,1)S(1)} all-to-all(bf16[8,2,256,256]{3,2,1,0:T(8,128)(2,1)S(1)} %broadcast_in_dim.5), channel_id=1, replica_groups=mesh['dp'=2,'z'=4,'y'=2,'x'=4,'core'=2] {'dp','x'}, dimensions={0} | all-to-all | bytes 4194304 | tf_op jit(solution)/shard_map/all_to_all | solution.py:224
  132.2 2.5 %collective-permute-start.13 = (bf16[16,256,256]{2,1,0:T(8,128)(2,1)S(1)}, bf16[16,256,256]{2,1,0:T(8,128)(2,1)}, u32[]{:S(2)}, u32[]{:S(2)}) collective-permute-start(bf16[16,256,256]{2,1,0:T(8,128)(2,1)S(1)} %bitcast.48), channel_id=1, source_target_pairs={{0,1},{1,0},{2,3},{3,2},{4,5},{5,4},{6,7},{7,6},{8,9},{9,8},{10,11... | collective-permute-start | bytes 6291464 | tf_op jit(solution)/shard_map/ppermute | solution.py:215
  134.7 0.9 collective-permute-start.12
  135.6 1.5 %collective-permute-start.11 = (bf16[16,640]{1,0:T(8,128)(2,1)S(1)}, bf16[16,640]{1,0:T(8,128)(2,1)S(1)}, u32[]{:S(2)}, u32[]{:S(2)}) collective-permute-start(bf16[16,640]{1,0:T(8,128)(2,1)S(1)} %get-tuple-element.49), channel_id=1, source_target_pairs={{0,4},{2,6},{4,0},{6,2},{1,5},{3,7},{5,1},{7,3},{8,12},{10,14},{12... | collective-permute-start | bytes 61448 | tf_op jit(solution)/shard_map/ppermute | solution.py:220
  137.1 4.0 %unfold_0.1 = (f32[16,512,128]{2,1,0:T(8,128)}, f32[16,512,128]{2,1,0:T(8,128)}) custom-call(s32[6]{0:T(128)} %copy-done, bf16[16,256,256]{2,1,0:T(8,128)(2,1)} %bitcast.49), custom_call_target="tpu_custom_call" | custom-call | bytes 6000000 | tf_op jit(solution)/shard_map/unfold_0/pallas_call | solution.py:198
  141.1 0.0 collective-permute-done.13.rows_ref
  141.2 4.0 %unfold_1.1 = (f32[16,512,128]{2,1,0:T(8,128)}, f32[16,512,128]{2,1,0:T(8,128)}) custom-call(s32[6]{0:T(128)} %copy-done, bf16[16,256,256]{2,1,0:T(8,128)(2,1)} %collective-permute-done.13.rows_ref, f32[16,512,128]{2,1,0:T(8,128)} %get-tuple-element.35.refs_0_, f32[16,512,128]{2,1,0:T(8,128)} %get-tuple-element.36.refs_1_), custom_call_target="tpu_custom_call", output_to_operand_aliasing={{0}: (2, {}), {1}: (3, {})} | custom-call | bytes 6000000 | tf_op jit(solution)/shard_map/unfold_1/pallas_call | solution.py:198
  145.2 0.6 convert_add_fusion.2
  (16 shorter events, 0.1 us)
Async XLA Ops:
  2.0 12.6 %all-to-all-start = ((bf16[8,16,576]{2,1,0:T(8,128)(2,1)}), bf16[8,16,576]{2,1,0:T(8,128)(2,1)S(1)}, u32[]{:S(2)}, u32[]{:S(2)}) async-start(bf16[8,16,576]{2,1,0:T(8,128)(2,1)} %broadcast_in_dim.4), calls=%async_computation | async-start | bytes 327680 | tf_op jit(solution)/shard_map/all_to_all | solution.py:224
  11.0 18.3 %copy-start.3 = (s32[1,8]{1,0:T(1,128)S(1)}, s32[1,8]{1,0:T(1,128)}, u32[]{:S(2)}) copy-start(s32[1,8]{1,0:T(1,128)} %param.11) | copy-start | bytes 100
  14.6 7.2 %collective-permute-start.2 = (bf16[128,576]{1,0:T(8,128)(2,1)S(1)}, bf16[128,576]{1,0:T(8,128)(2,1)S(1)}, u32[]{:S(2)}, u32[]{:S(2)}) collective-permute-start(bf16[128,576]{1,0:T(8,128)(2,1)S(1)} %bitcast.51), channel_id=1, source_target_pairs={{0,6},{2,0},{4,2},{6,4},{1,7},{3,1},{5,3},{7,5},{8,14},{10,8},{12,... | collective-permute-start | bytes 442376 | tf_op jit(solution)/shard_map/ppermute | solution.py:220
  17.1 5.8 %collective-permute-start.1 = (bf16[128,576]{1,0:T(8,128)(2,1)S(1)}, bf16[128,576]{1,0:T(8,128)(2,1)S(1)}, u32[]{:S(2)}, u32[]{:S(2)}) collective-permute-start(bf16[128,576]{1,0:T(8,128)(2,1)S(1)} %bitcast.52), channel_id=1, source_target_pairs={{0,4},{2,6},{4,0},{6,2},{1,5},{3,7},{5,1},{7,3},{8,12},{10,14},{12... | collective-permute-start | bytes 442376 | tf_op jit(solution)/shard_map/ppermute | solution.py:220
  17.6 9.3 %collective-permute-start = (bf16[128,576]{1,0:T(8,128)(2,1)S(1)}, bf16[128,576]{1,0:T(8,128)(2,1)S(1)}, u32[]{:S(2)}, u32[]{:S(2)}) collective-permute-start(bf16[128,576]{1,0:T(8,128)(2,1)S(1)} %bitcast.53), channel_id=1, source_target_pairs={{0,2},{2,4},{4,6},{6,0},{1,3},{3,5},{5,7},{7,1},{8,10},{10,12},{12... | collective-permute-start | bytes 442376 | tf_op jit(solution)/shard_map/ppermute | solution.py:220
  18.2 13.9 %all-to-all-start.1 = ((bf16[8,16,3072]{2,1,0:T(8,128)(2,1)}), bf16[8,16,3072]{2,1,0:T(8,128)(2,1)S(1)}, u32[]{:S(2)}, u32[]{:S(2)}) async-start(bf16[8,16,3072]{2,1,0:T(8,128)(2,1)} %bitcast.46), calls=%async_computation.1 | async-start | bytes 1572864 | tf_op jit(solution)/shard_map/all_to_all | solution.py:224
  27.4 4.4 %collective-permute-start.3 = (bf16[4,128,576]{1,2,0:T(8,128)(2,1)S(1)}, bf16[4,128,576]{1,2,0:T(8,128)(2,1)S(1)}, u32[]{:S(2)}, u32[]{:S(2)}) collective-permute-start(bf16[4,128,576]{1,2,0:T(8,128)(2,1)S(1)} %copy.15), channel_id=1, source_target_pairs={{0,1},{1,0},{2,3},{3,2},{4,5},{5,4},{6,7},{7,6},{8,9},{9,8},{10,11... | collective-permute-start | bytes 1769480 | tf_op jit(solution)/shard_map/ppermute | solution.py:215
  31.8 22.1 %copy-start = (s32[6]{0:T(128)}, s32[6]{0:T(128)S(1)}, u32[]{:S(2)}) copy-start(s32[6]{0:T(128)S(1)} %stack.39.place) | copy-start | bytes 76
  32.1 1.0 copy-start.1
  53.9 8.5 %collective-permute-start.4 = (bf16[16,256,256]{2,1,0:T(8,128)(2,1)}, bf16[16,256,256]{2,1,0:T(8,128)(2,1)S(1)}, u32[]{:S(2)}, u32[]{:S(2)}) collective-permute-start(bf16[16,256,256]{2,1,0:T(8,128)(2,1)} %get-tuple-element.30), channel_id=1, source_target_pairs={{0,1},{1,0},{2,3},{3,2},{4,5},{5,4},{6,7},{7,6},{8,9},{9,8},{10,11... | collective-permute-start | bytes 6291464 | tf_op jit(solution)/shard_map/ppermute | solution.py:215
  57.5 12.6 %collective-permute-start.5 = (bf16[4,2,4,16,640]{4,3,2,1,0:T(8,128)(2,1)S(1)}, bf16[4,2,4,16,640]{4,3,2,1,0:T(8,128)(2,1)}, u32[]{:S(2)}, u32[]{:S(2)}) collective-permute-start(bf16[4,2,4,16,640]{4,3,2,1,0:T(8,128)(2,1)S(1)} %get-tuple-element.32), channel_id=1, source_target_pairs={{0,1},{1,0},{2,3},{3,2},{4,5},{5,4},{6,7},{7,6},{8,9},{9,8},{10,11... | collective-permute-start | bytes 1966088 | tf_op jit(solution)/shard_map/ppermute | solution.py:215
  64.4 34.3 %all-to-all-start.2 = ((bf16[16,256,256]{2,1,0:T(8,128)(2,1)}), bf16[16,256,256]{2,1,0:T(8,128)(2,1)S(1)}, u32[]{:S(2)}, u32[]{:S(2)}) async-start(bf16[16,256,256]{2,1,0:T(8,128)(2,1)} %add_convert_fusion), calls=%async_computation.2 | async-start | bytes 4194304 | tf_op jit(solution)/shard_map/all_to_all | solution.py:224
  71.4 6.4 %collective-permute-start.6 = (bf16[2,4,16,640]{3,2,1,0:T(8,128)(2,1)S(1)}, bf16[2,4,16,640]{3,2,1,0:T(8,128)(2,1)S(1)}, u32[]{:S(2)}, u32[]{:S(2)}) collective-permute-start(bf16[2,4,16,640]{3,2,1,0:T(8,128)(2,1)S(1)} %get-tuple-element.45), channel_id=1, source_target_pairs={{0,16},{16,32},{32,48},{48,0},{1,17},{17,33},{33,49},{49,1},{2,18}... | collective-permute-start | bytes 491528 | tf_op jit(solution)/shard_map/ppermute | solution.py:220
  71.5 6.3 %collective-permute-start.8 = (bf16[2,4,16,640]{3,2,1,0:T(8,128)(2,1)S(1)}, bf16[2,4,16,640]{3,2,1,0:T(8,128)(2,1)S(1)}, u32[]{:S(2)}, u32[]{:S(2)}) collective-permute-start(bf16[2,4,16,640]{3,2,1,0:T(8,128)(2,1)S(1)} %get-tuple-element.46), channel_id=1, source_target_pairs={{0,48},{16,0},{32,16},{48,32},{1,49},{17,1},{33,17},{49,33},{2,50}... | collective-permute-start | bytes 491528 | tf_op jit(solution)/shard_map/ppermute | solution.py:220
  74.2 6.1 %collective-permute-start.7 = (bf16[2,4,16,640]{3,2,1,0:T(8,128)(2,1)S(1)}, bf16[2,4,16,640]{3,2,1,0:T(8,128)(2,1)S(1)}, u32[]{:S(2)}, u32[]{:S(2)}) collective-permute-start(bf16[2,4,16,640]{3,2,1,0:T(8,128)(2,1)S(1)} %get-tuple-element.47), channel_id=1, source_target_pairs={{0,32},{16,48},{32,0},{48,16},{1,33},{17,49},{33,1},{49,17},{2,34}... | collective-permute-start | bytes 491528 | tf_op jit(solution)/shard_map/ppermute | solution.py:220
  80.3 16.1 %collective-permute-start.9 = (bf16[4,16,640]{2,1,0:T(8,128)(2,1)S(1)}, bf16[4,16,640]{2,1,0:T(8,128)(2,1)S(1)}, u32[]{:S(2)}, u32[]{:S(2)}) collective-permute-start(bf16[4,16,640]{2,1,0:T(8,128)(2,1)S(1)} %slice_bitcast_fusion.4), channel_id=1, source_target_pairs={{0,8},{8,0},{1,9},{9,1},{2,10},{10,2},{3,11},{11,3},{4,12},{12,4},... | collective-permute-start | bytes 245768 | tf_op jit(solution)/shard_map/ppermute | solution.py:220
  132.2 4.9 %copy-start.2 = (bf16[8,2,256,256]{3,2,1,0:T(8,128)(2,1)}, bf16[8,2,256,256]{3,2,1,0:T(8,128)(2,1)S(1)}, u32[]{:S(2)}) copy-start(bf16[8,2,256,256]{3,2,1,0:T(8,128)(2,1)S(1)} %all_to_all.20) | copy-start | bytes 6291460
  132.2 9.0 %collective-permute-start.13 = (bf16[16,256,256]{2,1,0:T(8,128)(2,1)S(1)}, bf16[16,256,256]{2,1,0:T(8,128)(2,1)}, u32[]{:S(2)}, u32[]{:S(2)}) collective-permute-start(bf16[16,256,256]{2,1,0:T(8,128)(2,1)S(1)} %bitcast.48), channel_id=1, source_target_pairs={{0,1},{1,0},{2,3},{3,2},{4,5},{5,4},{6,7},{7,6},{8,9},{9,8},{10,11... | collective-permute-start | bytes 6291464 | tf_op jit(solution)/shard_map/ppermute | solution.py:215
  134.7 10.5 %collective-permute-start.12 = (bf16[16,640]{1,0:T(8,128)(2,1)S(1)}, bf16[16,640]{1,0:T(8,128)(2,1)S(1)}, u32[]{:S(2)}, u32[]{:S(2)}) collective-permute-start(bf16[16,640]{1,0:T(8,128)(2,1)S(1)} %get-tuple-element.48), channel_id=1, source_target_pairs={{0,6},{2,0},{4,2},{6,4},{1,7},{3,1},{5,3},{7,5},{8,14},{10,8},{12,... | collective-permute-start | bytes 61448 | tf_op jit(solution)/shard_map/ppermute | solution.py:220
  135.6 9.6 %collective-permute-start.11 = (bf16[16,640]{1,0:T(8,128)(2,1)S(1)}, bf16[16,640]{1,0:T(8,128)(2,1)S(1)}, u32[]{:S(2)}, u32[]{:S(2)}) collective-permute-start(bf16[16,640]{1,0:T(8,128)(2,1)S(1)} %get-tuple-element.49), channel_id=1, source_target_pairs={{0,4},{2,6},{4,0},{6,2},{1,5},{3,7},{5,1},{7,3},{8,12},{10,14},{12... | collective-permute-start | bytes 61448 | tf_op jit(solution)/shard_map/ppermute | solution.py:220
  137.1 8.1 %collective-permute-start.10 = (bf16[16,640]{1,0:T(8,128)(2,1)S(1)}, bf16[16,640]{1,0:T(8,128)(2,1)S(1)}, u32[]{:S(2)}, u32[]{:S(2)}) collective-permute-start(bf16[16,640]{1,0:T(8,128)(2,1)S(1)} %get-tuple-element.50), channel_id=1, source_target_pairs={{0,2},{2,4},{4,6},{6,0},{1,3},{3,5},{5,7},{7,1},{8,10},{10,12},{12... | collective-permute-start | bytes 61448 | tf_op jit(solution)/shard_map/ppermute | solution.py:220

commit v3 on v2

v3 whole, which is shorter than its diff:
```python
import jax
import jax.numpy as jnp
from jax import lax
from jax.experimental import pallas as pl
from jax.experimental.pallas import tpu as pltpu
from jax.sharding import Mesh
from jax.sharding import PartitionSpec as P

NOPE = 128
ROPE = 64
LATENT = 512
VHEAD = 128
BLOCK = 128
QUERY = NOPE + ROPE
KEY = LATENT + ROPE
KEY_PAD = 640
HALF = LATENT // 2
DOC_MOST = 6
WINDOW = DOC_MOST * BLOCK
GROUP = 4
ROWS = GROUP * BLOCK
SCALE = QUERY ** -0.5
MIB = 1024 * 1024

bf16 = jnp.bfloat16
f32 = jnp.float32
NT = ((1,), (1,))
TN = ((0,), (0,))
HEAD_AXES = ("z", "y")


def mul(a, b, dims=((1,), (0,))):
    return lax.dot_general(a, b, (dims, ((), ())), preferred_element_type=f32)


def at_block(block):
    return pl.ds(pl.multiple_of(block * BLOCK, BLOCK), BLOCK)


def attention_kernel(
    place, query_ref, own_ref, other_ref, key_ref, value_ref, grad_ref, got_grad_ref,
    attended_ref, query_grad_ref, far_right_ref, far_left_ref, right_top_ref, right_low_ref,
    left_top_ref, left_low_ref, stay_ref, keep_ref, send_ref,
    keys, flipped, bias, total,
):
    group = pl.program_id(0)
    core, x_here, z_here, y_here = place[0], place[1], place[2], place[3]
    n_x = own_ref.shape[0]
    sides = range(2)
    firsts = [jnp.maximum(x_here * 2 + side - (DOC_MOST - 1), 0) for side in sides]

    @pl.when(group == 0)
    def _():
        for s in range(n_x):
            x = lax.rem(x_here + n_x - s, n_x)
            keys[at_block(2 * x + core), :] = own_ref[s]
            keys[at_block(2 * x + 1 - core), :] = other_ref[s]
        flipped[:LATENT, :] = jnp.transpose(keys[:, :LATENT])
        flipped[LATENT:, :] = jnp.transpose(keys[:, LATENT:])
        total[...] = jnp.zeros_like(total)
        for side in sides:
            key_at = firsts[side] * BLOCK + lax.broadcasted_iota(jnp.int32, (WINDOW, BLOCK), 0)
            query_at = (x_here * 2 + side) * BLOCK + lax.broadcasted_iota(jnp.int32, (WINDOW, BLOCK), 1)
            seen = (key_at >= place[4 + side] * BLOCK) & (key_at <= query_at)
            bias[side] = jnp.where(seen, f32(0.0), f32(-1e30))

    here = [pl.ds(pl.multiple_of(first * BLOCK, BLOCK), WINDOW) for first in firsts]
    window = [keys.at[here[side], :] for side in sides]
    heads = range(GROUP)
    at = [slice(e * BLOCK, (e + 1) * BLOCK) for e in heads]
    queries = [query_ref[side] for side in sides]
    nope = [[queries[side][:, e * QUERY:e * QUERY + NOPE] for e in heads] for side in sides]
    turned = [
        jnp.concatenate([queries[side][:, e * QUERY + NOPE:(e + 1) * QUERY] for e in heads], axis=0)
        for side in sides
    ]
    all_grads = [jnp.where(side == core, grad_ref[...], got_grad_ref[...]) for side in sides]
    grads = [[all_grads[side][:, e * VHEAD:(e + 1) * VHEAD] for e in heads] for side in sides]
    query_lat = [
        jnp.concatenate([mul(key_ref[e], nope[side][e], NT).astype(bf16) for e in heads], axis=1)
        for side in sides
    ]
    context_grad = [
        jnp.concatenate([mul(value_ref[e], grads[side][e], NT).astype(bf16) for e in heads], axis=1)
        for side in sides
    ]

    def scores_of(side):
        hidden = jnp.concatenate([bias[side]] * GROUP, axis=1)
        latents, rotary = window[side][:, :LATENT], window[side][:, LATENT:]
        return (mul(latents, query_lat[side]) + mul(rotary, turned[side], NT)) * SCALE + hidden

    def softmax_of(scores):
        top = jnp.max(scores, axis=0, keepdims=True)
        expo = jnp.exp(scores - top)
        return expo, 1.0 / jnp.sum(expo, axis=0, keepdims=True)

    def context_of(side, expo, inverse):
        context = (mul(flipped[:LATENT, here[side]], expo.astype(bf16)) * inverse).astype(bf16)
        delta = jnp.sum(
            context.astype(f32) * context_grad[side].astype(f32), axis=0, keepdims=True
        )
        return context, delta

    def score_grad_of(side, expo, inverse, delta):
        probs = expo * inverse
        grad = mul(window[side][:, :LATENT], context_grad[side]) - delta
        return (probs * grad * SCALE).astype(bf16), probs.astype(bf16)

    def lat_grad_of(side, score_grad, low):
        lat_grad = mul(flipped[:, here[side]], score_grad)
        out = total.at[here[side], :]
        out[:, :LATENT] += mul(score_grad, query_lat[side], NT) + mul(low, context_grad[side], NT)
        out[:, LATENT:] += mul(score_grad, turned[side])
        return lat_grad[:LATENT, :].astype(bf16), lat_grad[LATENT:, :]

    scores = [scores_of(side) for side in sides]
    soft = [softmax_of(scores[side]) for side in sides]
    contexts = [context_of(side, *soft[side]) for side in sides]
    score_grads = [score_grad_of(side, *soft[side], contexts[side][1]) for side in sides]
    lat_grads = [lat_grad_of(side, *score_grads[side]) for side in sides]

    for side in sides:
        slot = lax.rem(side + core, 2)
        pieces = []
        for e in heads:
            pieces.append(mul(lat_grads[side][0][:, at[e]], key_ref[e], TN))
            pieces.append(jnp.transpose(lat_grads[side][1][:, at[e]]))
            attended_ref[slot, :, e * VHEAD:(e + 1) * VHEAD] = mul(
                contexts[side][0][:, at[e]], value_ref[e], TN
            ).astype(bf16)
        query_grad_ref[slot] = jnp.concatenate(pieces, axis=1).astype(bf16)
    both = lambda parts, axis: jnp.concatenate(parts, axis=axis)
    for e in heads:
        grad = both(
            [
                mul(both([side[0][:, at[e]] for side in lat_grads], 1), both([side[e] for side in nope], 0)),
                mul(both([side[0][:, at[e]] for side in contexts], 1), both([side[e] for side in grads], 0)),
            ],
            1,
        ).astype(bf16)
        top, low = grad[:HALF], grad[HALF:]
        away = lax.rem(e - x_here + n_x, n_x)
        places = (
            ((stay_ref, slice(0, HALF), top), (stay_ref, slice(HALF, LATENT), low)),
            ((right_top_ref, slice(0, HALF), top), (right_low_ref, slice(0, HALF), low)),
            ((far_right_ref, slice(0, HALF), top), (far_left_ref, slice(0, HALF), low)),
            ((left_top_ref, slice(0, HALF), top), (left_low_ref, slice(0, HALF), low)),
        )
        for distance, writes in enumerate(places):

            @pl.when(away == distance)
            def _():
                for ref, where, value in writes:
                    ref[0, where, :] = value

    @pl.when(group == pl.num_programs(0) - 1)
    def _():
        n_z, n_y, _, rows = keep_ref.shape[:4]
        empty = jnp.zeros((rows, KEY_PAD - KEY), bf16)
        for dz in range(n_z):
            for dy in range(n_y):
                head = lax.rem(z_here + dz, n_z) * n_y + lax.rem(y_here + dy, n_y)
                for dx in range(n_x):
                    x = lax.rem(x_here + dx, n_x)
                    for ref, parity in ((keep_ref, core), (send_ref, 1 - core)):
                        start = pl.multiple_of((2 * x + parity) * BLOCK + head * rows, rows)
                        ref[dz, dy, dx, :, :KEY] = total[pl.ds(start, rows), :].astype(bf16)
                        ref[dz, dy, dx, :, KEY:] = empty


def attention(place, queries, own, other, key_up, value_up, out_grad, got_grad, n_z, n_y):
    heads = key_up.shape[0] // 2
    groups = heads // GROUP
    n_x = own.shape[0]
    tokens = 2 * n_x * BLOCK
    whole = lambda shape: pl.BlockSpec(shape, lambda g, place: (0,) * len(shape))
    weights_at = lambda g, place: (place[0] * groups + g, 0, 0)
    sides_at = lambda g, place: (0, 0, g)
    side_at = lambda g, place: (g, 0, 0)
    rows_shape = jax.ShapeDtypeStruct((n_z, n_y, n_x, BLOCK // (n_z * n_y), KEY_PAD), bf16)
    return pl.pallas_call(
        attention_kernel,
        grid_spec=pltpu.PrefetchScalarGridSpec(
            num_scalar_prefetch=1,
            grid=(groups,),
            in_specs=[
                pl.BlockSpec((2, BLOCK, GROUP * QUERY), sides_at),
                whole(own.shape),
                whole(other.shape),
                pl.BlockSpec((GROUP, LATENT, NOPE), weights_at),
                pl.BlockSpec((GROUP, LATENT, VHEAD), weights_at),
                pl.BlockSpec((BLOCK, GROUP * VHEAD), lambda g, place: (0, place[0] * groups + g)),
                pl.BlockSpec((BLOCK, GROUP * VHEAD), lambda g, place: (0, g)),
            ],
            out_specs=[
                pl.BlockSpec((2, BLOCK, GROUP * VHEAD), sides_at),
                pl.BlockSpec((2, BLOCK, GROUP * QUERY), sides_at),
                *[pl.BlockSpec((1, HALF, NOPE + VHEAD), side_at)] * 6,
                pl.BlockSpec((1, LATENT, NOPE + VHEAD), side_at),
                whole(rows_shape.shape),
                whole(rows_shape.shape),
            ],
            scratch_shapes=[
                pltpu.VMEM((tokens, KEY), bf16),
                pltpu.VMEM((KEY, tokens), bf16),
                pltpu.VMEM((2, WINDOW, BLOCK), f32),
                pltpu.VMEM((tokens, KEY), f32),
            ],
        ),
        out_shape=[
            jax.ShapeDtypeStruct((2, BLOCK, heads * VHEAD), bf16),
            jax.ShapeDtypeStruct((2, BLOCK, heads * QUERY), bf16),
            *[jax.ShapeDtypeStruct((groups, HALF, NOPE + VHEAD), bf16)] * 6,
            jax.ShapeDtypeStruct((groups, LATENT, NOPE + VHEAD), bf16),
            rows_shape,
            rows_shape,
        ],
        name="attention",
        compiler_params=pltpu.CompilerParams(
            dimension_semantics=("arbitrary",), vmem_limit_bytes=48 * MIB
        ),
        cost_estimate=pl.CostEstimate(
            flops=12_000_000_000, bytes_accessed=15_000_000, transcendentals=1_600_000
        ),
    )(place, queries, own, other, key_up, value_up, out_grad, got_grad)


def join(place, *pairs):
    def kernel(place, *refs):
        count = len(pairs)
        for n in range(count):
            mine_ref, got_ref, out_ref = refs[2 * n], refs[2 * n + 1], refs[2 * count + n]
            width = mine_ref.shape[1]
            for ref, core in ((mine_ref, place[0]), (got_ref, 1 - place[0])):
                out_ref[:, pl.ds(pl.multiple_of(core * width, 128), width)] = ref[...]

    whole = lambda shape: pl.BlockSpec(shape, lambda i, place: (0,) * len(shape))
    shapes = [(mine.shape[0], 2 * mine.shape[1]) for mine, _ in pairs]
    return pl.pallas_call(
        kernel,
        grid_spec=pltpu.PrefetchScalarGridSpec(
            num_scalar_prefetch=1,
            grid=(1,),
            in_specs=[whole(value.shape) for pair in pairs for value in pair],
            out_specs=[whole(shape) for shape in shapes],
        ),
        out_shape=[jax.ShapeDtypeStruct(shape, bf16) for shape in shapes],
        name="join",
    )(place, *[value for pair in pairs for value in pair])


def unfold(place, heads, pieces, begun):
    shape = jax.ShapeDtypeStruct((heads, LATENT, NOPE), f32)
    parts = [part for _, *parts in pieces for part in parts]
    operands = parts + [swapped(part) for part in parts]
    sides = parts[0].shape[0]
    n_x = heads // (2 * sides)
    count = 2 * len(pieces) * sides

    def kernel(place, *refs):
        sources = list(refs[:len(operands)])
        key_out, value_out, keys, values, sems = refs[-5:]
        started = []
        for n in range(2 * len(pieces)):
            x_away, *part = pieces[n % len(pieces)]
            core = place[0] if n < len(pieces) else 1 - place[0]
            x = lax.rem(place[1] + x_away, n_x)
            part = [sources.pop(0) for _ in part]
            for side in range(sides):
                slot = n * sides + side
                start = 0
                for ref in part:
                    rows = slice(start, start + ref.shape[1])
                    keys[slot, rows, :] = ref[side, :, :NOPE].astype(f32)
                    values[slot, rows, :] = ref[side, :, NOPE:].astype(f32)
                    start += ref.shape[1]
                head = core * (heads // 2) + side * n_x + x
                for which, (done, out) in enumerate(((keys, key_out), (values, value_out))):
                    copy = pltpu.make_async_copy(done.at[slot], out.at[head], sems.at[which, slot])
                    copy.start()
                    started.append(copy)
        for copy in started:
            copy.wait()

    first = 1 + len(operands)
    return pl.pallas_call(
        kernel,
        grid_spec=pltpu.PrefetchScalarGridSpec(
            num_scalar_prefetch=1,
            grid=(1,),
            in_specs=[pl.BlockSpec(part.shape, lambda i, place: (0, 0, 0)) for part in operands]
            + [pl.BlockSpec(memory_space=pl.ANY)] * len(begun),
            out_specs=[pl.BlockSpec(memory_space=pl.ANY)] * 2,
            scratch_shapes=[pltpu.VMEM((count, LATENT, NOPE), f32)] * 2
            + [pltpu.SemaphoreType.DMA((2, count))],
        ),
        out_shape=[shape, shape],
        input_output_aliases={first: 0, first + 1: 1} if begun else {},
        name="unfold",
        compiler_params=pltpu.CompilerParams(vmem_limit_bytes=24 * MIB),
        cost_estimate=pl.CostEstimate(flops=0, bytes_accessed=4_000_000, transcendentals=0),
    )(place, *operands, *begun)


def pack(queries, n_head):
    rows, lanes = queries.shape
    lanes //= 2 * n_head

    def kernel(query_ref, out_ref):
        for head in range(n_head):
            for core in range(2):
                at = (2 * head + core) * lanes
                out_ref[core * n_head + head] = query_ref[:, at:at + lanes]

    return pl.pallas_call(
        kernel,
        out_shape=jax.ShapeDtypeStruct((2 * n_head, rows, lanes), bf16),
        name="pack",
    )(queries)


def swapped(value):
    return lax.ppermute(value, "core", [(0, 1), (1, 0)])


def shifted(value, axis, steps):
    count = lax.axis_size(axis)
    return lax.ppermute(value, axis, [(i, (i + steps) % count) for i in range(count)])


def exchanged(value, axes):
    return lax.all_to_all(value, axes, 0, 0, tiled=True)


def copies(value, count):
    return jnp.broadcast_to(value[None], (count,) + value.shape)


def added(*terms):
    return sum(term.astype(f32) for term in terms)


def folded(rows, axis):
    count = rows.shape[0]
    return added(rows[0], *[shifted(rows[s], axis, s) for s in range(1, count)])


def on_device(queries, latent, key_up, value_up, out_grad, block_docs):
    n_head = lax.axis_size(HEAD_AXES)
    n_x = lax.axis_size("x")
    core = lax.axis_index("core")
    x_here = lax.axis_index("x")
    n_z, n_y = [lax.axis_size(axis) for axis in HEAD_AXES]
    docs = block_docs[0]
    doc_first = [jnp.sum((docs < docs[2 * x_here + side]).astype(jnp.int32)) for side in range(2)]
    place = jnp.stack(
        [core, x_here] + [lax.axis_index(axis) for axis in HEAD_AXES] + doc_first
        + [lax.axis_index("dp")]
    ).astype(jnp.int32)

    half = out_grad.shape[1] // 2
    arrived = pack(queries, n_head)
    own = exchanged(copies(latent, n_head), HEAD_AXES)
    own, arrived, out_grad = lax.optimization_barrier((own, arrived, out_grad))
    arrived = exchanged(arrived, ("core",) + HEAD_AXES).reshape(2, BLOCK, -1)
    own = own.reshape(BLOCK, KEY)
    own = jnp.stack([own] + [shifted(own, "x", s) for s in range(1, n_x)])
    other = swapped(own)
    got_grad = swapped(lax.dynamic_slice_in_dim(out_grad, (1 - core) * half, half, 1))

    attended, query_grad, *kv, rows_keep, rows_send = attention(
        place, arrived, own, other, key_up, value_up, out_grad, got_grad, n_z, n_y
    )
    after = lax.optimization_barrier
    heads = key_up.shape[0]
    far_right, far_left, right_top, right_low, left_top, left_low, stay = kv
    past_right, past_left = shifted(far_right, "x", 1), shifted(far_left, "x", -1)
    low, top = shifted(right_low, "x", 1), shifted(left_top, "x", -1)
    rows = added(rows_keep, swapped(rows_send)).astype(bf16)
    from_left = shifted(added(right_top, past_right).astype(bf16), "x", 1)
    from_right = shifted(added(left_low, past_left).astype(bf16), "x", -1)
    upper = added(stay[:, :HALF], from_left, top)
    lower = added(stay[:, HALF:], from_right, low)
    kv = jnp.concatenate([upper, lower], axis=1).astype(bf16)
    kv, rows, attended, query_grad = after((kv, rows, attended, query_grad))
    kv = added(kv, shifted(kv, "dp", 1)).astype(bf16)
    rows = folded(rows, HEAD_AXES[0]).astype(bf16)
    got = swapped(attended[1]), swapped(query_grad[1])
    kv, rows, got = after((kv, rows, got))
    left, right = shifted(kv, "x", 1), shifted(kv, "x", -1)
    rows = folded(rows, HEAD_AXES[1]).astype(bf16)
    attended, query_grad = join(place, (attended[0], got[0]), (query_grad[0], got[1]))
    grads = unfold(place, heads, [(0, kv)], [])
    left, right, rows, attended, query_grad, grads = after(
        (left, right, rows, attended, query_grad, grads)
    )
    far = shifted(left[:, :HALF], "x", 1), shifted(right[:, HALF:], "x", -1)
    rows = [rows[0]] + [shifted(rows[s], "x", s) for s in range(1, n_x)]
    grads = unfold(place, heads, [(n_x - 1, left), (1, right)], grads)
    far, rows, grads = after((far, rows, grads))
    grads = unfold(place, heads, [(2,) + tuple(far)], grads)
    latent_grad = added(*rows)[:, :KEY]
    key_up_grad, value_up_grad = grads
    return (attended, query_grad, latent_grad, key_up_grad, value_up_grad)


def solution(mesh):
    n_dp, n_head, n_blk = mesh.devices.shape
    fine = Mesh(
        mesh.devices.reshape(n_dp, n_head // 2, 2, n_blk // 2, 2), ("dp", "z", "y", "x", "core")
    )
    head, blk = HEAD_AXES, ("x", "core")
    return jax.shard_map(
        on_device,
        mesh=fine,
        in_specs=(
            P(("dp",) + blk + head, None),
            P(("dp",) + blk + head, None),
            P(head, None, None),
            P(head, None, None),
            P(("dp",) + blk, head),
            P("dp", None),
        ),
        out_specs=(
            P(("dp",) + blk, head),
            P(("dp",) + blk, head),
            P(("dp",) + blk + head, None),
            P(head, None, None),
            P(head, None, None),
        ),
        check_vma=False,
    )
```

time: 147 us -> 131 us (0.89)
  blocking collectives: 32.9 us -> 0 us
  starting transfers between devices: 33 us -> 53.7 us
  waiting for transfers between devices: 38 us -> 32.7 us
  Pallas kernels: 28.9 us -> 32.6 us
  other arithmetic: 5.66 us -> 3.44 us
    all_to_all x1 -> x0, blocking collectives: 32.9 us -> none  [exchanged(): return lax.all_to_all(value, axes, 0, 0, tiled=True)]
    ppermute x10 -> x21, starting transfers between devices: 8.86 us -> 26 us  [shifted(): lax.ppermute(value, axis, [(i, (i + steps) % count) for i in range(count)])]
    ppermute x4 -> x10, starting transfers between devices: 8.01 us -> 14.5 us  [swapped(): return lax.ppermute(value, 'core', [(0, 1), (1, 0)])]
    pallas_call x0 -> x2, Pallas kernels: none -> 5.12 us  [the longest x1 3.05 us: join(): pl.pallas_call(kernel, grid_spec=pltpu.PrefetchScalarGridSpec(num_scalar_...]
    ppermute x10 -> x21, waiting for transfers between devices: 27.2 us -> 22.7 us  [shifted(): lax.ppermute(value, axis, [(i, (i + steps) % count) for i in range(count)])]
    ppermute x4 -> x10, waiting for transfers between devices: 4.85 us -> 0.83 us  [swapped(): return lax.ppermute(value, 'core', [(0, 1), (1, 0)])]
    all_to_all x3 -> x2, waiting for transfers between devices: 5.94 us -> 9.11 us  [exchanged(): return lax.all_to_all(value, axes, 0, 0, tiled=True)]
    all_to_all x3 -> x2, starting transfers between devices: 16.1 us -> 13.2 us  [exchanged(): return lax.all_to_all(value, axes, 0, 0, tiled=True)]
  transfers between devices with their start and end apart: 17 -> 33, of which waited for: 8 -> 12; matrix products, arithmetic and copies ran while one was open for 6% -> 6% of each run, Pallas kernels for 6% -> 7%
where the time goes in v3:
time: 131 us
  starting transfers between devices  53.7 us (41%)
  waiting for transfers between devices  32.7 us (25%)
  Pallas kernels  32.6 us (25%)
  local copies, waits for them, and re-layouts  7.38 us (6%)
  other arithmetic  3.44 us (3%)
    ppermute x21, starting transfers between devices, shifted(): lax.ppermute(value, axis, [(i, (i + steps) % count) for i in range(count)])  26 us
    ppermute x21, waiting for transfers between devices, shifted(): lax.ppermute(value, axis, [(i, (i + steps) % count) for i in range(count)])  22.7 us
    pallas_call x1, Pallas kernels, attention(): pl.pallas_call(attention_kernel, grid_spec=pltpu.PrefetchScalarGridSpec(n...  20.9 us
    ppermute x10, starting transfers between devices, swapped(): return lax.ppermute(value, 'core', [(0, 1), (1, 0)])  14.5 us
    all_to_all x2, starting transfers between devices, exchanged(): return lax.all_to_all(value, axes, 0, 0, tiled=True)  13.2 us
    all_to_all x2, waiting for transfers between devices, exchanged(): return lax.all_to_all(value, axes, 0, 0, tiled=True)  9.11 us
    pallas_call x3, Pallas kernels, unfold(): pl.pallas_call(kernel, grid_spec=pltpu.PrefetchScalarGridSpec(num_scalar_...  6.57 us
    pallas_call x1, Pallas kernels, join(): pl.pallas_call(kernel, grid_spec=pltpu.PrefetchScalarGridSpec(num_scalar_...  3.05 us
  transfers between devices with their start and end apart: 33, of which 12 were waited for; matrix products, arithmetic and copies ran while one was open for 6% of the time, Pallas kernels for 7%

profile of v3, /device:TPU:1, one launch (start us, length us, event | category | flops | bytes accessed | tf_op | source)
XLA Modules:
  0.0 130.8 jit_solution(6205887719316502341)
XLA Ops:
  0.7 1.5 %broadcast_in_dim.2 = bf16[8,16,576]{2,1,0:T(8,128)(2,1)} broadcast(bf16[16,576]{1,0:T(8,128)(2,1)} %param.7), dimensions={1,2} | broadcast | bytes 165888 | tf_op jit(solution)/shard_map/broadcast_in_dim | solution.py:337
  2.1 6.9 %all-to-all-start = ((bf16[8,16,576]{2,1,0:T(8,128)(2,1)}), bf16[8,16,576]{2,1,0:T(8,128)(2,1)S(1)}, u32[]{:S(2)}, u32[]{:S(2)}) async-start(bf16[8,16,576]{2,1,0:T(8,128)(2,1)} %broadcast_in_dim.2), calls=%async_computation | async-start | bytes 327680 | tf_op jit(solution)/shard_map/all_to_all | solution.py:333
  9.0 2.1 %pack.1 = bf16[16,16,1536]{2,1,0:T(8,128)(2,1)} custom-call(bf16[16,24576]{1,0:T(8,128)(2,1)} %query_ref.1), custom_call_target="tpu_custom_call" | custom-call | tf_op jit(solution)/shard_map/pack/pallas_call | solution.py:316
  11.1 3.7 %all-to-all-done = bf16[8,16,576]{2,1,0:T(8,128)(2,1)S(1)} async-done(((bf16[8,16,576]{2,1,0:T(8,128)(2,1)}), bf16[8,16,576]{2,1,0:T(8,128)(2,1)S(1)}, u32[]{:S(2)}, u32[]{:S(2)}) %all-to-all-start) | async-done | bytes 147488 | tf_op jit(solution)/shard_map/all_to_all | solution.py:333
  14.7 1.2 collective-permute-start
  15.9 2.5 %collective-permute-start.1 = (bf16[128,576]{1,0:T(8,128)(2,1)S(1)}, bf16[128,576]{1,0:T(8,128)(2,1)S(1)}, u32[]{:S(2)}, u32[]{:S(2)}) collective-permute-start(bf16[128,576]{1,0:T(8,128)(2,1)S(1)} %bitcast.47), channel_id=1, source_target_pairs={{0,4},{2,6},{4,0},{6,2},{1,5},{3,7},{5,1},{7,3},{8,12},{10,14},{12... | collective-permute-start | bytes 442376 | tf_op jit(solution)/shard_map/ppermute | solution.py:329
  18.4 1.2 collective-permute-start.2
  19.5 6.4 %all-to-all-start.1 = ((bf16[16,16,1536]{2,1,0:T(8,128)(2,1)}), bf16[16,16,1536]{2,1,0:T(8,128)(2,1)S(1)}, u32[]{:S(2)}, u32[]{:S(2)}) async-start(bf16[16,16,1536]{2,1,0:T(8,128)(2,1)} %pack.1), calls=%async_computation.1 | async-start | bytes 1572864 | tf_op jit(solution)/shard_map/all_to_all | solution.py:333
  26.4 1.2 collective-permute-start.3
  27.6 0.7 constant_dynamic-slice_fusion
  28.4 0.6 constant_dynamic-slice_fusion.2
  29.0 1.9 %fusion.5 = (s32[]{:T(128)}, s32[]{:T(128)}) fusion(s32[1,8]{1,0:T(1,128)S(1)} %copy-done.7, s32[]{:T(128)} %bitcast.6, s32[]{:T(128)} %bitcast.4), kind=kLoop, calls=%fused_computation.33 | loop fusion | flops 46 | bytes 48 | tf_op jit(solution)/shard_map/reduce_sum | solution.py:356
  30.9 1.3 %stack.43.place = s32[7]{0:T(128)S(1)} concatenate(s32[1]{0:T(128)} %bitcast, s32[1]{0:T(128)} %bitcast.1, s32[1]{0:T(128)} %bitcast.2, s32[1]{0:T(128)} %bitcast.3, s32[1]{0:T(128)} %bitcast.5, s32[1]{0:T(128)} %bitcast.7, s32[1]{0:T(128)} %bitcast.8), dimensions={0} | concatenate | bytes 56 | tf_op jit(solution)/shard_map/stack | solution.py:357
  32.6 5.5 %all-to-all-done.1 = bf16[16,16,1536]{2,1,0:T(8,128)(2,1)S(1)} async-done(((bf16[16,16,1536]{2,1,0:T(8,128)(2,1)}), bf16[16,16,1536]{2,1,0:T(8,128)(2,1)S(1)}, u32[]{:S(2)}, u32[]{:S(2)}) %all-to-all-start.1) | async-done | bytes 786464 | tf_op jit(solution)/shard_map/all_to_all | solution.py:333
  38.1 0.9 copy-done.3
  38.9 20.9 %attention.1 = (bf16[2,128,1024]{2,1,0:T(8,128)(2,1)S(1)}, bf16[2,128,1536]{2,1,0:T(8,128)(2,1)}, bf16[2,256,256]{2,1,0:T(8,128)(2,1)S(1)}, bf16[2,256,256]{2,1,...) custom-call(s32[7]{0:T(128)S(1)} %stack.43.place, ...), custom_call_target="tpu_custom_call" | custom-call | flops 12000000000 | bytes 15000000 | tf_op jit(solution)/shard_map/attention/pallas_call | solution.py:182
  59.9 1.5 %collective-permute-start.5 = (bf16[2,256,256]{2,1,0:T(8,128)(2,1)S(1)}, bf16[2,256,256]{2,1,0:T(8,128)(2,1)S(1)}, u32[]{:S(2)}, u32[]{:S(2)}) collective-permute-start(bf16[2,256,256]{2,1,0:T(8,128)(2,1)S(1)} %get-tuple-element.55), channel_id=1, source_target_pairs={{0,2},{2,4},{4,6},{6,0},{1,3},{3,5},{5,7},{7,1},{8,10},{10,12},{12... | collective-permute-start | bytes 786440 | tf_op jit(solution)/shard_map/ppermute | solution.py:329
  61.7 2.3 %collective-permute-start.7 = (bf16[2,256,256]{2,1,0:T(8,128)(2,1)S(1)}, bf16[2,256,256]{2,1,0:T(8,128)(2,1)S(1)}, u32[]{:S(2)}, u32[]{:S(2)}) collective-permute-start(bf16[2,256,256]{2,1,0:T(8,128)(2,1)S(1)} %get-tuple-element.56), channel_id=1, source_target_pairs={{0,6},{2,0},{4,2},{6,4},{1,7},{3,1},{5,3},{7,5},{8,14},{10,8},{12,... | collective-permute-start | bytes 786440 | tf_op jit(solution)/shard_map/ppermute | solution.py:329
  64.0 3.4 %collective-permute-done.8 = bf16[2,256,256]{2,1,0:T(8,128)(2,1)S(1)} collective-permute-done((bf16[2,256,256]{2,1,0:T(8,128)(2,1)S(1)}, bf16[2,256,256]{2,1,0:T(8,128)(2,1)S(1)}, u32[]{:S(2)}, u32[]{:S(2)}) %collective-permute-start.8) | collective-permute-done | bytes 262176 | tf_op jit(solution)/shard_map/ppermute | solution.py:329
  67.4 1.4 %collective-permute-start.9 = (bf16[2,256,256]{2,1,0:T(8,128)(2,1)S(1)}, bf16[2,256,256]{2,1,0:T(8,128)(2,1)S(1)}, u32[]{:S(2)}, u32[]{:S(2)}) collective-permute-start(bf16[2,256,256]{2,1,0:T(8,128)(2,1)S(1)} %add_convert_fusion.3), channel_id=1, source_target_pairs={{0,6},{2,0},{4,2},{6,4},{1,7},{3,1},{5,3},{7,5},{8,14},{10,8},{12,... | collective-permute-start | bytes 786440 | tf_op jit(solution)/shard_map/ppermute | solution.py:329
  69.1 2.6 %collective-permute-start.11 = (bf16[4,2,4,16,640]{4,3,2,1,0:T(8,128)(2,1)S(1)}, bf16[4,2,4,16,640]{4,3,2,1,0:T(8,128)(2,1)S(1)}, u32[]{:S(2)}, u32[]{:S(2)}) collective-permute-start(bf16[4,2,4,16,640]{4,3,2,1,0:T(8,128)(2,1)S(1)} %get-tuple-element.61), channel_id=1, source_target_pairs={{0,1},{1,0},{2,3},{3,2},{4,5},{5,4},{6,7},{7,6},{8,9},{9,8},{10,11... | collective-permute-start | bytes 1966088 | tf_op jit(solution)/shard_map/ppermute | solution.py:324
  71.7 2.5 %collective-permute-done.10 = bf16[2,256,256]{2,1,0:T(8,128)(2,1)S(1)} collective-permute-done((bf16[2,256,256]{2,1,0:T(8,128)(2,1)S(1)}, bf16[2,256,256]{2,1,0:T(8,128)(2,1)S(1)}, u32[]{:S(2)}, u32[]{:S(2)}) %collective-permute-start.10) | collective-permute-done | bytes 262176 | tf_op jit(solution)/shard_map/ppermute | solution.py:329
  74.2 4.4 %collective-permute-done.9 = bf16[2,256,256]{2,1,0:T(8,128)(2,1)S(1)} collective-permute-done((bf16[2,256,256]{2,1,0:T(8,128)(2,1)S(1)}, bf16[2,256,256]{2,1,0:T(8,128)(2,1)S(1)}, u32[]{:S(2)}, u32[]{:S(2)}) %collective-permute-start.9) | collective-permute-done | bytes 262176 | tf_op jit(solution)/shard_map/ppermute | solution.py:329
  78.6 1.2 collective-permute-done.6
  80.4 1.8 %collective-permute-start.14 = (bf16[2,4,16,640]{3,2,1,0:T(8,128)(2,1)S(1)}, bf16[2,4,16,640]{3,2,1,0:T(8,128)(2,1)S(1)}, u32[]{:S(2)}, u32[]{:S(2)}) collective-permute-start(bf16[2,4,16,640]{3,2,1,0:T(8,128)(2,1)S(1)} %get-tuple-element.101), channel_id=1, source_target_pairs={{0,32},{16,48},{32,0},{48,16},{1,33},{17,49},{33,1},{49,17},{2,34}... | collective-permute-start | bytes 491528 | tf_op jit(solution)/shard_map/ppermute | solution.py:329
  82.1 1.2 collective-permute-start.15
  83.3 2.6 %collective-permute-start.12 = (bf16[2,512,256]{2,1,0:T(8,128)(2,1)S(1)}, bf16[2,512,256]{2,1,0:T(8,128)(2,1)S(1)}, u32[]{:S(2)}, u32[]{:S(2)}) collective-permute-start(bf16[2,512,256]{2,1,0:T(8,128)(2,1)S(1)} %pad_maximum_fusion.1), channel_id=1, source_target_pairs={{0,64},{64,0},{1,65},{65,1},{2,66},{66,2},{3,67},{67,3},{4,68},{68... | collective-permute-start | bytes 1572872 | tf_op jit(solution)/shard_map/ppermute | solution.py:329
  85.9 0.8 slice_bitcast_fusion
  86.7 3.0 %collective-permute-start.17 = (bf16[128,1536]{1,0:T(8,128)(2,1)S(1)}, bf16[128,1536]{1,0:T(8,128)(2,1)S(1)}, u32[]{:S(2)}, u32[]{:S(2)}) collective-permute-start(bf16[128,1536]{1,0:T(8,128)(2,1)S(1)} %get-tuple-element.98), channel_id=1, source_target_pairs={{0,1},{1,0},{2,3},{3,2},{4,5},{5,4},{6,7},{7,6},{8,9},{9,8},{10,11... | collective-permute-start | bytes 1179656 | tf_op jit(solution)/shard_map/ppermute | solution.py:324
  89.7 0.7 slice_bitcast_fusion.2
  90.4 1.3 collective-permute-start.16
  91.8 3.7 %collective-permute-done.12 = bf16[2,512,256]{2,1,0:T(8,128)(2,1)S(1)} collective-permute-done((bf16[2,512,256]{2,1,0:T(8,128)(2,1)S(1)}, bf16[2,512,256]{2,1,0:T(8,128)(2,1)S(1)}, u32[]{:S(2)}, u32[]{:S(2)}) %collective-permute-start.12) | collective-permute-done | bytes 524320 | tf_op jit(solution)/shard_map/ppermute | solution.py:329
  95.7 3.7 %collective-permute-start.21 = (bf16[2,512,256]{2,1,0:T(8,128)(2,1)S(1)}, bf16[2,512,256]{2,1,0:T(8,128)(2,1)S(1)}, u32[]{:S(2)}, u32[]{:S(2)}) collective-permute-start(bf16[2,512,256]{2,1,0:T(8,128)(2,1)S(1)} %add_convert_fusion.1.refs_0_), channel_id=1, source_target_pairs={{0,1},{1,0},{2,3},{3,2},{4,5},{5,4},{6,7},{7,6},{8,9},{9,8},{10,11... | collective-permute-start | bytes 1572872 | tf_op jit(solution)/shard_map/ppermute | solution.py:324
  99.4 2.7 %collective-permute-start.19 = (bf16[2,512,256]{2,1,0:T(8,128)(2,1)S(1)}, bf16[2,512,256]{2,1,0:T(8,128)(2,1)S(1)}, u32[]{:S(2)}, u32[]{:S(2)}) collective-permute-start(bf16[2,512,256]{2,1,0:T(8,128)(2,1)S(1)} %add_convert_fusion.1.refs_0_), channel_id=1, source_target_pairs={{0,6},{2,0},{4,2},{6,4},{1,7},{3,1},{5,3},{7,5},{8,14},{10,8},{12,... | collective-permute-start | bytes 1572872 | tf_op jit(solution)/shard_map/ppermute | solution.py:329
  102.1 1.1 collective-permute-start.20
  103.2 3.1 %join.1 = (bf16[128,2048]{1,0:T(8,128)(2,1)}, bf16[128,3072]{1,0:T(8,128)(2,1)}) custom-call(s32[7]{0:T(128)} %copy-done.1, bf16[128,1024]{1,0:T(8,128)(2,1)} %get-tuple-element.102.refs_0_, bf16[128,1024]{1,0:T(8,128)(2,1)} %copy-done.6, bf16[128,1536]{1,0:T(8,128)(2,1)} %get-tuple-element.97.refs_2_, bf16[128,1536]{1,0:T(8,128)(2,1)} %copy-done.5), custom_call_target="tpu_custom_call" | custom-call | tf_op jit(solution)/shard_map/join/pallas_call | solution.py:240
  106.3 1.9 %unfold.3 = (f32[16,512,128]{2,1,0:T(8,128)}, f32[16,512,128]{2,1,0:T(8,128)}) custom-call(s32[7]{0:T(128)S(1)} %copy-done.2, bf16[2,512,256]{2,1,0:T(8,128)(2,1)S(1)} %add_convert_fusion.1.refs_0_, bf16[2,512,256]{2,1,0:T(8,128)(2,1)S(1)} %collective-permute-done.21.refs_1_), custom_call_target="tpu_custom_call" | custom-call | bytes 4000000 | tf_op jit(solution)/shard_map/unfold/pallas_call | solution.py:287
  108.2 5.9 %collective-permute-done.18.refs_0_ = bf16[2,512,256]{2,1,0:T(8,128)(2,1)S(1)} collective-permute-done((bf16[2,512,256]{2,1,0:T(8,128)(2,1)S(1)}, bf16[2,512,256]{2,1,0:T(8,128)(2,1)S(1)}, u32[]{:S(2)}, u32[]{:S(2)}) %collective-permute-start.18) | collective-permute-done | bytes 524320 | tf_op jit(solution)/shard_map/ppermute | solution.py:329
  114.1 0.9 collective-permute-start.27
  115.1 2.7 %collective-permute-start.23 = (bf16[2,256,256]{2,1,0:T(8,128)(2,1)S(1)}, bf16[2,256,256]{2,1,0:T(8,128)(2,1)S(1)}, u32[]{:S(2)}, u32[]{:S(2)}) collective-permute-start(bf16[2,256,256]{2,1,0:T(8,128)(2,1)S(1)} %slice.70), channel_id=1, source_target_pairs={{0,6},{2,0},{4,2},{6,4},{1,7},{3,1},{5,3},{7,5},{8,14},{10,8},{12,... | collective-permute-start | bytes 786440 | tf_op jit(solution)/shard_map/ppermute | solution.py:329
  118.0 2.5 %collective-permute-start.25 = (bf16[16,640]{1,0:T(8,128)(2,1)S(1)}, bf16[16,640]{1,0:T(8,128)(2,1)S(1)}, u32[]{:S(2)}, u32[]{:S(2)}) collective-permute-start(bf16[16,640]{1,0:T(8,128)(2,1)S(1)} %get-tuple-element.107), channel_id=1, source_target_pairs={{0,4},{2,6},{4,0},{6,2},{1,5},{3,7},{5,1},{7,3},{8,12},{10,14},{12... | collective-permute-start | bytes 61448 | tf_op jit(solution)/shard_map/ppermute | solution.py:329
  120.5 0.6 collective-permute-start.26
  121.1 2.7 %unfold.4 = (f32[16,512,128]{2,1,0:T(8,128)}, f32[16,512,128]{2,1,0:T(8,128)}) custom-call(s32[7]{0:T(128)S(1)} %copy-done.2, bf16[2,512,256]{2,1,0:T(8,128)(2,1)S(1)} %collective-permute-done.18.refs_0_, bf16[2,512,256]{2,1,0:T(8,128)(2,1)S(1)} %collective-permute-done.19.refs_1_, ...), custom_call_target="tpu_custom_call", output_to_operand_aliasing={{0}: (5, {}), {1}: (6, {})} | custom-call | bytes 4000000 | tf_op jit(solution)/shard_map/unfold/pallas_call | solution.py:287
  124.1 1.3 %collective-permute-done.25 = bf16[16,640]{1,0:T(8,128)(2,1)S(1)} collective-permute-done((bf16[16,640]{1,0:T(8,128)(2,1)S(1)}, bf16[16,640]{1,0:T(8,128)(2,1)S(1)}, u32[]{:S(2)}, u32[]{:S(2)}) %collective-permute-start.25) | collective-permute-done | bytes 20512 | tf_op jit(solution)/shard_map/ppermute | solution.py:329
  125.5 1.7 %collective-permute-start.29 = (bf16[2,256,256]{2,1,0:T(8,128)(2,1)S(1)}, bf16[2,256,256]{2,1,0:T(8,128)(2,1)S(1)}, u32[]{:S(2)}, u32[]{:S(2)}) collective-permute-start(bf16[2,256,256]{2,1,0:T(8,128)(2,1)S(1)} %collective-permute-done.22.refs_0_), channel_id=1, source_target_pairs={{0,1},{1,0},{2,3},{3,2},{4,5},{5,4},{6,7},{7,6},{8,9},{9,8},{10,11... | collective-permute-start | bytes 786440 | tf_op jit(solution)/shard_map/ppermute | solution.py:324
  127.3 0.6 convert_add_fusion.2
  127.9 0.4 collective-permute-done.29.refs_2_
  128.7 1.9 %unfold.5 = (f32[16,512,128]{2,1,0:T(8,128)}, f32[16,512,128]{2,1,0:T(8,128)}) custom-call(s32[7]{0:T(128)S(1)} %copy-done.2, bf16[2,256,256]{2,1,0:T(8,128)(2,1)S(1)} %collective-permute-done.22.refs_0_, bf16[2,256,256]{2,1,0:T(8,128)(2,1)S(1)} %collective-permute-done.23.refs_1_, ...), custom_call_target="tpu_custom_call", output_to_operand_aliasing={{0}: (5, {}), {1}: (6, {})} | custom-call | bytes 4000000 | tf_op jit(solution)/shard_map/unfold/pallas_call | solution.py:287
  (64 shorter events, 3.4 us)
Async XLA Ops:
  0.6 27.0 %copy-start = (bf16[128,2048]{1,0:T(8,128)(2,1)S(1)}, bf16[128,2048]{1,0:T(8,128)(2,1)}, u32[]{:S(2)}) copy-start(bf16[128,2048]{1,0:T(8,128)(2,1)} %grad_ref) | copy-start | bytes 1572868
  0.6 27.7 %copy-start.7 = (s32[1,8]{1,0:T(1,128)S(1)}, s32[1,8]{1,0:T(1,128)}, u32[]{:S(2)}) copy-start(s32[1,8]{1,0:T(1,128)} %param.11) | copy-start | bytes 100
  2.1 12.6 %all-to-all-start = ((bf16[8,16,576]{2,1,0:T(8,128)(2,1)}), bf16[8,16,576]{2,1,0:T(8,128)(2,1)S(1)}, u32[]{:S(2)}, u32[]{:S(2)}) async-start(bf16[8,16,576]{2,1,0:T(8,128)(2,1)} %broadcast_in_dim.2), calls=%async_computation | async-start | bytes 327680 | tf_op jit(solution)/shard_map/all_to_all | solution.py:333
  14.7 11.2 %collective-permute-start = (bf16[128,576]{1,0:T(8,128)(2,1)S(1)}, bf16[128,576]{1,0:T(8,128)(2,1)S(1)}, u32[]{:S(2)}, u32[]{:S(2)}) collective-permute-start(bf16[128,576]{1,0:T(8,128)(2,1)S(1)} %bitcast.46), channel_id=1, source_target_pairs={{0,2},{2,4},{4,6},{6,0},{1,3},{3,5},{5,7},{7,1},{8,10},{10,12},{12... | collective-permute-start | bytes 442376 | tf_op jit(solution)/shard_map/ppermute | solution.py:329
  15.9 10.0 %collective-permute-start.1 = (bf16[128,576]{1,0:T(8,128)(2,1)S(1)}, bf16[128,576]{1,0:T(8,128)(2,1)S(1)}, u32[]{:S(2)}, u32[]{:S(2)}) collective-permute-start(bf16[128,576]{1,0:T(8,128)(2,1)S(1)} %bitcast.47), channel_id=1, source_target_pairs={{0,4},{2,6},{4,0},{6,2},{1,5},{3,7},{5,1},{7,3},{8,12},{10,14},{12... | collective-permute-start | bytes 442376 | tf_op jit(solution)/shard_map/ppermute | solution.py:329
  18.4 7.5 %collective-permute-start.2 = (bf16[128,576]{1,0:T(8,128)(2,1)S(1)}, bf16[128,576]{1,0:T(8,128)(2,1)S(1)}, u32[]{:S(2)}, u32[]{:S(2)}) collective-permute-start(bf16[128,576]{1,0:T(8,128)(2,1)S(1)} %bitcast.48), channel_id=1, source_target_pairs={{0,6},{2,0},{4,2},{6,4},{1,7},{3,1},{5,3},{7,5},{8,14},{10,8},{12,... | collective-permute-start | bytes 442376 | tf_op jit(solution)/shard_map/ppermute | solution.py:329
  19.5 18.5 %all-to-all-start.1 = ((bf16[16,16,1536]{2,1,0:T(8,128)(2,1)}), bf16[16,16,1536]{2,1,0:T(8,128)(2,1)S(1)}, u32[]{:S(2)}, u32[]{:S(2)}) async-start(bf16[16,16,1536]{2,1,0:T(8,128)(2,1)} %pack.1), calls=%async_computation.1 | async-start | bytes 1572864 | tf_op jit(solution)/shard_map/all_to_all | solution.py:333
  26.4 5.9 %collective-permute-start.3 = (bf16[4,128,576]{1,2,0:T(8,128)(2,1)S(1)}, bf16[4,128,576]{1,2,0:T(8,128)(2,1)S(1)}, u32[]{:S(2)}, u32[]{:S(2)}) collective-permute-start(bf16[4,128,576]{1,2,0:T(8,128)(2,1)S(1)} %copy.15), channel_id=1, source_target_pairs={{0,1},{1,0},{2,3},{3,2},{4,5},{5,4},{6,7},{7,6},{8,9},{9,8},{10,11... | collective-permute-start | bytes 1769480 | tf_op jit(solution)/shard_map/ppermute | solution.py:324
  28.3 4.3 %collective-permute-start.4 = (bf16[128,1024]{1,0:T(8,128)(2,1)}, bf16[128,1024]{1,0:T(8,128)(2,1)S(1)}, u32[]{:S(2)}, u32[]{:S(2)}) collective-permute-start(bf16[128,1024]{1,0:T(8,128)(2,1)} %constant_dynamic-slice_fusion), channel_id=1, source_target_pairs={{0,1},{1,0},{2,3},{3,2},{4,5},{5,4},{6,7},{7,6},{8,9},{9,8},{10,11... | collective-permute-start | bytes 786440 | tf_op jit(solution)/shard_map/ppermute | solution.py:324
  32.3 27.5 %copy-start.1 = (s32[7]{0:T(128)}, s32[7]{0:T(128)S(1)}, u32[]{:S(2)}) copy-start(s32[7]{0:T(128)S(1)} %stack.43.place) | copy-start | bytes 88
  38.1 0.9 copy-start.3
  59.8 26.1 %copy-start.4 = (bf16[2,128,1536]{2,1,0:T(8,128)(2,1)S(1)}, bf16[2,128,1536]{2,1,0:T(8,128)(2,1)}, u32[]{:S(2)}) copy-start(bf16[2,128,1536]{2,1,0:T(8,128)(2,1)} %get-tuple-element.67) | copy-start | bytes 2359300
  59.8 7.6 %collective-permute-start.8 = (bf16[2,256,256]{2,1,0:T(8,128)(2,1)S(1)}, bf16[2,256,256]{2,1,0:T(8,128)(2,1)S(1)}, u32[]{:S(2)}, u32[]{:S(2)}) collective-permute-start(bf16[2,256,256]{2,1,0:T(8,128)(2,1)S(1)} %get-tuple-element.58), channel_id=1, source_target_pairs={{0,6},{2,0},{4,2},{6,4},{1,7},{3,1},{5,3},{7,5},{8,14},{10,8},{12,... | collective-permute-start | bytes 786440 | tf_op jit(solution)/shard_map/ppermute | solution.py:329
  59.9 9.0 %collective-permute-start.5 = (bf16[2,256,256]{2,1,0:T(8,128)(2,1)S(1)}, bf16[2,256,256]{2,1,0:T(8,128)(2,1)S(1)}, u32[]{:S(2)}, u32[]{:S(2)}) collective-permute-start(bf16[2,256,256]{2,1,0:T(8,128)(2,1)S(1)} %get-tuple-element.55), channel_id=1, source_target_pairs={{0,2},{2,4},{4,6},{6,0},{1,3},{3,5},{5,7},{7,1},{8,10},{10,12},{12... | collective-permute-start | bytes 786440 | tf_op jit(solution)/shard_map/ppermute | solution.py:329
  61.3 12.8 %collective-permute-start.10 = (bf16[2,256,256]{2,1,0:T(8,128)(2,1)S(1)}, bf16[2,256,256]{2,1,0:T(8,128)(2,1)S(1)}, u32[]{:S(2)}, u32[]{:S(2)}) collective-permute-start(bf16[2,256,256]{2,1,0:T(8,128)(2,1)S(1)} %get-tuple-element.59), channel_id=1, source_target_pairs={{0,2},{2,4},{4,6},{6,0},{1,3},{3,5},{5,7},{7,1},{8,10},{10,12},{12... | collective-permute-start | bytes 786440 | tf_op jit(solution)/shard_map/ppermute | solution.py:329
  61.7 12.5 %collective-permute-start.7 = (bf16[2,256,256]{2,1,0:T(8,128)(2,1)S(1)}, bf16[2,256,256]{2,1,0:T(8,128)(2,1)S(1)}, u32[]{:S(2)}, u32[]{:S(2)}) collective-permute-start(bf16[2,256,256]{2,1,0:T(8,128)(2,1)S(1)} %get-tuple-element.56), channel_id=1, source_target_pairs={{0,6},{2,0},{4,2},{6,4},{1,7},{3,1},{5,3},{7,5},{8,14},{10,8},{12,... | collective-permute-start | bytes 786440 | tf_op jit(solution)/shard_map/ppermute | solution.py:329
  67.4 11.2 %collective-permute-start.9 = (bf16[2,256,256]{2,1,0:T(8,128)(2,1)S(1)}, bf16[2,256,256]{2,1,0:T(8,128)(2,1)S(1)}, u32[]{:S(2)}, u32[]{:S(2)}) collective-permute-start(bf16[2,256,256]{2,1,0:T(8,128)(2,1)S(1)} %add_convert_fusion.3), channel_id=1, source_target_pairs={{0,6},{2,0},{4,2},{6,4},{1,7},{3,1},{5,3},{7,5},{8,14},{10,8},{12,... | collective-permute-start | bytes 786440 | tf_op jit(solution)/shard_map/ppermute | solution.py:329
  68.9 10.9 %collective-permute-start.6 = (bf16[2,256,256]{2,1,0:T(8,128)(2,1)S(1)}, bf16[2,256,256]{2,1,0:T(8,128)(2,1)S(1)}, u32[]{:S(2)}, u32[]{:S(2)}) collective-permute-start(bf16[2,256,256]{2,1,0:T(8,128)(2,1)S(1)} %add_convert_fusion.5), channel_id=1, source_target_pairs={{0,2},{2,4},{4,6},{6,0},{1,3},{3,5},{5,7},{7,1},{8,10},{10,12},{12... | collective-permute-start | bytes 786440 | tf_op jit(solution)/shard_map/ppermute | solution.py:329
  69.1 10.9 %collective-permute-start.11 = (bf16[4,2,4,16,640]{4,3,2,1,0:T(8,128)(2,1)S(1)}, bf16[4,2,4,16,640]{4,3,2,1,0:T(8,128)(2,1)S(1)}, u32[]{:S(2)}, u32[]{:S(2)}) collective-permute-start(bf16[4,2,4,16,640]{4,3,2,1,0:T(8,128)(2,1)S(1)} %get-tuple-element.61), channel_id=1, source_target_pairs={{0,1},{1,0},{2,3},{3,2},{4,5},{5,4},{6,7},{7,6},{8,9},{9,8},{10,11... | collective-permute-start | bytes 1966088 | tf_op jit(solution)/shard_map/ppermute | solution.py:324
  80.2 26.0 %copy-start.2 = (s32[7]{0:T(128)S(1)}, s32[7]{0:T(128)}, u32[]{:S(2)}) copy-start(s32[7]{0:T(128)} %copy-done.1) | copy-start | bytes 88
  80.3 10.1 %collective-permute-start.13 = (bf16[2,4,16,640]{3,2,1,0:T(8,128)(2,1)S(1)}, bf16[2,4,16,640]{3,2,1,0:T(8,128)(2,1)S(1)}, u32[]{:S(2)}, u32[]{:S(2)}) collective-permute-start(bf16[2,4,16,640]{3,2,1,0:T(8,128)(2,1)S(1)} %get-tuple-element.99), channel_id=1, source_target_pairs={{0,16},{16,32},{32,48},{48,0},{1,17},{17,33},{33,49},{49,1},{2,18}... | collective-permute-start | bytes 491528 | tf_op jit(solution)/shard_map/ppermute | solution.py:329
  80.4 11.3 %collective-permute-start.14 = (bf16[2,4,16,640]{3,2,1,0:T(8,128)(2,1)S(1)}, bf16[2,4,16,640]{3,2,1,0:T(8,128)(2,1)S(1)}, u32[]{:S(2)}, u32[]{:S(2)}) collective-permute-start(bf16[2,4,16,640]{3,2,1,0:T(8,128)(2,1)S(1)} %get-tuple-element.101), channel_id=1, source_target_pairs={{0,32},{16,48},{32,0},{48,16},{1,33},{17,49},{33,1},{49,17},{2,34}... | collective-permute-start | bytes 491528 | tf_op jit(solution)/shard_map/ppermute | solution.py:329
  82.1 9.6 %collective-permute-start.15 = (bf16[2,4,16,640]{3,2,1,0:T(8,128)(2,1)S(1)}, bf16[2,4,16,640]{3,2,1,0:T(8,128)(2,1)S(1)}, u32[]{:S(2)}, u32[]{:S(2)}) collective-permute-start(bf16[2,4,16,640]{3,2,1,0:T(8,128)(2,1)S(1)} %get-tuple-element.100), channel_id=1, source_target_pairs={{0,48},{16,0},{32,16},{48,32},{1,49},{17,1},{33,17},{49,33},{2,50}... | collective-permute-start | bytes 491528 | tf_op jit(solution)/shard_map/ppermute | solution.py:329
  83.3 12.2 %collective-permute-start.12 = (bf16[2,512,256]{2,1,0:T(8,128)(2,1)S(1)}, bf16[2,512,256]{2,1,0:T(8,128)(2,1)S(1)}, u32[]{:S(2)}, u32[]{:S(2)}) collective-permute-start(bf16[2,512,256]{2,1,0:T(8,128)(2,1)S(1)} %pad_maximum_fusion.1), channel_id=1, source_target_pairs={{0,64},{64,0},{1,65},{65,1},{2,66},{66,2},{3,67},{67,3},{4,68},{68... | collective-permute-start | bytes 1572872 | tf_op jit(solution)/shard_map/ppermute | solution.py:329
  86.7 9.0 %collective-permute-start.17 = (bf16[128,1536]{1,0:T(8,128)(2,1)S(1)}, bf16[128,1536]{1,0:T(8,128)(2,1)S(1)}, u32[]{:S(2)}, u32[]{:S(2)}) collective-permute-start(bf16[128,1536]{1,0:T(8,128)(2,1)S(1)} %get-tuple-element.98), channel_id=1, source_target_pairs={{0,1},{1,0},{2,3},{3,2},{4,5},{5,4},{6,7},{7,6},{8,9},{9,8},{10,11... | collective-permute-start | bytes 1179656 | tf_op jit(solution)/shard_map/ppermute | solution.py:324
  90.4 5.2 %collective-permute-start.16 = (bf16[128,1024]{1,0:T(8,128)(2,1)S(1)}, bf16[128,1024]{1,0:T(8,128)(2,1)S(1)}, u32[]{:S(2)}, u32[]{:S(2)}) collective-permute-start(bf16[128,1024]{1,0:T(8,128)(2,1)S(1)} %get-tuple-element.103), channel_id=1, source_target_pairs={{0,1},{1,0},{2,3},{3,2},{4,5},{5,4},{6,7},{7,6},{8,9},{9,8},{10,11... | collective-permute-start | bytes 786440 | tf_op jit(solution)/shard_map/ppermute | solution.py:324
  95.7 7.5 %copy-start.6 = (bf16[128,1024]{1,0:T(8,128)(2,1)}, bf16[128,1024]{1,0:T(8,128)(2,1)S(1)}, u32[]{:S(2)}) copy-start(bf16[128,1024]{1,0:T(8,128)(2,1)S(1)} %collective-permute-done.16.refs_1_) | copy-start | bytes 786436
  95.7 7.5 %copy-start.5 = (bf16[128,1536]{1,0:T(8,128)(2,1)}, bf16[128,1536]{1,0:T(8,128)(2,1)S(1)}, u32[]{:S(2)}) copy-start(bf16[128,1536]{1,0:T(8,128)(2,1)S(1)} %collective-permute-done.17.refs_3_) | copy-start | bytes 1179652
  95.7 10.5 %collective-permute-start.21 = (bf16[2,512,256]{2,1,0:T(8,128)(2,1)S(1)}, bf16[2,512,256]{2,1,0:T(8,128)(2,1)S(1)}, u32[]{:S(2)}, u32[]{:S(2)}) collective-permute-start(bf16[2,512,256]{2,1,0:T(8,128)(2,1)S(1)} %add_convert_fusion.1.refs_0_), channel_id=1, source_target_pairs={{0,1},{1,0},{2,3},{3,2},{4,5},{5,4},{6,7},{7,6},{8,9},{9,8},{10,11... | collective-permute-start | bytes 1572872 | tf_op jit(solution)/shard_map/ppermute | solution.py:324
  99.4 14.7 %collective-permute-start.18 = (bf16[2,512,256]{2,1,0:T(8,128)(2,1)S(1)}, bf16[2,512,256]{2,1,0:T(8,128)(2,1)S(1)}, u32[]{:S(2)}, u32[]{:S(2)}) collective-permute-start(bf16[2,512,256]{2,1,0:T(8,128)(2,1)S(1)} %add_convert_fusion.1.refs_0_), channel_id=1, source_target_pairs={{0,2},{2,4},{4,6},{6,0},{1,3},{3,5},{5,7},{7,1},{8,10},{10,12},{12... | collective-permute-start | bytes 1572872 | tf_op jit(solution)/shard_map/ppermute | solution.py:329
  99.4 14.7 %collective-permute-start.19 = (bf16[2,512,256]{2,1,0:T(8,128)(2,1)S(1)}, bf16[2,512,256]{2,1,0:T(8,128)(2,1)S(1)}, u32[]{:S(2)}, u32[]{:S(2)}) collective-permute-start(bf16[2,512,256]{2,1,0:T(8,128)(2,1)S(1)} %add_convert_fusion.1.refs_0_), channel_id=1, source_target_pairs={{0,6},{2,0},{4,2},{6,4},{1,7},{3,1},{5,3},{7,5},{8,14},{10,8},{12,... | collective-permute-start | bytes 1572872 | tf_op jit(solution)/shard_map/ppermute | solution.py:329
  102.1 4.1 %collective-permute-start.20 = (bf16[4,16,640]{2,1,0:T(8,128)(2,1)S(1)}, bf16[4,16,640]{2,1,0:T(8,128)(2,1)S(1)}, u32[]{:S(2)}, u32[]{:S(2)}) collective-permute-start(bf16[4,16,640]{2,1,0:T(8,128)(2,1)S(1)} %slice_bitcast_fusion.7), channel_id=1, source_target_pairs={{0,8},{8,0},{1,9},{9,1},{2,10},{10,2},{3,11},{11,3},{4,12},{12,4},... | collective-permute-start | bytes 245768 | tf_op jit(solution)/shard_map/ppermute | solution.py:329
  114.1 3.8 %collective-permute-start.27 = (bf16[2,512,256]{2,1,0:T(8,128)(2,1)S(1)}, bf16[2,512,256]{2,1,0:T(8,128)(2,1)S(1)}, u32[]{:S(2)}, u32[]{:S(2)}) collective-permute-start(bf16[2,512,256]{2,1,0:T(8,128)(2,1)S(1)} %collective-permute-done.18.refs_0_), channel_id=1, source_target_pairs={{0,1},{1,0},{2,3},{3,2},{4,5},{5,4},{6,7},{7,6},{8,9},{9,8},{10,11... | collective-permute-start | bytes 1572872 | tf_op jit(solution)/shard_map/ppermute | solution.py:324
  115.0 5.5 %collective-permute-start.28 = (bf16[2,512,256]{2,1,0:T(8,128)(2,1)S(1)}, bf16[2,512,256]{2,1,0:T(8,128)(2,1)S(1)}, u32[]{:S(2)}, u32[]{:S(2)}) collective-permute-start(bf16[2,512,256]{2,1,0:T(8,128)(2,1)S(1)} %collective-permute-done.19.refs_1_), channel_id=1, source_target_pairs={{0,1},{1,0},{2,3},{3,2},{4,5},{5,4},{6,7},{7,6},{8,9},{9,8},{10,11... | collective-permute-start | bytes 1572872 | tf_op jit(solution)/shard_map/ppermute | solution.py:324
  115.0 10.4 %collective-permute-start.22 = (bf16[2,256,256]{2,1,0:T(8,128)(2,1)S(1)}, bf16[2,256,256]{2,1,0:T(8,128)(2,1)S(1)}, u32[]{:S(2)}, u32[]{:S(2)}) collective-permute-start(bf16[2,256,256]{2,1,0:T(8,128)(2,1)S(1)} %slice.69), channel_id=1, source_target_pairs={{0,2},{2,4},{4,6},{6,0},{1,3},{3,5},{5,7},{7,1},{8,10},{10,12},{12... | collective-permute-start | bytes 786440 | tf_op jit(solution)/shard_map/ppermute | solution.py:329
  115.1 10.3 %collective-permute-start.23 = (bf16[2,256,256]{2,1,0:T(8,128)(2,1)S(1)}, bf16[2,256,256]{2,1,0:T(8,128)(2,1)S(1)}, u32[]{:S(2)}, u32[]{:S(2)}) collective-permute-start(bf16[2,256,256]{2,1,0:T(8,128)(2,1)S(1)} %slice.70), channel_id=1, source_target_pairs={{0,6},{2,0},{4,2},{6,4},{1,7},{3,1},{5,3},{7,5},{8,14},{10,8},{12,... | collective-permute-start | bytes 786440 | tf_op jit(solution)/shard_map/ppermute | solution.py:329
  117.9 6.3 %collective-permute-start.24 = (bf16[16,640]{1,0:T(8,128)(2,1)S(1)}, bf16[16,640]{1,0:T(8,128)(2,1)S(1)}, u32[]{:S(2)}, u32[]{:S(2)}) collective-permute-start(bf16[16,640]{1,0:T(8,128)(2,1)S(1)} %get-tuple-element.108), channel_id=1, source_target_pairs={{0,2},{2,4},{4,6},{6,0},{1,3},{3,5},{5,7},{7,1},{8,10},{10,12},{12... | collective-permute-start | bytes 61448 | tf_op jit(solution)/shard_map/ppermute | solution.py:329
  118.0 7.5 %collective-permute-start.25 = (bf16[16,640]{1,0:T(8,128)(2,1)S(1)}, bf16[16,640]{1,0:T(8,128)(2,1)S(1)}, u32[]{:S(2)}, u32[]{:S(2)}) collective-permute-start(bf16[16,640]{1,0:T(8,128)(2,1)S(1)} %get-tuple-element.107), channel_id=1, source_target_pairs={{0,4},{2,6},{4,0},{6,2},{1,5},{3,7},{5,1},{7,3},{8,12},{10,14},{12... | collective-permute-start | bytes 61448 | tf_op jit(solution)/shard_map/ppermute | solution.py:329
  120.5 4.9 %collective-permute-start.26 = (bf16[16,640]{1,0:T(8,128)(2,1)S(1)}, bf16[16,640]{1,0:T(8,128)(2,1)S(1)}, u32[]{:S(2)}, u32[]{:S(2)}) collective-permute-start(bf16[16,640]{1,0:T(8,128)(2,1)S(1)} %get-tuple-element.106), channel_id=1, source_target_pairs={{0,6},{2,0},{4,2},{6,4},{1,7},{3,1},{5,3},{7,5},{8,14},{10,8},{12,... | collective-permute-start | bytes 61448 | tf_op jit(solution)/shard_map/ppermute | solution.py:329
  125.5 2.9 %collective-permute-start.29 = (bf16[2,256,256]{2,1,0:T(8,128)(2,1)S(1)}, bf16[2,256,256]{2,1,0:T(8,128)(2,1)S(1)}, u32[]{:S(2)}, u32[]{:S(2)}) collective-permute-start(bf16[2,256,256]{2,1,0:T(8,128)(2,1)S(1)} %collective-permute-done.22.refs_0_), channel_id=1, source_target_pairs={{0,1},{1,0},{2,3},{3,2},{4,5},{5,4},{6,7},{7,6},{8,9},{9,8},{10,11... | collective-permute-start | bytes 786440 | tf_op jit(solution)/shard_map/ppermute | solution.py:324
  127.2 1.5 %collective-permute-start.30 = (bf16[2,256,256]{2,1,0:T(8,128)(2,1)S(1)}, bf16[2,256,256]{2,1,0:T(8,128)(2,1)S(1)}, u32[]{:S(2)}, u32[]{:S(2)}) collective-permute-start(bf16[2,256,256]{2,1,0:T(8,128)(2,1)S(1)} %collective-permute-done.23.refs_1_), channel_id=1, source_target_pairs={{0,1},{1,0},{2,3},{3,2},{4,5},{5,4},{6,7},{7,6},{8,9},{9,8},{10,11... | collective-permute-start | bytes 786440 | tf_op jit(solution)/shard_map/ppermute | solution.py:324

commit v4 on v3

v4 whole, which is shorter than its diff:
```python
import jax
import jax.numpy as jnp
from jax import lax
from jax.experimental import pallas as pl
from jax.experimental.pallas import tpu as pltpu
from jax.sharding import Mesh
from jax.sharding import PartitionSpec as P

NOPE = 128
ROPE = 64
LATENT = 512
VHEAD = 128
BLOCK = 128
QUERY = NOPE + ROPE
KEY = LATENT + ROPE
KEY_PAD = 640
HALF = LATENT // 2
DOC_MOST = 6
WINDOW = DOC_MOST * BLOCK
PAIR = 2
SCALE = QUERY ** -0.5
MIB = 1024 * 1024

bf16 = jnp.bfloat16
f32 = jnp.float32
NT = ((1,), (1,))
TN = ((0,), (0,))
HEAD_AXES = ("z", "y")


def mul(a, b, dims=((1,), (0,))):
    return lax.dot_general(a, b, (dims, ((), ())), preferred_element_type=f32)


def at_block(block):
    return pl.ds(pl.multiple_of(block * BLOCK, BLOCK), BLOCK)


def attention_kernel(
    place, docs, query_ref, own_ref, other_ref, key_ref, value_ref, grad_ref,
    back_ref, kv_ref, keep_ref, send_ref,
    keys, flipped, total, query_lat, context_grad, contexts, lat_grads,
):
    core, x_here, z_here, y_here = place[0], place[1], place[2], place[3]
    n_x = own_ref.shape[0]
    blocks = 2 * n_x
    pair = range(PAIR)
    doc_first = [
        sum([(docs[0, earlier] < docs[0, block]).astype(jnp.int32) for earlier in range(block)], 0)
        for block in range(blocks)
    ]
    for s in range(n_x):
        x = lax.rem(x_here + n_x - s, n_x)
        keys[at_block(2 * x + core), :] = own_ref[s]
        keys[at_block(2 * x + 1 - core), :] = other_ref[s]
    flipped[:LATENT, :] = jnp.transpose(keys[:, :LATENT])
    flipped[LATENT:, :] = jnp.transpose(keys[:, LATENT:])
    total[...] = jnp.zeros_like(total)

    slot = lambda block: (block % 2) * n_x + block // 2
    lanes = lambda block: slice(block * BLOCK, (block + 1) * BLOCK)
    columns = lambda block, e: slice((PAIR * block + e) * BLOCK, (PAIR * block + e + 1) * BLOCK)
    both = lambda block: slice(PAIR * block * BLOCK, PAIR * (block + 1) * BLOCK)
    nope = [query_ref[:, e * QUERY:e * QUERY + NOPE] for e in pair]
    grads = [
        jnp.concatenate(
            [grad_ref[slot(block), :, e * VHEAD:(e + 1) * VHEAD] for block in range(blocks)], axis=0
        )
        for e in pair
    ]
    for e in pair:
        spread_query = mul(key_ref[e], nope[e], NT).astype(bf16)
        spread_grad = mul(value_ref[e], grads[e], NT).astype(bf16)
        for block in range(blocks):
            query_lat[:, columns(block, e)] = spread_query[:, lanes(block)]
            context_grad[:, columns(block, e)] = spread_grad[:, lanes(block)]

    def window_of(block):
        return slice(max(block + 1 - DOC_MOST, 0) * BLOCK, (block + 1) * BLOCK)

    def turned_of(block):
        return jnp.concatenate(
            [query_ref[lanes(block), e * QUERY + NOPE:(e + 1) * QUERY] for e in pair], axis=0
        )

    def scores_of(block):
        window = window_of(block)
        shape = (window.stop - window.start, BLOCK)
        key_at = window.start + lax.broadcasted_iota(jnp.int32, shape, 0)
        query_at = block * BLOCK + lax.broadcasted_iota(jnp.int32, shape, 1)
        seen = (key_at >= doc_first[block] * BLOCK) & (key_at <= query_at)
        hidden = jnp.concatenate([jnp.where(seen, f32(0.0), f32(-1e30))] * PAIR, axis=1)
        near = mul(keys[window, :LATENT], query_lat[:, both(block)])
        return (near + mul(keys[window, LATENT:], turned_of(block), NT)) * SCALE + hidden

    def softmax_of(scores):
        top = jnp.max(scores, axis=0, keepdims=True)
        expo = jnp.exp(scores - top)
        return expo, 1.0 / jnp.sum(expo, axis=0, keepdims=True)

    def context_of(block, expo, inverse):
        context = (mul(flipped[:LATENT, window_of(block)], expo.astype(bf16)) * inverse).astype(bf16)
        delta = jnp.sum(
            context.astype(f32) * context_grad[:, both(block)].astype(f32), axis=0, keepdims=True
        )
        return context, delta

    def score_grad_of(block, expo, inverse, delta):
        probs = expo * inverse
        grad = mul(keys[window_of(block), :LATENT], context_grad[:, both(block)]) - delta
        return (probs * grad * SCALE).astype(bf16), probs.astype(bf16)

    def lat_grad_of(block, score_grad, low):
        window = window_of(block)
        lat_grad = mul(flipped[:, window], score_grad)
        total[window, :LATENT] += mul(score_grad, query_lat[:, both(block)], NT) + mul(
            low, context_grad[:, both(block)], NT
        )
        total[window, LATENT:] += mul(score_grad, turned_of(block))
        return lat_grad[:LATENT, :].astype(bf16), lat_grad[LATENT:, :]

    def finish(block, context, lat_grad, turned_grad):
        pieces = []
        for e in pair:
            at = slice(e * BLOCK, (e + 1) * BLOCK)
            contexts[e, :, lanes(block)] = context[:, at]
            lat_grads[e, :, lanes(block)] = lat_grad[:, at]
            back_ref[slot(block), :, e * VHEAD:(e + 1) * VHEAD] = mul(
                context[:, at], value_ref[e], TN
            ).astype(bf16)
            pieces.append(mul(lat_grad[:, at], key_ref[e], TN))
            pieces.append(jnp.transpose(turned_grad[:, at]))
        back_ref[slot(block), :, PAIR * VHEAD:] = jnp.concatenate(pieces, axis=1).astype(bf16)

    for low_block in range(blocks // 2):
        duo = (blocks - 1 - low_block, low_block)
        scores = [scores_of(block) for block in duo]
        soft = [softmax_of(score) for score in scores]
        done = [context_of(block, *soft[n]) for n, block in enumerate(duo)]
        score_grads = [
            score_grad_of(block, *soft[n], done[n][1]) for n, block in enumerate(duo)
        ]
        last = [lat_grad_of(block, *score_grads[n]) for n, block in enumerate(duo)]
        for n, block in enumerate(duo):
            finish(block, done[n][0], *last[n])

    for e in pair:
        kv_ref[e, :, :NOPE] = mul(lat_grads[e], nope[e]).astype(bf16)
        kv_ref[e, :, NOPE:] = mul(contexts[e], grads[e]).astype(bf16)

    n_z, n_y, _, rows = keep_ref.shape[:4]
    empty = jnp.zeros((rows, KEY_PAD - KEY), bf16)
    for dz in range(n_z):
        for dy in range(n_y):
            head = lax.rem(z_here + dz, n_z) * n_y + lax.rem(y_here + dy, n_y)
            for dx in range(n_x):
                x = lax.rem(x_here + dx, n_x)
                for ref, parity in ((keep_ref, core), (send_ref, 1 - core)):
                    start = pl.multiple_of((2 * x + parity) * BLOCK + head * rows, rows)
                    ref[dz, dy, dx, :, :KEY] = total[pl.ds(start, rows), :].astype(bf16)
                    ref[dz, dy, dx, :, KEY:] = empty


def attention(place, docs, queries, own, other, key_up, value_up, grads, n_z, n_y):
    n_x = own.shape[0]
    tokens = 2 * n_x * BLOCK
    whole = lambda shape: pl.BlockSpec(shape, lambda i, place, docs: (0,) * len(shape))
    weights = pl.BlockSpec((PAIR, LATENT, NOPE), lambda i, place, docs: (place[0] * n_x + place[1], 0, 0))
    rows_shape = (n_z, n_y, n_x, BLOCK // (n_z * n_y), KEY_PAD)
    out_shapes = [
        (2 * n_x, BLOCK, PAIR * (VHEAD + QUERY)),
        (PAIR, LATENT, NOPE + VHEAD),
        rows_shape,
        rows_shape,
    ]
    return pl.pallas_call(
        attention_kernel,
        grid_spec=pltpu.PrefetchScalarGridSpec(
            num_scalar_prefetch=2,
            grid=(1,),
            in_specs=[
                whole(queries.shape),
                whole(own.shape),
                whole(other.shape),
                weights,
                weights,
                whole(grads.shape),
            ],
            out_specs=[whole(shape) for shape in out_shapes],
            scratch_shapes=[
                pltpu.VMEM((tokens, KEY), bf16),
                pltpu.VMEM((KEY, tokens), bf16),
                pltpu.VMEM((tokens, KEY), f32),
                pltpu.VMEM((LATENT, PAIR * tokens), bf16),
                pltpu.VMEM((LATENT, PAIR * tokens), bf16),
                pltpu.VMEM((PAIR, LATENT, tokens), bf16),
                pltpu.VMEM((PAIR, LATENT, tokens), bf16),
            ],
        ),
        out_shape=[jax.ShapeDtypeStruct(shape, bf16) for shape in out_shapes],
        name="attention",
        compiler_params=pltpu.CompilerParams(
            dimension_semantics=("arbitrary",), vmem_limit_bytes=48 * MIB
        ),
        cost_estimate=pl.CostEstimate(
            flops=9_000_000_000, bytes_accessed=15_000_000, transcendentals=1_600_000
        ),
    )(place, docs, queries, own, other, key_up, value_up, grads)


def join(back):
    slots, rows, width = back.shape
    value = PAIR * VHEAD

    def kernel(back_ref, attended_ref, query_grad_ref):
        for n in range(slots):
            attended_ref[:, n * value:(n + 1) * value] = back_ref[n, :, :value]
            at = slice(n * (width - value), (n + 1) * (width - value))
            query_grad_ref[:, at] = back_ref[n, :, value:]

    return pl.pallas_call(
        kernel,
        out_shape=[
            jax.ShapeDtypeStruct((rows, slots * value), bf16),
            jax.ShapeDtypeStruct((rows, slots * (width - value)), bf16),
        ],
        name="join",
    )(back)


def unfold(place, heads, pieces, begun):
    shape = jax.ShapeDtypeStruct((heads, LATENT, NOPE), f32)
    parts = [part for _, *parts in pieces for part in parts]
    operands = parts + [swapped(part) for part in parts]
    sides = parts[0].shape[0]
    n_x = heads // (2 * sides)
    count = 2 * len(pieces) * sides

    def kernel(place, *refs):
        sources = list(refs[:len(operands)])
        key_out, value_out, keys, values, sems = refs[-5:]
        started = []
        for n in range(2 * len(pieces)):
            x_away, *part = pieces[n % len(pieces)]
            core = place[0] if n < len(pieces) else 1 - place[0]
            x = lax.rem(place[1] + x_away, n_x)
            part = [sources.pop(0) for _ in part]
            for side in range(sides):
                slot = n * sides + side
                start = 0
                for ref in part:
                    rows = slice(start, start + ref.shape[1])
                    keys[slot, rows, :] = ref[side, :, :NOPE].astype(f32)
                    values[slot, rows, :] = ref[side, :, NOPE:].astype(f32)
                    start += ref.shape[1]
                head = core * (heads // 2) + x * sides + side
                for which, (done, out) in enumerate(((keys, key_out), (values, value_out))):
                    copy = pltpu.make_async_copy(done.at[slot], out.at[head], sems.at[which, slot])
                    copy.start()
                    started.append(copy)
        for copy in started:
            copy.wait()

    first = 1 + len(operands)
    return pl.pallas_call(
        kernel,
        grid_spec=pltpu.PrefetchScalarGridSpec(
            num_scalar_prefetch=1,
            grid=(1,),
            in_specs=[pl.BlockSpec(part.shape, lambda i, place: (0, 0, 0)) for part in operands]
            + [pl.BlockSpec(memory_space=pl.ANY)] * len(begun),
            out_specs=[pl.BlockSpec(memory_space=pl.ANY)] * 2,
            scratch_shapes=[pltpu.VMEM((count, LATENT, NOPE), f32)] * 2
            + [pltpu.SemaphoreType.DMA((2, count))],
        ),
        out_shape=[shape, shape],
        input_output_aliases={first: 0, first + 1: 1} if begun else {},
        name="unfold",
        compiler_params=pltpu.CompilerParams(vmem_limit_bytes=24 * MIB),
        cost_estimate=pl.CostEstimate(flops=0, bytes_accessed=4_000_000, transcendentals=0),
    )(place, *operands, *begun)


def pack(queries, n_head, n_x):
    rows, lanes = queries.shape
    lanes //= 2 * n_head * n_x

    def kernel(query_ref, out_ref):
        for head in range(n_head):
            for core in range(2):
                for x in range(n_x):
                    at = ((head * 2 + core) * n_x + x) * lanes
                    out_ref[(x * 2 + core) * n_head + head] = query_ref[:, at:at + lanes]

    return pl.pallas_call(
        kernel,
        out_shape=jax.ShapeDtypeStruct((2 * n_head * n_x, rows, lanes), bf16),
        name="pack",
    )(queries)


def swapped(value):
    return lax.ppermute(value, "core", [(0, 1), (1, 0)])


def shifted(value, axis, steps):
    count = lax.axis_size(axis)
    return lax.ppermute(value, axis, [(i, (i + steps) % count) for i in range(count)])


def exchanged(value, axes):
    return lax.all_to_all(value, axes, 0, 0, tiled=True)


def copies(value, count):
    return jnp.broadcast_to(value[None], (count,) + value.shape)


def added(*terms):
    return sum(term.astype(f32) for term in terms)


def folded(rows, axis):
    count = rows.shape[0]
    return added(rows[0], *[shifted(rows[s], axis, s) for s in range(1, count)])


def on_device(queries, latent, key_up, value_up, out_grad, block_docs):
    n_head = lax.axis_size(HEAD_AXES)
    n_x = lax.axis_size("x")
    core = lax.axis_index("core")
    x_here = lax.axis_index("x")
    n_z, n_y = [lax.axis_size(axis) for axis in HEAD_AXES]
    place = jnp.stack(
        [core, x_here] + [lax.axis_index(axis) for axis in HEAD_AXES]
    ).astype(jnp.int32)

    heads = key_up.shape[0]
    fine_axes = ("core", "x")
    grads = jnp.swapaxes(out_grad.reshape(BLOCK, 2 * n_x, -1), 0, 1)
    arrived = pack(queries, n_head, n_x)
    own = exchanged(copies(latent, n_head), HEAD_AXES)
    own, arrived = lax.optimization_barrier((own, arrived))
    arrived = exchanged(arrived, ("x", "core") + HEAD_AXES).reshape(2 * n_x * BLOCK, -1)
    own = own.reshape(BLOCK, KEY)
    own = jnp.stack([own] + [shifted(own, "x", s) for s in range(1, n_x)])
    other = swapped(own)
    grads = exchanged(grads, fine_axes)

    back, kv, rows_keep, rows_send = attention(
        place, block_docs, arrived, own, other, key_up, value_up, grads, n_z, n_y
    )
    after = lax.optimization_barrier
    rows = added(rows_keep, swapped(rows_send)).astype(bf16)
    back = exchanged(back, fine_axes)
    kv = added(kv, shifted(kv, "dp", 1)).astype(bf16)
    rows = folded(rows, HEAD_AXES[0]).astype(bf16)
    kv, back = after((kv, back))
    upper, lower = kv[:, :HALF], kv[:, HALF:]
    before = [shifted(upper, "x", 1), shifted(lower, "x", 1)]
    behind = [shifted(lower, "x", -1), shifted(upper, "x", -1)]
    rows = folded(rows, HEAD_AXES[1]).astype(bf16)
    grads = unfold(place, heads, [(0, kv)], [])
    attended, query_grad = join(back)
    before[0], behind[0], rows, grads, attended, query_grad = after(
        (before[0], behind[0], rows, grads, attended, query_grad)
    )
    far = shifted(before[0], "x", 1), shifted(behind[0], "x", -1)
    rows = [rows[0]] + [shifted(rows[s], "x", s) for s in range(1, n_x)]
    grads = unfold(place, heads, [(n_x - 1, *before), (1, *behind[::-1])], grads)
    far, rows, grads, attended, query_grad = after((far, rows, grads, attended, query_grad))
    grads = unfold(place, heads, [(2,) + tuple(far)], grads)
    latent_grad = added(*rows)[:, :KEY]
    key_up_grad, value_up_grad = grads
    return (attended, query_grad, latent_grad, key_up_grad, value_up_grad)


def solution(mesh):
    n_dp, n_head, n_blk = mesh.devices.shape
    fine = Mesh(
        mesh.devices.reshape(n_dp, n_head // 2, 2, n_blk // 2, 2), ("dp", "z", "y", "x", "core")
    )
    head, blk = HEAD_AXES, ("x", "core")
    return jax.shard_map(
        on_device,
        mesh=fine,
        in_specs=(
            P(("dp",) + blk + head, None),
            P(("dp",) + blk + head, None),
            P(head, None, None),
            P(head, None, None),
            P(("dp",) + blk, head),
            P("dp", None),
        ),
        out_specs=(
            P(("dp",) + blk, head),
            P(("dp",) + blk, head),
            P(("dp",) + blk + head, None),
            P(head, None, None),
            P(head, None, None),
        ),
        check_vma=False,
    )
```

time: 131 us -> 125 us (0.954)
  waiting for transfers between devices: 32.7 us -> 37.7 us
  starting transfers between devices: 53.7 us -> 49.8 us
  Pallas kernels: 32.6 us -> 29.2 us
  other arithmetic: 3.44 us -> 1.23 us
  local copies, waits for them, and re-layouts: 7.38 us -> 5.49 us
    all_to_all x2 -> x4, waiting for transfers between devices: 9.11 us -> 18.5 us  [exchanged(): return lax.all_to_all(value, axes, 0, 0, tiled=True)]
    all_to_all x2 -> x4, starting transfers between devices: 13.2 us -> 22.5 us  [exchanged(): return lax.all_to_all(value, axes, 0, 0, tiled=True)]
    ppermute x10 -> x9, starting transfers between devices: 14.5 us -> 5.92 us  [swapped(): return lax.ppermute(value, 'core', [(0, 1), (1, 0)])]
    ppermute x21 -> x17, waiting for transfers between devices: 22.7 us -> 16.8 us  [shifted(): lax.ppermute(value, axis, [(i, (i + steps) % count) for i in range(count)])]
    ppermute x21 -> x17, starting transfers between devices: 26 us -> 21.4 us  [shifted(): lax.ppermute(value, axis, [(i, (i + steps) % count) for i in range(count)])]
    pallas_call x1, Pallas kernels: 20.9 us -> 18.1 us  [attention(): pl.pallas_call(attention_kernel, grid_spec=pltpu.PrefetchScalarGridSpec(n...]
    reduce_sum x1 -> x0, other arithmetic: 1.92 us -> none  [on_device(): jnp.sum((docs < docs[2 * x_here + side]).astype(jnp.int32))]
    ppermute x10 -> x9, waiting for transfers between devices: 0.83 us -> 2.38 us  [swapped(): return lax.ppermute(value, 'core', [(0, 1), (1, 0)])]
  transfers between devices with their start and end apart: 33 -> 30, of which waited for: 12 -> 13; matrix products, arithmetic and copies ran while one was open for 6% -> 3% of each run, Pallas kernels for 7% -> 7%
where the time goes in v4:
time: 125 us; the launch traced here: 124 us
  starting transfers between devices  49.8 us (40%)
  waiting for transfers between devices  37.7 us (30%)
  Pallas kernels  29.2 us (23%)
  local copies, waits for them, and re-layouts  5.49 us (4%)
    all_to_all x4, starting transfers between devices, exchanged(): return lax.all_to_all(value, axes, 0, 0, tiled=True)  22.5 us
    ppermute x17, starting transfers between devices, shifted(): lax.ppermute(value, axis, [(i, (i + steps) % count) for i in range(count)])  21.4 us
    all_to_all x4, waiting for transfers between devices, exchanged(): return lax.all_to_all(value, axes, 0, 0, tiled=True)  18.5 us
    pallas_call x1, Pallas kernels, attention(): pl.pallas_call(attention_kernel, grid_spec=pltpu.PrefetchScalarGridSpec(n...  18.1 us
    ppermute x17, waiting for transfers between devices, shifted(): lax.ppermute(value, axis, [(i, (i + steps) % count) for i in range(count)])  16.8 us
    pallas_call x3, Pallas kernels, unfold(): pl.pallas_call(kernel, grid_spec=pltpu.PrefetchScalarGridSpec(num_scalar_...  6.57 us
    ppermute x9, starting transfers between devices, swapped(): return lax.ppermute(value, 'core', [(0, 1), (1, 0)])  5.92 us
  transfers between devices with their start and end apart: 30, of which 13 were waited for; matrix products, arithmetic and copies ran while one was open for 3% of the time, Pallas kernels for 7%

profile of v4, /device:TPU:1, one launch (start us, length us, event | category | flops | bytes accessed | tf_op | source)
XLA Modules:
  0.0 124.5 jit_solution(7656879713674525671)
XLA Ops:
  0.6 1.4 %broadcast_in_dim.2 = bf16[8,16,576]{2,1,0:T(8,128)(2,1)} broadcast(bf16[16,576]{1,0:T(8,128)(2,1)} %param.7), dimensions={1,2} | broadcast | bytes 165888 | tf_op jit(solution)/shard_map/broadcast_in_dim | solution.py:316
  2.0 6.9 %all-to-all-start = ((bf16[8,16,576]{2,1,0:T(8,128)(2,1)}), bf16[8,16,576]{2,1,0:T(8,128)(2,1)S(1)}, u32[]{:S(2)}, u32[]{:S(2)}) async-start(bf16[8,16,576]{2,1,0:T(8,128)(2,1)} %broadcast_in_dim.2), calls=%async_computation | async-start | bytes 327680 | tf_op jit(solution)/shard_map/all_to_all | solution.py:312
  8.9 1.3 %copy.18 = bf16[128,2048]{0,1:T(8,128)(2,1)S(1)} copy(bf16[128,2048]{1,0:T(8,128)(2,1)} %param.10) | data formatting | bytes 1048576 | tf_op args[4]
  10.2 1.0 copy.19
  11.2 3.4 %all-to-all-done = bf16[8,16,576]{2,1,0:T(8,128)(2,1)S(1)} async-done(((bf16[8,16,576]{2,1,0:T(8,128)(2,1)}), bf16[8,16,576]{2,1,0:T(8,128)(2,1)S(1)}, u32[]{:S(2)}, u32[]{:S(2)}) %all-to-all-start) | async-done | bytes 147488 | tf_op jit(solution)/shard_map/all_to_all | solution.py:312
  14.6 6.4 %all-to-all-start.2 = ((bf16[8,128,256]{2,1,0:T(8,128)(2,1)}), bf16[8,128,256]{2,1,0:T(8,128)(2,1)S(1)}, u32[]{:S(2)}, u32[]{:S(2)}) async-start(bf16[8,128,256]{2,1,0:T(8,128)(2,1)} %bitcast.11), calls=%async_computation.2 | async-start | bytes 1048576 | tf_op jit(solution)/shard_map/all_to_all | solution.py:312
  21.0 2.1 %pack.1 = bf16[64,16,384]{2,1,0:T(8,128)(2,1)} custom-call(bf16[16,24576]{1,0:T(8,128)(2,1)} %query_ref.1), custom_call_target="tpu_custom_call" | custom-call | tf_op jit(solution)/shard_map/pack/pallas_call | solution.py:295
  23.1 1.4 %collective-permute-start = (bf16[128,576]{1,0:T(8,128)(2,1)S(1)}, bf16[128,576]{1,0:T(8,128)(2,1)S(1)}, u32[]{:S(2)}, u32[]{:S(2)}) collective-permute-start(bf16[128,576]{1,0:T(8,128)(2,1)S(1)} %bitcast.40), channel_id=1, source_target_pairs={{0,2},{2,4},{4,6},{6,0},{1,3},{3,5},{5,7},{7,1},{8,10},{10,12},{12... | collective-permute-start | bytes 442376 | tf_op jit(solution)/shard_map/ppermute | solution.py:308
  24.5 2.4 %collective-permute-start.1 = (bf16[128,576]{1,0:T(8,128)(2,1)S(1)}, bf16[128,576]{1,0:T(8,128)(2,1)S(1)}, u32[]{:S(2)}, u32[]{:S(2)}) collective-permute-start(bf16[128,576]{1,0:T(8,128)(2,1)S(1)} %bitcast.41), channel_id=1, source_target_pairs={{0,4},{2,6},{4,0},{6,2},{1,5},{3,7},{5,1},{7,3},{8,12},{10,14},{12... | collective-permute-start | bytes 442376 | tf_op jit(solution)/shard_map/ppermute | solution.py:308
  26.9 1.2 collective-permute-start.2
  28.0 2.7 %all-to-all-done.2.grad_ref = bf16[8,128,256]{2,1,0:T(8,128)(2,1)S(1)} async-done(((bf16[8,128,256]{2,1,0:T(8,128)(2,1)}), bf16[8,128,256]{2,1,0:T(8,128)(2,1)S(1)}, u32[]{:S(2)}, u32[]{:S(2)}) %all-to-all-start.2) | async-done | bytes 524320 | tf_op jit(solution)/shard_map/all_to_all | solution.py:312
  30.7 5.0 %all-to-all-start.1 = ((bf16[64,16,384]{2,1,0:T(8,128)(2,1)}), bf16[64,16,384]{2,1,0:T(8,128)(2,1)S(1)}, u32[]{:S(2)}, u32[]{:S(2)}) async-start(bf16[64,16,384]{2,1,0:T(8,128)(2,1)} %pack.1), calls=%async_computation.1 | async-start | bytes 1572864 | tf_op jit(solution)/shard_map/all_to_all | solution.py:312
  35.7 1.8 %collective-permute-done.1 = bf16[128,576]{1,0:T(8,128)(2,1)S(1)} collective-permute-done((bf16[128,576]{1,0:T(8,128)(2,1)S(1)}, bf16[128,576]{1,0:T(8,128)(2,1)S(1)}, u32[]{:S(2)}, u32[]{:S(2)}) %collective-permute-start.1) | collective-permute-done | bytes 147488 | tf_op jit(solution)/shard_map/ppermute | solution.py:308
  37.7 0.3 copy.17
  38.0 1.1 collective-permute-start.3
  39.2 1.6 %collective-permute-done.3 = bf16[4,128,576]{1,2,0:T(8,128)(2,1)S(1)} collective-permute-done((bf16[4,128,576]{1,2,0:T(8,128)(2,1)S(1)}, bf16[4,128,576]{1,2,0:T(8,128)(2,1)S(1)}, u32[]{:S(2)}, u32[]{:S(2)}) %collective-permute-start.3) | collective-permute-done | bytes 589856 | tf_op jit(solution)/shard_map/ppermute | solution.py:303
  41.1 9.8 %all-to-all-done.1 = bf16[64,16,384]{2,1,0:T(8,128)(2,1)S(1)} async-done(((bf16[64,16,384]{2,1,0:T(8,128)(2,1)}), bf16[64,16,384]{2,1,0:T(8,128)(2,1)S(1)}, u32[]{:S(2)}, u32[]{:S(2)}) %all-to-all-start.1) | async-done | bytes 786464 | tf_op jit(solution)/shard_map/all_to_all | solution.py:312
  50.8 1.0 copy-done.1
  51.9 18.1 %attention.1 = (bf16[8,128,640]{2,1,0:T(8,128)(2,1)}, bf16[2,512,256]{2,1,0:T(8,128)(2,1)S(1)}, bf16[4,2,4,16,640]{4,3,2,1,0:T(8,128)(2,1)S(1)}, bf16[4,2,4,16,640]{4,3,2,1,0:T(8,128)(2,1)}) custom-call(s32[4]{0:T(128)S(1)} %pad_add_fusion.place, s32[1,8]{1,0:T(1,128)S(1)} %copy-done.2, bf16[1024,384]{1,0:T(8,128)(2,1)S(1)} %bitcast.38, ...), custom_call_target="tpu_custom_call" | custom-call | flops 8999999488 | bytes 15000000 | tf_op jit(solution)/shard_map/attention/pallas_call | solution.py:176
  70.0 0.4 collective-permute-start.7
  70.4 4.3 %all-to-all-start.3 = ((bf16[8,128,640]{2,1,0:T(8,128)(2,1)}), bf16[8,128,640]{2,1,0:T(8,128)(2,1)}, u32[]{:S(2)}, u32[]{:S(2)}) async-start(bf16[8,128,640]{2,1,0:T(8,128)(2,1)} %get-tuple-element.41), calls=%async_computation.3 | async-start | bytes 2621440 | tf_op jit(solution)/shard_map/all_to_all | solution.py:312
  74.6 2.7 %collective-permute-start.4 = (bf16[2,512,256]{2,1,0:T(8,128)(2,1)S(1)}, bf16[2,512,256]{2,1,0:T(8,128)(2,1)S(1)}, u32[]{:S(2)}, u32[]{:S(2)}) collective-permute-start(bf16[2,512,256]{2,1,0:T(8,128)(2,1)S(1)} %get-tuple-element.40), channel_id=1, source_target_pairs={{0,64},{64,0},{1,65},{65,1},{2,66},{66,2},{3,67},{67,3},{4,68},{68... | collective-permute-start | bytes 1572872 | tf_op jit(solution)/shard_map/ppermute | solution.py:308
  77.5 0.9 collective-permute-start.10
  78.5 0.6 collective-permute-start.8
  79.1 0.8 collective-permute-start.9
  79.8 9.7 %collective-permute-done.4 = bf16[2,512,256]{2,1,0:T(8,128)(2,1)S(1)} collective-permute-done((bf16[2,512,256]{2,1,0:T(8,128)(2,1)S(1)}, bf16[2,512,256]{2,1,0:T(8,128)(2,1)S(1)}, u32[]{:S(2)}, u32[]{:S(2)}) %collective-permute-start.4) | collective-permute-done | bytes 524320 | tf_op jit(solution)/shard_map/ppermute | solution.py:308
  89.8 2.7 %all-to-all-done.3.back_ref = bf16[8,128,640]{2,1,0:T(8,128)(2,1)} async-done(((bf16[8,128,640]{2,1,0:T(8,128)(2,1)}), bf16[8,128,640]{2,1,0:T(8,128)(2,1)}, u32[]{:S(2)}, u32[]{:S(2)}) %all-to-all-start.3) | async-done | bytes 1310752 | tf_op jit(solution)/shard_map/all_to_all | solution.py:312
  92.5 0.4 collective-permute-start.12
  92.9 0.5 collective-permute-start.18
  93.5 2.3 %collective-permute-start.19 = (bf16[2,256,256]{2,1,0:T(8,128)(2,1)S(1)}, bf16[2,256,256]{2,1,0:T(8,128)(2,1)S(1)}, u32[]{:S(2)}, u32[]{:S(2)}) collective-permute-start(bf16[2,256,256]{2,1,0:T(8,128)(2,1)S(1)} %get-tuple-element.75), channel_id=1, source_target_pairs={{0,6},{2,0},{4,2},{6,4},{1,7},{3,1},{5,3},{7,5},{8,14},{10,8},{12,... | collective-permute-start | bytes 786440 | tf_op jit(solution)/shard_map/ppermute | solution.py:308
  95.9 1.0 collective-permute-done.11
  96.8 2.5 %collective-permute-start.6 = (bf16[2,256,256]{2,1,0:T(8,128)(2,1)S(1)}, bf16[2,256,256]{2,1,0:T(8,128)(2,1)S(1)}, u32[]{:S(2)}, u32[]{:S(2)}) collective-permute-start(bf16[2,256,256]{2,1,0:T(8,128)(2,1)S(1)} %get-tuple-element.74), channel_id=1, source_target_pairs={{0,6},{2,0},{4,2},{6,4},{1,7},{3,1},{5,3},{7,5},{8,14},{10,8},{12,... | collective-permute-start | bytes 786440 | tf_op jit(solution)/shard_map/ppermute | solution.py:308
  99.4 2.6 %collective-permute-done.18.refs_1_ = bf16[2,256,256]{2,1,0:T(8,128)(2,1)S(1)} collective-permute-done((bf16[2,256,256]{2,1,0:T(8,128)(2,1)S(1)}, bf16[2,256,256]{2,1,0:T(8,128)(2,1)S(1)}, u32[]{:S(2)}, u32[]{:S(2)}) %collective-permute-start.18) | collective-permute-done | bytes 262176 | tf_op jit(solution)/shard_map/ppermute | solution.py:308
  102.0 1.5 %collective-permute-start.21 = (bf16[2,256,256]{2,1,0:T(8,128)(2,1)S(1)}, bf16[2,256,256]{2,1,0:T(8,128)(2,1)S(1)}, u32[]{:S(2)}, u32[]{:S(2)}) collective-permute-start(bf16[2,256,256]{2,1,0:T(8,128)(2,1)S(1)} %collective-permute-done.18.refs_1_), channel_id=1, source_target_pairs={{0,1},{1,0},{2,3},{3,2},{4,5},{5,4},{6,7},{7,6},{8,9},{9,8},{10,11... | collective-permute-start | bytes 786440 | tf_op jit(solution)/shard_map/ppermute | solution.py:303
  103.5 2.5 %join.1 = (bf16[128,2048]{1,0:T(8,128)(2,1)}, bf16[128,3072]{1,0:T(8,128)(2,1)}) custom-call(bf16[8,128,640]{2,1,0:T(8,128)(2,1)} %all-to-all-done.3.back_ref), custom_call_target="tpu_custom_call" | custom-call | tf_op jit(solution)/shard_map/join/pallas_call | solution.py:221
  106.0 1.9 %unfold.3 = (f32[16,512,128]{2,1,0:T(8,128)}, f32[16,512,128]{2,1,0:T(8,128)}) custom-call(s32[4]{0:T(128)S(1)} %pad_add_fusion.place, bf16[2,512,256]{2,1,0:T(8,128)(2,1)S(1)} %add_convert_fusion.1.refs_0_, bf16[2,512,256]{2,1,0:T(8,128)(2,1)S(1)} %collective-permute-done.12.refs_1_), custom_call_target="tpu_custom_call" | custom-call | bytes 4000000 | tf_op jit(solution)/shard_map/unfold/pallas_call | solution.py:265
  108.0 0.6 collective-permute-start.20
  108.7 2.8 %collective-permute-start.14 = (bf16[2,256,256]{2,1,0:T(8,128)(2,1)S(1)}, bf16[2,256,256]{2,1,0:T(8,128)(2,1)S(1)}, u32[]{:S(2)}, u32[]{:S(2)}) collective-permute-start(bf16[2,256,256]{2,1,0:T(8,128)(2,1)S(1)} %collective-permute-done.6.refs_3_), channel_id=1, source_target_pairs={{0,6},{2,0},{4,2},{6,4},{1,7},{3,1},{5,3},{7,5},{8,14},{10,8},{12,... | collective-permute-start | bytes 786440 | tf_op jit(solution)/shard_map/ppermute | solution.py:308
  111.6 2.6 %collective-permute-start.16 = (bf16[16,640]{1,0:T(8,128)(2,1)S(1)}, bf16[16,640]{1,0:T(8,128)(2,1)S(1)}, u32[]{:S(2)}, u32[]{:S(2)}) collective-permute-start(bf16[16,640]{1,0:T(8,128)(2,1)S(1)} %get-tuple-element.77), channel_id=1, source_target_pairs={{0,4},{2,6},{4,0},{6,2},{1,5},{3,7},{5,1},{7,3},{8,12},{10,14},{12... | collective-permute-start | bytes 61448 | tf_op jit(solution)/shard_map/ppermute | solution.py:308
  114.2 0.6 collective-permute-start.17
  114.8 2.7 %unfold.4 = (f32[16,512,128]{2,1,0:T(8,128)}, f32[16,512,128]{2,1,0:T(8,128)}) custom-call(s32[4]{0:T(128)S(1)} %pad_add_fusion.place, bf16[2,256,256]{2,1,0:T(8,128)(2,1)S(1)} %collective-permute-done.5.refs_0_, bf16[2,256,256]{2,1,0:T(8,128)(2,1)S(1)} %collective-permute-done.18.refs_1_, ...), custom_call_target="tpu_custom_call", output_to_operand_aliasing={{0}: (9, {}), {1}: (10, {})} | custom-call | bytes 4000000 | tf_op jit(solution)/shard_map/unfold/pallas_call | solution.py:265
  117.5 0.4 collective-permute-done.15
  117.9 1.2 collective-permute-done.16
  119.1 1.7 %collective-permute-start.24 = (bf16[2,256,256]{2,1,0:T(8,128)(2,1)S(1)}, bf16[2,256,256]{2,1,0:T(8,128)(2,1)S(1)}, u32[]{:S(2)}, u32[]{:S(2)}) collective-permute-start(bf16[2,256,256]{2,1,0:T(8,128)(2,1)S(1)} %collective-permute-done.13.refs_0_), channel_id=1, source_target_pairs={{0,1},{1,0},{2,3},{3,2},{4,5},{5,4},{6,7},{7,6},{8,9},{9,8},{10,11... | collective-permute-start | bytes 786440 | tf_op jit(solution)/shard_map/ppermute | solution.py:303
  120.9 0.6 convert_add_fusion.2
  121.6 0.4 collective-permute-done.24.refs_2_
  122.0 0.4 collective-permute-done.25.refs_3_
  122.4 1.9 %unfold.5 = (f32[16,512,128]{2,1,0:T(8,128)}, f32[16,512,128]{2,1,0:T(8,128)}) custom-call(s32[4]{0:T(128)S(1)} %pad_add_fusion.place, bf16[2,256,256]{2,1,0:T(8,128)(2,1)S(1)} %collective-permute-done.13.refs_0_, bf16[2,256,256]{2,1,0:T(8,128)(2,1)S(1)} %collective-permute-done.14.refs_1_, ...), custom_call_target="tpu_custom_call", output_to_operand_aliasing={{0}: (5, {}), {1}: (6, {})} | custom-call | bytes 4000000 | tf_op jit(solution)/shard_map/unfold/pallas_call | solution.py:265
  (40 shorter events, 1.4 us)
Async XLA Ops:
  2.0 12.6 %all-to-all-start = ((bf16[8,16,576]{2,1,0:T(8,128)(2,1)}), bf16[8,16,576]{2,1,0:T(8,128)(2,1)S(1)}, u32[]{:S(2)}, u32[]{:S(2)}) async-start(bf16[8,16,576]{2,1,0:T(8,128)(2,1)} %broadcast_in_dim.2), calls=%async_computation | async-start | bytes 327680 | tf_op jit(solution)/shard_map/all_to_all | solution.py:312
  14.6 16.1 %all-to-all-start.2 = ((bf16[8,128,256]{2,1,0:T(8,128)(2,1)}), bf16[8,128,256]{2,1,0:T(8,128)(2,1)S(1)}, u32[]{:S(2)}, u32[]{:S(2)}) async-start(bf16[8,128,256]{2,1,0:T(8,128)(2,1)} %bitcast.11), calls=%async_computation.2 | async-start | bytes 1048576 | tf_op jit(solution)/shard_map/all_to_all | solution.py:312
  23.1 12.6 %collective-permute-start = (bf16[128,576]{1,0:T(8,128)(2,1)S(1)}, bf16[128,576]{1,0:T(8,128)(2,1)S(1)}, u32[]{:S(2)}, u32[]{:S(2)}) collective-permute-start(bf16[128,576]{1,0:T(8,128)(2,1)S(1)} %bitcast.40), channel_id=1, source_target_pairs={{0,2},{2,4},{4,6},{6,0},{1,3},{3,5},{5,7},{7,1},{8,10},{10,12},{12... | collective-permute-start | bytes 442376 | tf_op jit(solution)/shard_map/ppermute | solution.py:308
  24.5 13.1 %collective-permute-start.1 = (bf16[128,576]{1,0:T(8,128)(2,1)S(1)}, bf16[128,576]{1,0:T(8,128)(2,1)S(1)}, u32[]{:S(2)}, u32[]{:S(2)}) collective-permute-start(bf16[128,576]{1,0:T(8,128)(2,1)S(1)} %bitcast.41), channel_id=1, source_target_pairs={{0,4},{2,6},{4,0},{6,2},{1,5},{3,7},{5,1},{7,3},{8,12},{10,14},{12... | collective-permute-start | bytes 442376 | tf_op jit(solution)/shard_map/ppermute | solution.py:308
  26.9 10.7 %collective-permute-start.2 = (bf16[128,576]{1,0:T(8,128)(2,1)S(1)}, bf16[128,576]{1,0:T(8,128)(2,1)S(1)}, u32[]{:S(2)}, u32[]{:S(2)}) collective-permute-start(bf16[128,576]{1,0:T(8,128)(2,1)S(1)} %bitcast.42), channel_id=1, source_target_pairs={{0,6},{2,0},{4,2},{6,4},{1,7},{3,1},{5,3},{7,5},{8,14},{10,8},{12,... | collective-permute-start | bytes 442376 | tf_op jit(solution)/shard_map/ppermute | solution.py:308
  30.7 6.9 %copy-start = (bf16[8,128,256]{2,1,0:T(8,128)(2,1)}, bf16[8,128,256]{2,1,0:T(8,128)(2,1)S(1)}, u32[]{:S(2)}) copy-start(bf16[8,128,256]{2,1,0:T(8,128)(2,1)S(1)} %all-to-all-done.2.grad_ref) | copy-start | bytes 1572868
  30.7 20.1 %all-to-all-start.1 = ((bf16[64,16,384]{2,1,0:T(8,128)(2,1)}), bf16[64,16,384]{2,1,0:T(8,128)(2,1)S(1)}, u32[]{:S(2)}, u32[]{:S(2)}) async-start(bf16[64,16,384]{2,1,0:T(8,128)(2,1)} %pack.1), calls=%async_computation.1 | async-start | bytes 1572864 | tf_op jit(solution)/shard_map/all_to_all | solution.py:312
  35.7 15.1 %copy-start.2 = (s32[1,8]{1,0:T(1,128)S(1)}, s32[1,8]{1,0:T(1,128)}, u32[]{:S(2)}) copy-start(s32[1,8]{1,0:T(1,128)} %docs.1) | copy-start | bytes 100
  38.0 2.8 %collective-permute-start.3 = (bf16[4,128,576]{1,2,0:T(8,128)(2,1)S(1)}, bf16[4,128,576]{1,2,0:T(8,128)(2,1)S(1)}, u32[]{:S(2)}, u32[]{:S(2)}) collective-permute-start(bf16[4,128,576]{1,2,0:T(8,128)(2,1)S(1)} %copy.17), channel_id=1, source_target_pairs={{0,1},{1,0},{2,3},{3,2},{4,5},{5,4},{6,7},{7,6},{8,9},{9,8},{10,11... | collective-permute-start | bytes 1769480 | tf_op jit(solution)/shard_map/ppermute | solution.py:303
  50.8 1.0 copy-start.1
  70.0 7.3 %collective-permute-start.7 = (bf16[4,2,4,16,640]{4,3,2,1,0:T(8,128)(2,1)}, bf16[4,2,4,16,640]{4,3,2,1,0:T(8,128)(2,1)S(1)}, u32[]{:S(2)}, u32[]{:S(2)}) collective-permute-start(bf16[4,2,4,16,640]{4,3,2,1,0:T(8,128)(2,1)} %get-tuple-element.44), channel_id=1, source_target_pairs={{0,1},{1,0},{2,3},{3,2},{4,5},{5,4},{6,7},{7,6},{8,9},{9,8},{10,11... | collective-permute-start | bytes 1966088 | tf_op jit(solution)/shard_map/ppermute | solution.py:303
  70.4 22.2 %all-to-all-start.3 = ((bf16[8,128,640]{2,1,0:T(8,128)(2,1)}), bf16[8,128,640]{2,1,0:T(8,128)(2,1)}, u32[]{:S(2)}, u32[]{:S(2)}) async-start(bf16[8,128,640]{2,1,0:T(8,128)(2,1)} %get-tuple-element.41), calls=%async_computation.3 | async-start | bytes 2621440 | tf_op jit(solution)/shard_map/all_to_all | solution.py:312
  74.6 14.9 %collective-permute-start.4 = (bf16[2,512,256]{2,1,0:T(8,128)(2,1)S(1)}, bf16[2,512,256]{2,1,0:T(8,128)(2,1)S(1)}, u32[]{:S(2)}, u32[]{:S(2)}) collective-permute-start(bf16[2,512,256]{2,1,0:T(8,128)(2,1)S(1)} %get-tuple-element.40), channel_id=1, source_target_pairs={{0,64},{64,0},{1,65},{65,1},{2,66},{66,2},{3,67},{67,3},{4,68},{68... | collective-permute-start | bytes 1572872 | tf_op jit(solution)/shard_map/ppermute | solution.py:308
  77.5 12.2 %collective-permute-start.10 = (bf16[2,4,16,640]{3,2,1,0:T(8,128)(2,1)S(1)}, bf16[2,4,16,640]{3,2,1,0:T(8,128)(2,1)S(1)}, u32[]{:S(2)}, u32[]{:S(2)}) collective-permute-start(bf16[2,4,16,640]{3,2,1,0:T(8,128)(2,1)S(1)} %get-tuple-element.72), channel_id=1, source_target_pairs={{0,48},{16,0},{32,16},{48,32},{1,49},{17,1},{33,17},{49,33},{2,50}... | collective-permute-start | bytes 491528 | tf_op jit(solution)/shard_map/ppermute | solution.py:308
  78.5 11.2 %collective-permute-start.8 = (bf16[2,4,16,640]{3,2,1,0:T(8,128)(2,1)S(1)}, bf16[2,4,16,640]{3,2,1,0:T(8,128)(2,1)S(1)}, u32[]{:S(2)}, u32[]{:S(2)}) collective-permute-start(bf16[2,4,16,640]{3,2,1,0:T(8,128)(2,1)S(1)} %get-tuple-element.71), channel_id=1, source_target_pairs={{0,16},{16,32},{32,48},{48,0},{1,17},{17,33},{33,49},{49,1},{2,18}... | collective-permute-start | bytes 491528 | tf_op jit(solution)/shard_map/ppermute | solution.py:308
  79.1 10.7 %collective-permute-start.9 = (bf16[2,4,16,640]{3,2,1,0:T(8,128)(2,1)S(1)}, bf16[2,4,16,640]{3,2,1,0:T(8,128)(2,1)S(1)}, u32[]{:S(2)}, u32[]{:S(2)}) collective-permute-start(bf16[2,4,16,640]{3,2,1,0:T(8,128)(2,1)S(1)} %get-tuple-element.73), channel_id=1, source_target_pairs={{0,32},{16,48},{32,0},{48,16},{1,33},{17,49},{33,1},{49,17},{2,34}... | collective-permute-start | bytes 491528 | tf_op jit(solution)/shard_map/ppermute | solution.py:308
  92.5 13.5 %collective-permute-start.12 = (bf16[2,512,256]{2,1,0:T(8,128)(2,1)S(1)}, bf16[2,512,256]{2,1,0:T(8,128)(2,1)S(1)}, u32[]{:S(2)}, u32[]{:S(2)}) collective-permute-start(bf16[2,512,256]{2,1,0:T(8,128)(2,1)S(1)} %add_convert_fusion.1.refs_0_), channel_id=1, source_target_pairs={{0,1},{1,0},{2,3},{3,2},{4,5},{5,4},{6,7},{7,6},{8,9},{9,8},{10,11... | collective-permute-start | bytes 1572872 | tf_op jit(solution)/shard_map/ppermute | solution.py:303
  92.9 9.0 %collective-permute-start.18 = (bf16[2,256,256]{2,1,0:T(8,128)(2,1)S(1)}, bf16[2,256,256]{2,1,0:T(8,128)(2,1)S(1)}, u32[]{:S(2)}, u32[]{:S(2)}) collective-permute-start(bf16[2,256,256]{2,1,0:T(8,128)(2,1)S(1)} %get-tuple-element.74), channel_id=1, source_target_pairs={{0,2},{2,4},{4,6},{6,0},{1,3},{3,5},{5,7},{7,1},{8,10},{10,12},{12... | collective-permute-start | bytes 786440 | tf_op jit(solution)/shard_map/ppermute | solution.py:308
  93.5 3.4 %collective-permute-start.11 = (bf16[4,16,640]{2,1,0:T(8,128)(2,1)S(1)}, bf16[4,16,640]{2,1,0:T(8,128)(2,1)S(1)}, u32[]{:S(2)}, u32[]{:S(2)}) collective-permute-start(bf16[4,16,640]{2,1,0:T(8,128)(2,1)S(1)} %slice_bitcast_fusion.4), channel_id=1, source_target_pairs={{0,8},{8,0},{1,9},{9,1},{2,10},{10,2},{3,11},{11,3},{4,12},{12,4},... | collective-permute-start | bytes 245768 | tf_op jit(solution)/shard_map/ppermute | solution.py:308
  93.5 12.5 %collective-permute-start.19 = (bf16[2,256,256]{2,1,0:T(8,128)(2,1)S(1)}, bf16[2,256,256]{2,1,0:T(8,128)(2,1)S(1)}, u32[]{:S(2)}, u32[]{:S(2)}) collective-permute-start(bf16[2,256,256]{2,1,0:T(8,128)(2,1)S(1)} %get-tuple-element.75), channel_id=1, source_target_pairs={{0,6},{2,0},{4,2},{6,4},{1,7},{3,1},{5,3},{7,5},{8,14},{10,8},{12,... | collective-permute-start | bytes 786440 | tf_op jit(solution)/shard_map/ppermute | solution.py:308
  95.9 12.1 %collective-permute-start.5 = (bf16[2,256,256]{2,1,0:T(8,128)(2,1)S(1)}, bf16[2,256,256]{2,1,0:T(8,128)(2,1)S(1)}, u32[]{:S(2)}, u32[]{:S(2)}) collective-permute-start(bf16[2,256,256]{2,1,0:T(8,128)(2,1)S(1)} %get-tuple-element.75), channel_id=1, source_target_pairs={{0,2},{2,4},{4,6},{6,0},{1,3},{3,5},{5,7},{7,1},{8,10},{10,12},{12... | collective-permute-start | bytes 786440 | tf_op jit(solution)/shard_map/ppermute | solution.py:308
  96.8 11.2 %collective-permute-start.6 = (bf16[2,256,256]{2,1,0:T(8,128)(2,1)S(1)}, bf16[2,256,256]{2,1,0:T(8,128)(2,1)S(1)}, u32[]{:S(2)}, u32[]{:S(2)}) collective-permute-start(bf16[2,256,256]{2,1,0:T(8,128)(2,1)S(1)} %get-tuple-element.74), channel_id=1, source_target_pairs={{0,6},{2,0},{4,2},{6,4},{1,7},{3,1},{5,3},{7,5},{8,14},{10,8},{12,... | collective-permute-start | bytes 786440 | tf_op jit(solution)/shard_map/ppermute | solution.py:308
  102.0 6.7 %collective-permute-start.21 = (bf16[2,256,256]{2,1,0:T(8,128)(2,1)S(1)}, bf16[2,256,256]{2,1,0:T(8,128)(2,1)S(1)}, u32[]{:S(2)}, u32[]{:S(2)}) collective-permute-start(bf16[2,256,256]{2,1,0:T(8,128)(2,1)S(1)} %collective-permute-done.18.refs_1_), channel_id=1, source_target_pairs={{0,1},{1,0},{2,3},{3,2},{4,5},{5,4},{6,7},{7,6},{8,9},{9,8},{10,11... | collective-permute-start | bytes 786440 | tf_op jit(solution)/shard_map/ppermute | solution.py:303
  106.0 5.5 %collective-permute-start.22 = (bf16[2,256,256]{2,1,0:T(8,128)(2,1)S(1)}, bf16[2,256,256]{2,1,0:T(8,128)(2,1)S(1)}, u32[]{:S(2)}, u32[]{:S(2)}) collective-permute-start(bf16[2,256,256]{2,1,0:T(8,128)(2,1)S(1)} %collective-permute-done.19.refs_2_), channel_id=1, source_target_pairs={{0,1},{1,0},{2,3},{3,2},{4,5},{5,4},{6,7},{7,6},{8,9},{9,8},{10,11... | collective-permute-start | bytes 786440 | tf_op jit(solution)/shard_map/ppermute | solution.py:303
  108.0 3.6 %collective-permute-start.20 = (bf16[2,256,256]{2,1,0:T(8,128)(2,1)S(1)}, bf16[2,256,256]{2,1,0:T(8,128)(2,1)S(1)}, u32[]{:S(2)}, u32[]{:S(2)}) collective-permute-start(bf16[2,256,256]{2,1,0:T(8,128)(2,1)S(1)} %collective-permute-done.5.refs_0_), channel_id=1, source_target_pairs={{0,1},{1,0},{2,3},{3,2},{4,5},{5,4},{6,7},{7,6},{8,9},{9,8},{10,11... | collective-permute-start | bytes 786440 | tf_op jit(solution)/shard_map/ppermute | solution.py:303
  108.6 5.6 %collective-permute-start.23 = (bf16[2,256,256]{2,1,0:T(8,128)(2,1)S(1)}, bf16[2,256,256]{2,1,0:T(8,128)(2,1)S(1)}, u32[]{:S(2)}, u32[]{:S(2)}) collective-permute-start(bf16[2,256,256]{2,1,0:T(8,128)(2,1)S(1)} %collective-permute-done.6.refs_3_), channel_id=1, source_target_pairs={{0,1},{1,0},{2,3},{3,2},{4,5},{5,4},{6,7},{7,6},{8,9},{9,8},{10,11... | collective-permute-start | bytes 786440 | tf_op jit(solution)/shard_map/ppermute | solution.py:303
  108.7 10.4 %collective-permute-start.13 = (bf16[2,256,256]{2,1,0:T(8,128)(2,1)S(1)}, bf16[2,256,256]{2,1,0:T(8,128)(2,1)S(1)}, u32[]{:S(2)}, u32[]{:S(2)}) collective-permute-start(bf16[2,256,256]{2,1,0:T(8,128)(2,1)S(1)} %collective-permute-done.5.refs_0_), channel_id=1, source_target_pairs={{0,2},{2,4},{4,6},{6,0},{1,3},{3,5},{5,7},{7,1},{8,10},{10,12},{12... | collective-permute-start | bytes 786440 | tf_op jit(solution)/shard_map/ppermute | solution.py:308
  108.7 10.4 %collective-permute-start.14 = (bf16[2,256,256]{2,1,0:T(8,128)(2,1)S(1)}, bf16[2,256,256]{2,1,0:T(8,128)(2,1)S(1)}, u32[]{:S(2)}, u32[]{:S(2)}) collective-permute-start(bf16[2,256,256]{2,1,0:T(8,128)(2,1)S(1)} %collective-permute-done.6.refs_3_), channel_id=1, source_target_pairs={{0,6},{2,0},{4,2},{6,4},{1,7},{3,1},{5,3},{7,5},{8,14},{10,8},{12,... | collective-permute-start | bytes 786440 | tf_op jit(solution)/shard_map/ppermute | solution.py:308
  111.5 6.4 %collective-permute-start.15 = (bf16[16,640]{1,0:T(8,128)(2,1)S(1)}, bf16[16,640]{1,0:T(8,128)(2,1)S(1)}, u32[]{:S(2)}, u32[]{:S(2)}) collective-permute-start(bf16[16,640]{1,0:T(8,128)(2,1)S(1)} %get-tuple-element.78), channel_id=1, source_target_pairs={{0,2},{2,4},{4,6},{6,0},{1,3},{3,5},{5,7},{7,1},{8,10},{10,12},{12... | collective-permute-start | bytes 61448 | tf_op jit(solution)/shard_map/ppermute | solution.py:308
  111.6 7.5 %collective-permute-start.16 = (bf16[16,640]{1,0:T(8,128)(2,1)S(1)}, bf16[16,640]{1,0:T(8,128)(2,1)S(1)}, u32[]{:S(2)}, u32[]{:S(2)}) collective-permute-start(bf16[16,640]{1,0:T(8,128)(2,1)S(1)} %get-tuple-element.77), channel_id=1, source_target_pairs={{0,4},{2,6},{4,0},{6,2},{1,5},{3,7},{5,1},{7,3},{8,12},{10,14},{12... | collective-permute-start | bytes 61448 | tf_op jit(solution)/shard_map/ppermute | solution.py:308
  114.2 4.9 %collective-permute-start.17 = (bf16[16,640]{1,0:T(8,128)(2,1)S(1)}, bf16[16,640]{1,0:T(8,128)(2,1)S(1)}, u32[]{:S(2)}, u32[]{:S(2)}) collective-permute-start(bf16[16,640]{1,0:T(8,128)(2,1)S(1)} %get-tuple-element.76), channel_id=1, source_target_pairs={{0,6},{2,0},{4,2},{6,4},{1,7},{3,1},{5,3},{7,5},{8,14},{10,8},{12,... | collective-permute-start | bytes 61448 | tf_op jit(solution)/shard_map/ppermute | solution.py:308
  119.1 2.9 %collective-permute-start.24 = (bf16[2,256,256]{2,1,0:T(8,128)(2,1)S(1)}, bf16[2,256,256]{2,1,0:T(8,128)(2,1)S(1)}, u32[]{:S(2)}, u32[]{:S(2)}) collective-permute-start(bf16[2,256,256]{2,1,0:T(8,128)(2,1)S(1)} %collective-permute-done.13.refs_0_), channel_id=1, source_target_pairs={{0,1},{1,0},{2,3},{3,2},{4,5},{5,4},{6,7},{7,6},{8,9},{9,8},{10,11... | collective-permute-start | bytes 786440 | tf_op jit(solution)/shard_map/ppermute | solution.py:303
  120.8 1.5 %collective-permute-start.25 = (bf16[2,256,256]{2,1,0:T(8,128)(2,1)S(1)}, bf16[2,256,256]{2,1,0:T(8,128)(2,1)S(1)}, u32[]{:S(2)}, u32[]{:S(2)}) collective-permute-start(bf16[2,256,256]{2,1,0:T(8,128)(2,1)S(1)} %collective-permute-done.14.refs_1_), channel_id=1, source_target_pairs={{0,1},{1,0},{2,3},{3,2},{4,5},{5,4},{6,7},{7,6},{8,9},{9,8},{10,11... | collective-permute-start | bytes 786440 | tf_op jit(solution)/shard_map/ppermute | solution.py:303

commit v5 on v4

--- a/solution.py
+++ b/solution.py
@@ -51,8 +51,14 @@
     ]
     for s in range(n_x):
         x = lax.rem(x_here + n_x - s, n_x)
-        keys[at_block(2 * x + core), :] = own_ref[s]
-        keys[at_block(2 * x + 1 - core), :] = other_ref[s]
+        n_z, n_y, _, rows = keep_ref.shape[:4]
+        for dz in range(n_z):
+            for dy in range(n_y):
+                head = lax.rem(z_here + n_z - dz, n_z) * n_y + lax.rem(y_here + n_y - dy, n_y)
+                at_row = (dy * n_z + dz) * rows
+                for ref, parity in ((own_ref, core), (other_ref, 1 - core)):
+                    start = pl.multiple_of((2 * x + parity) * BLOCK + head * rows, rows)
+                    keys[pl.ds(start, rows), :] = ref[s, at_row:at_row + rows, :]
     flipped[:LATENT, :] = jnp.transpose(keys[:, :LATENT])
     flipped[LATENT:, :] = jnp.transpose(keys[:, LATENT:])
     total[...] = jnp.zeros_like(total)
@@ -339,13 +345,15 @@
     fine_axes = ("core", "x")
     grads = jnp.swapaxes(out_grad.reshape(BLOCK, 2 * n_x, -1), 0, 1)
     arrived = pack(queries, n_head, n_x)
-    own = exchanged(copies(latent, n_head), HEAD_AXES)
+    own = jnp.stack([latent] + [shifted(latent, "z", s) for s in range(1, n_z)])
+    own, grads = lax.optimization_barrier((own, grads))
+    grads = exchanged(grads, fine_axes)
+    own = jnp.stack([own] + [shifted(own, "y", s) for s in range(1, n_y)]).reshape(BLOCK, KEY)
     own, arrived = lax.optimization_barrier((own, arrived))
+    grads, arrived = lax.optimization_barrier((grads, arrived))
     arrived = exchanged(arrived, ("x", "core") + HEAD_AXES).reshape(2 * n_x * BLOCK, -1)
-    own = own.reshape(BLOCK, KEY)
     own = jnp.stack([own] + [shifted(own, "x", s) for s in range(1, n_x)])
     other = swapped(own)
-    grads = exchanged(grads, fine_axes)
 
     back, kv, rows_keep, rows_send = attention(
         place, block_docs, arrived, own, other, key_up, value_up, grads, n_z, n_y

time: 125 us -> 121 us (0.968)
  waiting for transfers between devices: 37.7 us -> 34.5 us
  local copies, waits for them, and re-layouts: 5.49 us -> 4.09 us
    ppermute x17 -> x21, starting transfers between devices: 21.4 us -> 27.7 us  [shifted(): lax.ppermute(value, axis, [(i, (i + steps) % count) for i in range(count)])]
    all_to_all x4 -> x3, starting transfers between devices: 22.5 us -> 17.1 us  [exchanged(): return lax.all_to_all(value, axes, 0, 0, tiled=True)]
    all_to_all x4 -> x3, waiting for transfers between devices: 18.5 us -> 14.8 us  [exchanged(): return lax.all_to_all(value, axes, 0, 0, tiled=True)]
    broadcast_in_dim x1 -> x0, local copies, waits for them, and re-layouts: 1.41 us -> none  [copies(): return jnp.broadcast_to(value[None], (count,) + value.shape)]
    ppermute x17 -> x21, waiting for transfers between devices: 16.8 us -> 17.3 us  [shifted(): lax.ppermute(value, axis, [(i, (i + steps) % count) for i in range(count)])]
  transfers between devices with their start and end apart: 30 -> 33, of which waited for: 13 -> 13; matrix products, arithmetic and copies ran while one was open for 3% -> 4% of each run, Pallas kernels for 7% -> 8%
where the time goes in v5:
time: 121 us
  starting transfers between devices  50.7 us (42%)
  waiting for transfers between devices  34.5 us (29%)
  Pallas kernels  29.2 us (24%)
  local copies, waits for them, and re-layouts  4.09 us (3%)
  other arithmetic  1.28 us (1%)
    ppermute x21, starting transfers between devices, shifted(): lax.ppermute(value, axis, [(i, (i + steps) % count) for i in range(count)])  27.7 us
    pallas_call x1, Pallas kernels, attention(): pl.pallas_call(attention_kernel, grid_spec=pltpu.PrefetchScalarGridSpec(n...  18.1 us
    ppermute x21, waiting for transfers between devices, shifted(): lax.ppermute(value, axis, [(i, (i + steps) % count) for i in range(count)])  17.3 us
    all_to_all x3, starting transfers between devices, exchanged(): return lax.all_to_all(value, axes, 0, 0, tiled=True)  17.1 us
    all_to_all x3, waiting for transfers between devices, exchanged(): return lax.all_to_all(value, axes, 0, 0, tiled=True)  14.8 us
    pallas_call x3, Pallas kernels, unfold(): pl.pallas_call(kernel, grid_spec=pltpu.PrefetchScalarGridSpec(num_scalar_...  6.57 us
    ppermute x9, starting transfers between devices, swapped(): return lax.ppermute(value, 'core', [(0, 1), (1, 0)])  5.92 us
    pallas_call x1, Pallas kernels, join(): pl.pallas_call(kernel, out_shape=[jax.ShapeDtypeStruct((rows, slots * val...  2.5 us
  transfers between devices with their start and end apart: 33, of which 13 were waited for; matrix products, arithmetic and copies ran while one was open for 4% of the time, Pallas kernels for 8%

profile of v5, /device:TPU:1, one launch (start us, length us, event | category | flops | bytes accessed | tf_op | source)
XLA Modules:
  0.0 120.9 jit_solution(7263103339666130151)
XLA Ops:
  0.6 2.5 %collective-permute-start = (bf16[16,576]{1,0:T(8,128)(2,1)}, bf16[16,576]{1,0:T(8,128)(2,1)S(1)}, u32[]{:S(2)}, u32[]{:S(2)}) collective-permute-start(bf16[16,576]{1,0:T(8,128)(2,1)} %param.7), channel_id=1, source_target_pairs={{0,16},{16,32},{32,48},{48,0},{1,17},{17,33},{33,49},{49,1},{2,18}... | collective-permute-start | bytes 55304 | tf_op jit(solution)/shard_map/ppermute | solution.py:314
  3.2 3.3 %collective-permute-start.1 = (bf16[16,576]{1,0:T(8,128)(2,1)}, bf16[16,576]{1,0:T(8,128)(2,1)S(1)}, u32[]{:S(2)}, u32[]{:S(2)}) collective-permute-start(bf16[16,576]{1,0:T(8,128)(2,1)} %param.7), channel_id=1, source_target_pairs={{0,32},{16,48},{32,0},{48,16},{1,33},{17,49},{33,1},{49,17},{2,34}... | collective-permute-start | bytes 55304 | tf_op jit(solution)/shard_map/ppermute | solution.py:314
  6.5 0.7 collective-permute-start.2
  7.2 1.3 %copy.17 = bf16[128,2048]{0,1:T(8,128)(2,1)S(1)} copy(bf16[128,2048]{1,0:T(8,128)(2,1)} %param.10) | data formatting | bytes 1048576 | tf_op args[4]
  8.5 1.0 copy.18
  9.6 6.5 %all-to-all-start = ((bf16[8,128,256]{2,1,0:T(8,128)(2,1)}), bf16[8,128,256]{2,1,0:T(8,128)(2,1)S(1)}, u32[]{:S(2)}, u32[]{:S(2)}) async-start(bf16[8,128,256]{2,1,0:T(8,128)(2,1)} %bitcast.9), calls=%async_computation | async-start | bytes 1048576 | tf_op jit(solution)/shard_map/all_to_all | solution.py:318
  16.0 1.3 %collective-permute-start.3 = (bf16[4,16,576]{2,1,0:T(8,128)(2,1)S(1)}, bf16[4,16,576]{2,1,0:T(8,128)(2,1)S(1)}, u32[]{:S(2)}, u32[]{:S(2)}) collective-permute-start(bf16[4,16,576]{2,1,0:T(8,128)(2,1)S(1)} %pad_maximum_fusion.2), channel_id=1, source_target_pairs={{0,8},{8,0},{1,9},{9,1},{2,10},{10,2},{3,11},{11,3},{4,12},{12,4},... | collective-permute-start | bytes 221192 | tf_op jit(solution)/shard_map/ppermute | solution.py:314
  17.3 2.1 %pack.1 = bf16[64,16,384]{2,1,0:T(8,128)(2,1)} custom-call(bf16[16,24576]{1,0:T(8,128)(2,1)} %query_ref.1), custom_call_target="tpu_custom_call" | custom-call | tf_op jit(solution)/shard_map/pack/pallas_call | solution.py:301
  19.4 0.7 collective-permute-done.3
  20.2 1.0 collective-permute-start.4
  21.2 2.4 %collective-permute-start.5 = (bf16[128,576]{1,0:T(8,128)(2,1)S(1)}, bf16[128,576]{1,0:T(8,128)(2,1)S(1)}, u32[]{:S(2)}, u32[]{:S(2)}) collective-permute-start(bf16[128,576]{1,0:T(8,128)(2,1)S(1)} %bitcast.47), channel_id=1, source_target_pairs={{0,4},{2,6},{4,0},{6,2},{1,5},{3,7},{5,1},{7,3},{8,12},{10,14},{12... | collective-permute-start | bytes 442376 | tf_op jit(solution)/shard_map/ppermute | solution.py:314
  23.6 1.2 collective-permute-start.6
  24.8 1.0 all-to-all-done.grad_ref
  25.7 6.3 %all-to-all-start.1 = ((bf16[64,16,384]{2,1,0:T(8,128)(2,1)}), bf16[64,16,384]{2,1,0:T(8,128)(2,1)S(1)}, u32[]{:S(2)}, u32[]{:S(2)}) async-start(bf16[64,16,384]{2,1,0:T(8,128)(2,1)} %pack.1), calls=%async_computation.1 | async-start | bytes 1572864 | tf_op jit(solution)/shard_map/all_to_all | solution.py:318
  32.1 0.5 collective-permute-done.5
  33.1 1.1 collective-permute-start.7
  34.3 1.6 %collective-permute-done.7 = bf16[4,128,576]{1,2,0:T(8,128)(2,1)S(1)} collective-permute-done((bf16[4,128,576]{1,2,0:T(8,128)(2,1)S(1)}, bf16[4,128,576]{1,2,0:T(8,128)(2,1)S(1)}, u32[]{:S(2)}, u32[]{:S(2)}) %collective-permute-start.7) | collective-permute-done | bytes 589856 | tf_op jit(solution)/shard_map/ppermute | solution.py:309
  36.1 11.1 %all-to-all-done.1 = bf16[64,16,384]{2,1,0:T(8,128)(2,1)S(1)} async-done(((bf16[64,16,384]{2,1,0:T(8,128)(2,1)}), bf16[64,16,384]{2,1,0:T(8,128)(2,1)S(1)}, u32[]{:S(2)}, u32[]{:S(2)}) %all-to-all-start.1) | async-done | bytes 786464 | tf_op jit(solution)/shard_map/all_to_all | solution.py:318
  47.2 1.0 copy-done.1
  48.3 18.1 %attention.1 = (bf16[8,128,640]{2,1,0:T(8,128)(2,1)}, bf16[2,512,256]{2,1,0:T(8,128)(2,1)S(1)}, bf16[4,2,4,16,640]{4,3,2,1,0:T(8,128)(2,1)S(1)}, bf16[4,2,4,16,640]{4,3,2,1,0:T(8,128)(2,1)}) custom-call(s32[4]{0:T(128)S(1)} %pad_add_fusion.place, s32[1,8]{1,0:T(1,128)S(1)} %copy-done.2, bf16[1024,384]{1,0:T(8,128)(2,1)S(1)} %bitcast.44, ...), custom_call_target="tpu_custom_call" | custom-call | flops 8999999488 | bytes 15000000 | tf_op jit(solution)/shard_map/attention/pallas_call | solution.py:182
  66.3 0.4 collective-permute-start.11
  66.7 4.3 %all-to-all-start.2 = ((bf16[8,128,640]{2,1,0:T(8,128)(2,1)}), bf16[8,128,640]{2,1,0:T(8,128)(2,1)}, u32[]{:S(2)}, u32[]{:S(2)}) async-start(bf16[8,128,640]{2,1,0:T(8,128)(2,1)} %get-tuple-element.49), calls=%async_computation.2 | async-start | bytes 2621440 | tf_op jit(solution)/shard_map/all_to_all | solution.py:318
  71.0 2.6 %collective-permute-start.8 = (bf16[2,512,256]{2,1,0:T(8,128)(2,1)S(1)}, bf16[2,512,256]{2,1,0:T(8,128)(2,1)S(1)}, u32[]{:S(2)}, u32[]{:S(2)}) collective-permute-start(bf16[2,512,256]{2,1,0:T(8,128)(2,1)S(1)} %get-tuple-element.48), channel_id=1, source_target_pairs={{0,64},{64,0},{1,65},{65,1},{2,66},{66,2},{3,67},{67,3},{4,68},{68... | collective-permute-start | bytes 1572872 | tf_op jit(solution)/shard_map/ppermute | solution.py:314
  73.9 0.4 collective-permute-start.12
  74.2 1.8 %collective-permute-start.13 = (bf16[2,4,16,640]{3,2,1,0:T(8,128)(2,1)S(1)}, bf16[2,4,16,640]{3,2,1,0:T(8,128)(2,1)S(1)}, u32[]{:S(2)}, u32[]{:S(2)}) collective-permute-start(bf16[2,4,16,640]{3,2,1,0:T(8,128)(2,1)S(1)} %get-tuple-element.81), channel_id=1, source_target_pairs={{0,32},{16,48},{32,0},{48,16},{1,33},{17,49},{33,1},{49,17},{2,34}... | collective-permute-start | bytes 491528 | tf_op jit(solution)/shard_map/ppermute | solution.py:314
  76.0 0.7 collective-permute-start.14
  76.7 9.2 %collective-permute-done.8 = bf16[2,512,256]{2,1,0:T(8,128)(2,1)S(1)} collective-permute-done((bf16[2,512,256]{2,1,0:T(8,128)(2,1)S(1)}, bf16[2,512,256]{2,1,0:T(8,128)(2,1)S(1)}, u32[]{:S(2)}, u32[]{:S(2)}) %collective-permute-start.8) | collective-permute-done | bytes 524320 | tf_op jit(solution)/shard_map/ppermute | solution.py:314
  86.2 2.7 %all-to-all-done.2.back_ref = bf16[8,128,640]{2,1,0:T(8,128)(2,1)} async-done(((bf16[8,128,640]{2,1,0:T(8,128)(2,1)}), bf16[8,128,640]{2,1,0:T(8,128)(2,1)}, u32[]{:S(2)}, u32[]{:S(2)}) %all-to-all-start.2) | async-done | bytes 1310752 | tf_op jit(solution)/shard_map/all_to_all | solution.py:318
  89.3 0.5 collective-permute-start.22
  89.9 2.3 %collective-permute-start.23 = (bf16[2,256,256]{2,1,0:T(8,128)(2,1)S(1)}, bf16[2,256,256]{2,1,0:T(8,128)(2,1)S(1)}, u32[]{:S(2)}, u32[]{:S(2)}) collective-permute-start(bf16[2,256,256]{2,1,0:T(8,128)(2,1)S(1)} %get-tuple-element.83), channel_id=1, source_target_pairs={{0,6},{2,0},{4,2},{6,4},{1,7},{3,1},{5,3},{7,5},{8,14},{10,8},{12,... | collective-permute-start | bytes 786440 | tf_op jit(solution)/shard_map/ppermute | solution.py:314
  92.5 0.7 collective-permute-done.15
  93.2 0.5 collective-permute-start.9
  93.7 4.7 %collective-permute-done.22.refs_1_ = bf16[2,256,256]{2,1,0:T(8,128)(2,1)S(1)} collective-permute-done((bf16[2,256,256]{2,1,0:T(8,128)(2,1)S(1)}, bf16[2,256,256]{2,1,0:T(8,128)(2,1)S(1)}, u32[]{:S(2)}, u32[]{:S(2)}) %collective-permute-start.22) | collective-permute-done | bytes 262176 | tf_op jit(solution)/shard_map/ppermute | solution.py:314
  98.4 1.5 %collective-permute-start.25 = (bf16[2,256,256]{2,1,0:T(8,128)(2,1)S(1)}, bf16[2,256,256]{2,1,0:T(8,128)(2,1)S(1)}, u32[]{:S(2)}, u32[]{:S(2)}) collective-permute-start(bf16[2,256,256]{2,1,0:T(8,128)(2,1)S(1)} %collective-permute-done.22.refs_1_), channel_id=1, source_target_pairs={{0,1},{1,0},{2,3},{3,2},{4,5},{5,4},{6,7},{7,6},{8,9},{9,8},{10,11... | collective-permute-start | bytes 786440 | tf_op jit(solution)/shard_map/ppermute | solution.py:309
  99.9 2.5 %join.1 = (bf16[128,2048]{1,0:T(8,128)(2,1)}, bf16[128,3072]{1,0:T(8,128)(2,1)}) custom-call(bf16[8,128,640]{2,1,0:T(8,128)(2,1)} %all-to-all-done.2.back_ref), custom_call_target="tpu_custom_call" | custom-call | tf_op jit(solution)/shard_map/join/pallas_call | solution.py:227
  102.4 1.9 %unfold.3 = (f32[16,512,128]{2,1,0:T(8,128)}, f32[16,512,128]{2,1,0:T(8,128)}) custom-call(s32[4]{0:T(128)S(1)} %pad_add_fusion.place, bf16[2,512,256]{2,1,0:T(8,128)(2,1)S(1)} %add_convert_fusion.1.refs_0_, bf16[2,512,256]{2,1,0:T(8,128)(2,1)S(1)} %collective-permute-done.16.refs_1_), custom_call_target="tpu_custom_call" | custom-call | bytes 4000000 | tf_op jit(solution)/shard_map/unfold/pallas_call | solution.py:271
  104.4 0.6 collective-permute-start.24
  105.1 2.8 %collective-permute-start.18 = (bf16[2,256,256]{2,1,0:T(8,128)(2,1)S(1)}, bf16[2,256,256]{2,1,0:T(8,128)(2,1)S(1)}, u32[]{:S(2)}, u32[]{:S(2)}) collective-permute-start(bf16[2,256,256]{2,1,0:T(8,128)(2,1)S(1)} %collective-permute-done.10.refs_3_), channel_id=1, source_target_pairs={{0,6},{2,0},{4,2},{6,4},{1,7},{3,1},{5,3},{7,5},{8,14},{10,8},{12,... | collective-permute-start | bytes 786440 | tf_op jit(solution)/shard_map/ppermute | solution.py:314
  108.0 2.6 %collective-permute-start.20 = (bf16[16,640]{1,0:T(8,128)(2,1)S(1)}, bf16[16,640]{1,0:T(8,128)(2,1)S(1)}, u32[]{:S(2)}, u32[]{:S(2)}) collective-permute-start(bf16[16,640]{1,0:T(8,128)(2,1)S(1)} %get-tuple-element.85), channel_id=1, source_target_pairs={{0,4},{2,6},{4,0},{6,2},{1,5},{3,7},{5,1},{7,3},{8,12},{10,14},{12... | collective-permute-start | bytes 61448 | tf_op jit(solution)/shard_map/ppermute | solution.py:314
  110.5 0.6 collective-permute-start.21
  111.1 2.7 %unfold.4 = (f32[16,512,128]{2,1,0:T(8,128)}, f32[16,512,128]{2,1,0:T(8,128)}) custom-call(s32[4]{0:T(128)S(1)} %pad_add_fusion.place, bf16[2,256,256]{2,1,0:T(8,128)(2,1)S(1)} %collective-permute-done.9.refs_0_, bf16[2,256,256]{2,1,0:T(8,128)(2,1)S(1)} %collective-permute-done.22.refs_1_, ...), custom_call_target="tpu_custom_call", output_to_operand_aliasing={{0}: (9, {}), {1}: (10, {})} | custom-call | bytes 4000000 | tf_op jit(solution)/shard_map/unfold/pallas_call | solution.py:271
  113.9 0.4 collective-permute-done.19
  114.3 1.1 collective-permute-done.20
  115.5 1.7 %collective-permute-start.28 = (bf16[2,256,256]{2,1,0:T(8,128)(2,1)S(1)}, bf16[2,256,256]{2,1,0:T(8,128)(2,1)S(1)}, u32[]{:S(2)}, u32[]{:S(2)}) collective-permute-start(bf16[2,256,256]{2,1,0:T(8,128)(2,1)S(1)} %collective-permute-done.17.refs_0_), channel_id=1, source_target_pairs={{0,1},{1,0},{2,3},{3,2},{4,5},{5,4},{6,7},{7,6},{8,9},{9,8},{10,11... | collective-permute-start | bytes 786440 | tf_op jit(solution)/shard_map/ppermute | solution.py:309
  117.3 0.6 convert_add_fusion.2
  117.9 0.4 collective-permute-done.28.refs_2_
  118.4 0.4 collective-permute-done.29.refs_3_
  118.7 1.9 %unfold.5 = (f32[16,512,128]{2,1,0:T(8,128)}, f32[16,512,128]{2,1,0:T(8,128)}) custom-call(s32[4]{0:T(128)S(1)} %pad_add_fusion.place, bf16[2,256,256]{2,1,0:T(8,128)(2,1)S(1)} %collective-permute-done.17.refs_0_, bf16[2,256,256]{2,1,0:T(8,128)(2,1)S(1)} %collective-permute-done.18.refs_1_, ...), custom_call_target="tpu_custom_call", output_to_operand_aliasing={{0}: (5, {}), {1}: (6, {})} | custom-call | bytes 4000000 | tf_op jit(solution)/shard_map/unfold/pallas_call | solution.py:271
  (49 shorter events, 2.4 us)
Async XLA Ops:
  0.6 8.9 %copy-start.3 = (bf16[16,576]{1,0:T(8,128)(2,1)S(1)}, bf16[16,576]{1,0:T(8,128)(2,1)}, u32[]{:S(2)}) copy-start(bf16[16,576]{1,0:T(8,128)(2,1)} %param.7) | copy-start | bytes 55300
  0.6 8.9 %collective-permute-start = (bf16[16,576]{1,0:T(8,128)(2,1)}, bf16[16,576]{1,0:T(8,128)(2,1)S(1)}, u32[]{:S(2)}, u32[]{:S(2)}) collective-permute-start(bf16[16,576]{1,0:T(8,128)(2,1)} %param.7), channel_id=1, source_target_pairs={{0,16},{16,32},{32,48},{48,0},{1,17},{17,33},{33,49},{49,1},{2,18}... | collective-permute-start | bytes 55304 | tf_op jit(solution)/shard_map/ppermute | solution.py:314
  3.2 6.4 %collective-permute-start.1 = (bf16[16,576]{1,0:T(8,128)(2,1)}, bf16[16,576]{1,0:T(8,128)(2,1)S(1)}, u32[]{:S(2)}, u32[]{:S(2)}) collective-permute-start(bf16[16,576]{1,0:T(8,128)(2,1)} %param.7), channel_id=1, source_target_pairs={{0,32},{16,48},{32,0},{48,16},{1,33},{17,49},{33,1},{49,17},{2,34}... | collective-permute-start | bytes 55304 | tf_op jit(solution)/shard_map/ppermute | solution.py:314
  6.5 3.1 %collective-permute-start.2 = (bf16[16,576]{1,0:T(8,128)(2,1)}, bf16[16,576]{1,0:T(8,128)(2,1)S(1)}, u32[]{:S(2)}, u32[]{:S(2)}) collective-permute-start(bf16[16,576]{1,0:T(8,128)(2,1)} %param.7), channel_id=1, source_target_pairs={{0,48},{16,0},{32,16},{48,32},{1,49},{17,1},{33,17},{49,33},{2,50}... | collective-permute-start | bytes 55304 | tf_op jit(solution)/shard_map/ppermute | solution.py:314
  9.6 16.1 %all-to-all-start = ((bf16[8,128,256]{2,1,0:T(8,128)(2,1)}), bf16[8,128,256]{2,1,0:T(8,128)(2,1)S(1)}, u32[]{:S(2)}, u32[]{:S(2)}) async-start(bf16[8,128,256]{2,1,0:T(8,128)(2,1)} %bitcast.9), calls=%async_computation | async-start | bytes 1048576 | tf_op jit(solution)/shard_map/all_to_all | solution.py:318
  16.0 4.1 %collective-permute-start.3 = (bf16[4,16,576]{2,1,0:T(8,128)(2,1)S(1)}, bf16[4,16,576]{2,1,0:T(8,128)(2,1)S(1)}, u32[]{:S(2)}, u32[]{:S(2)}) collective-permute-start(bf16[4,16,576]{2,1,0:T(8,128)(2,1)S(1)} %pad_maximum_fusion.2), channel_id=1, source_target_pairs={{0,8},{8,0},{1,9},{9,1},{2,10},{10,2},{3,11},{11,3},{4,12},{12,4},... | collective-permute-start | bytes 221192 | tf_op jit(solution)/shard_map/ppermute | solution.py:314
  20.2 11.9 %collective-permute-start.4 = (bf16[128,576]{1,0:T(8,128)(2,1)S(1)}, bf16[128,576]{1,0:T(8,128)(2,1)S(1)}, u32[]{:S(2)}, u32[]{:S(2)}) collective-permute-start(bf16[128,576]{1,0:T(8,128)(2,1)S(1)} %bitcast.46), channel_id=1, source_target_pairs={{0,2},{2,4},{4,6},{6,0},{1,3},{3,5},{5,7},{7,1},{8,10},{10,12},{12... | collective-permute-start | bytes 442376 | tf_op jit(solution)/shard_map/ppermute | solution.py:314
  21.2 11.4 %collective-permute-start.5 = (bf16[128,576]{1,0:T(8,128)(2,1)S(1)}, bf16[128,576]{1,0:T(8,128)(2,1)S(1)}, u32[]{:S(2)}, u32[]{:S(2)}) collective-permute-start(bf16[128,576]{1,0:T(8,128)(2,1)S(1)} %bitcast.47), channel_id=1, source_target_pairs={{0,4},{2,6},{4,0},{6,2},{1,5},{3,7},{5,1},{7,3},{8,12},{10,14},{12... | collective-permute-start | bytes 442376 | tf_op jit(solution)/shard_map/ppermute | solution.py:314
  23.6 9.0 %collective-permute-start.6 = (bf16[128,576]{1,0:T(8,128)(2,1)S(1)}, bf16[128,576]{1,0:T(8,128)(2,1)S(1)}, u32[]{:S(2)}, u32[]{:S(2)}) collective-permute-start(bf16[128,576]{1,0:T(8,128)(2,1)S(1)} %bitcast.48), channel_id=1, source_target_pairs={{0,6},{2,0},{4,2},{6,4},{1,7},{3,1},{5,3},{7,5},{8,14},{10,8},{12,... | collective-permute-start | bytes 442376 | tf_op jit(solution)/shard_map/ppermute | solution.py:314
  25.7 6.9 %copy-start = (bf16[8,128,256]{2,1,0:T(8,128)(2,1)}, bf16[8,128,256]{2,1,0:T(8,128)(2,1)S(1)}, u32[]{:S(2)}) copy-start(bf16[8,128,256]{2,1,0:T(8,128)(2,1)S(1)} %all-to-all-done.grad_ref) | copy-start | bytes 1572868
  25.7 21.5 %all-to-all-start.1 = ((bf16[64,16,384]{2,1,0:T(8,128)(2,1)}), bf16[64,16,384]{2,1,0:T(8,128)(2,1)S(1)}, u32[]{:S(2)}, u32[]{:S(2)}) async-start(bf16[64,16,384]{2,1,0:T(8,128)(2,1)} %pack.1), calls=%async_computation.1 | async-start | bytes 1572864 | tf_op jit(solution)/shard_map/all_to_all | solution.py:318
  32.1 15.1 %copy-start.2 = (s32[1,8]{1,0:T(1,128)S(1)}, s32[1,8]{1,0:T(1,128)}, u32[]{:S(2)}) copy-start(s32[1,8]{1,0:T(1,128)} %docs.1) | copy-start | bytes 100
  33.1 2.8 %collective-permute-start.7 = (bf16[4,128,576]{1,2,0:T(8,128)(2,1)S(1)}, bf16[4,128,576]{1,2,0:T(8,128)(2,1)S(1)}, u32[]{:S(2)}, u32[]{:S(2)}) collective-permute-start(bf16[4,128,576]{1,2,0:T(8,128)(2,1)S(1)} %copy.19), channel_id=1, source_target_pairs={{0,1},{1,0},{2,3},{3,2},{4,5},{5,4},{6,7},{7,6},{8,9},{9,8},{10,11... | collective-permute-start | bytes 1769480 | tf_op jit(solution)/shard_map/ppermute | solution.py:309
  47.2 1.0 copy-start.1
  66.3 7.3 %collective-permute-start.11 = (bf16[4,2,4,16,640]{4,3,2,1,0:T(8,128)(2,1)}, bf16[4,2,4,16,640]{4,3,2,1,0:T(8,128)(2,1)S(1)}, u32[]{:S(2)}, u32[]{:S(2)}) collective-permute-start(bf16[4,2,4,16,640]{4,3,2,1,0:T(8,128)(2,1)} %get-tuple-element.52), channel_id=1, source_target_pairs={{0,1},{1,0},{2,3},{3,2},{4,5},{5,4},{6,7},{7,6},{8,9},{9,8},{10,11... | collective-permute-start | bytes 1966088 | tf_op jit(solution)/shard_map/ppermute | solution.py:309
  66.7 22.2 %all-to-all-start.2 = ((bf16[8,128,640]{2,1,0:T(8,128)(2,1)}), bf16[8,128,640]{2,1,0:T(8,128)(2,1)}, u32[]{:S(2)}, u32[]{:S(2)}) async-start(bf16[8,128,640]{2,1,0:T(8,128)(2,1)} %get-tuple-element.49), calls=%async_computation.2 | async-start | bytes 2621440 | tf_op jit(solution)/shard_map/all_to_all | solution.py:318
  71.0 14.9 %collective-permute-start.8 = (bf16[2,512,256]{2,1,0:T(8,128)(2,1)S(1)}, bf16[2,512,256]{2,1,0:T(8,128)(2,1)S(1)}, u32[]{:S(2)}, u32[]{:S(2)}) collective-permute-start(bf16[2,512,256]{2,1,0:T(8,128)(2,1)S(1)} %get-tuple-element.48), channel_id=1, source_target_pairs={{0,64},{64,0},{1,65},{65,1},{2,66},{66,2},{3,67},{67,3},{4,68},{68... | collective-permute-start | bytes 1572872 | tf_op jit(solution)/shard_map/ppermute | solution.py:314
  73.9 12.2 %collective-permute-start.12 = (bf16[2,4,16,640]{3,2,1,0:T(8,128)(2,1)S(1)}, bf16[2,4,16,640]{3,2,1,0:T(8,128)(2,1)S(1)}, u32[]{:S(2)}, u32[]{:S(2)}) collective-permute-start(bf16[2,4,16,640]{3,2,1,0:T(8,128)(2,1)S(1)} %get-tuple-element.79), channel_id=1, source_target_pairs={{0,16},{16,32},{32,48},{48,0},{1,17},{17,33},{33,49},{49,1},{2,18}... | collective-permute-start | bytes 491528 | tf_op jit(solution)/shard_map/ppermute | solution.py:314
  74.2 11.8 %collective-permute-start.13 = (bf16[2,4,16,640]{3,2,1,0:T(8,128)(2,1)S(1)}, bf16[2,4,16,640]{3,2,1,0:T(8,128)(2,1)S(1)}, u32[]{:S(2)}, u32[]{:S(2)}) collective-permute-start(bf16[2,4,16,640]{3,2,1,0:T(8,128)(2,1)S(1)} %get-tuple-element.81), channel_id=1, source_target_pairs={{0,32},{16,48},{32,0},{48,16},{1,33},{17,49},{33,1},{49,17},{2,34}... | collective-permute-start | bytes 491528 | tf_op jit(solution)/shard_map/ppermute | solution.py:314
  76.0 10.1 %collective-permute-start.14 = (bf16[2,4,16,640]{3,2,1,0:T(8,128)(2,1)S(1)}, bf16[2,4,16,640]{3,2,1,0:T(8,128)(2,1)S(1)}, u32[]{:S(2)}, u32[]{:S(2)}) collective-permute-start(bf16[2,4,16,640]{3,2,1,0:T(8,128)(2,1)S(1)} %get-tuple-element.80), channel_id=1, source_target_pairs={{0,48},{16,0},{32,16},{48,32},{1,49},{17,1},{33,17},{49,33},{2,50}... | collective-permute-start | bytes 491528 | tf_op jit(solution)/shard_map/ppermute | solution.py:314
  88.9 13.5 %collective-permute-start.16 = (bf16[2,512,256]{2,1,0:T(8,128)(2,1)S(1)}, bf16[2,512,256]{2,1,0:T(8,128)(2,1)S(1)}, u32[]{:S(2)}, u32[]{:S(2)}) collective-permute-start(bf16[2,512,256]{2,1,0:T(8,128)(2,1)S(1)} %add_convert_fusion.1.refs_0_), channel_id=1, source_target_pairs={{0,1},{1,0},{2,3},{3,2},{4,5},{5,4},{6,7},{7,6},{8,9},{9,8},{10,11... | collective-permute-start | bytes 1572872 | tf_op jit(solution)/shard_map/ppermute | solution.py:309
  89.3 9.0 %collective-permute-start.22 = (bf16[2,256,256]{2,1,0:T(8,128)(2,1)S(1)}, bf16[2,256,256]{2,1,0:T(8,128)(2,1)S(1)}, u32[]{:S(2)}, u32[]{:S(2)}) collective-permute-start(bf16[2,256,256]{2,1,0:T(8,128)(2,1)S(1)} %get-tuple-element.82), channel_id=1, source_target_pairs={{0,2},{2,4},{4,6},{6,0},{1,3},{3,5},{5,7},{7,1},{8,10},{10,12},{12... | collective-permute-start | bytes 786440 | tf_op jit(solution)/shard_map/ppermute | solution.py:314
  89.8 3.4 %collective-permute-start.15 = (bf16[4,16,640]{2,1,0:T(8,128)(2,1)S(1)}, bf16[4,16,640]{2,1,0:T(8,128)(2,1)S(1)}, u32[]{:S(2)}, u32[]{:S(2)}) collective-permute-start(bf16[4,16,640]{2,1,0:T(8,128)(2,1)S(1)} %slice_bitcast_fusion.4), channel_id=1, source_target_pairs={{0,8},{8,0},{1,9},{9,1},{2,10},{10,2},{3,11},{11,3},{4,12},{12,4},... | collective-permute-start | bytes 245768 | tf_op jit(solution)/shard_map/ppermute | solution.py:314
  89.9 12.5 %collective-permute-start.23 = (bf16[2,256,256]{2,1,0:T(8,128)(2,1)S(1)}, bf16[2,256,256]{2,1,0:T(8,128)(2,1)S(1)}, u32[]{:S(2)}, u32[]{:S(2)}) collective-permute-start(bf16[2,256,256]{2,1,0:T(8,128)(2,1)S(1)} %get-tuple-element.83), channel_id=1, source_target_pairs={{0,6},{2,0},{4,2},{6,4},{1,7},{3,1},{5,3},{7,5},{8,14},{10,8},{12,... | collective-permute-start | bytes 786440 | tf_op jit(solution)/shard_map/ppermute | solution.py:314
  92.2 12.1 %collective-permute-start.10 = (bf16[2,256,256]{2,1,0:T(8,128)(2,1)S(1)}, bf16[2,256,256]{2,1,0:T(8,128)(2,1)S(1)}, u32[]{:S(2)}, u32[]{:S(2)}) collective-permute-start(bf16[2,256,256]{2,1,0:T(8,128)(2,1)S(1)} %get-tuple-element.82), channel_id=1, source_target_pairs={{0,6},{2,0},{4,2},{6,4},{1,7},{3,1},{5,3},{7,5},{8,14},{10,8},{12,... | collective-permute-start | bytes 786440 | tf_op jit(solution)/shard_map/ppermute | solution.py:314
  93.2 11.2 %collective-permute-start.9 = (bf16[2,256,256]{2,1,0:T(8,128)(2,1)S(1)}, bf16[2,256,256]{2,1,0:T(8,128)(2,1)S(1)}, u32[]{:S(2)}, u32[]{:S(2)}) collective-permute-start(bf16[2,256,256]{2,1,0:T(8,128)(2,1)S(1)} %get-tuple-element.83), channel_id=1, source_target_pairs={{0,2},{2,4},{4,6},{6,0},{1,3},{3,5},{5,7},{7,1},{8,10},{10,12},{12... | collective-permute-start | bytes 786440 | tf_op jit(solution)/shard_map/ppermute | solution.py:314
  98.4 6.7 %collective-permute-start.25 = (bf16[2,256,256]{2,1,0:T(8,128)(2,1)S(1)}, bf16[2,256,256]{2,1,0:T(8,128)(2,1)S(1)}, u32[]{:S(2)}, u32[]{:S(2)}) collective-permute-start(bf16[2,256,256]{2,1,0:T(8,128)(2,1)S(1)} %collective-permute-done.22.refs_1_), channel_id=1, source_target_pairs={{0,1},{1,0},{2,3},{3,2},{4,5},{5,4},{6,7},{7,6},{8,9},{9,8},{10,11... | collective-permute-start | bytes 786440 | tf_op jit(solution)/shard_map/ppermute | solution.py:309
  102.4 5.5 %collective-permute-start.26 = (bf16[2,256,256]{2,1,0:T(8,128)(2,1)S(1)}, bf16[2,256,256]{2,1,0:T(8,128)(2,1)S(1)}, u32[]{:S(2)}, u32[]{:S(2)}) collective-permute-start(bf16[2,256,256]{2,1,0:T(8,128)(2,1)S(1)} %collective-permute-done.23.refs_2_), channel_id=1, source_target_pairs={{0,1},{1,0},{2,3},{3,2},{4,5},{5,4},{6,7},{7,6},{8,9},{9,8},{10,11... | collective-permute-start | bytes 786440 | tf_op jit(solution)/shard_map/ppermute | solution.py:309
  104.4 3.6 %collective-permute-start.24 = (bf16[2,256,256]{2,1,0:T(8,128)(2,1)S(1)}, bf16[2,256,256]{2,1,0:T(8,128)(2,1)S(1)}, u32[]{:S(2)}, u32[]{:S(2)}) collective-permute-start(bf16[2,256,256]{2,1,0:T(8,128)(2,1)S(1)} %collective-permute-done.9.refs_0_), channel_id=1, source_target_pairs={{0,1},{1,0},{2,3},{3,2},{4,5},{5,4},{6,7},{7,6},{8,9},{9,8},{10,11... | collective-permute-start | bytes 786440 | tf_op jit(solution)/shard_map/ppermute | solution.py:309
  105.0 5.6 %collective-permute-start.27 = (bf16[2,256,256]{2,1,0:T(8,128)(2,1)S(1)}, bf16[2,256,256]{2,1,0:T(8,128)(2,1)S(1)}, u32[]{:S(2)}, u32[]{:S(2)}) collective-permute-start(bf16[2,256,256]{2,1,0:T(8,128)(2,1)S(1)} %collective-permute-done.10.refs_3_), channel_id=1, source_target_pairs={{0,1},{1,0},{2,3},{3,2},{4,5},{5,4},{6,7},{7,6},{8,9},{9,8},{10,11... | collective-permute-start | bytes 786440 | tf_op jit(solution)/shard_map/ppermute | solution.py:309
  105.1 10.4 %collective-permute-start.17 = (bf16[2,256,256]{2,1,0:T(8,128)(2,1)S(1)}, bf16[2,256,256]{2,1,0:T(8,128)(2,1)S(1)}, u32[]{:S(2)}, u32[]{:S(2)}) collective-permute-start(bf16[2,256,256]{2,1,0:T(8,128)(2,1)S(1)} %collective-permute-done.9.refs_0_), channel_id=1, source_target_pairs={{0,2},{2,4},{4,6},{6,0},{1,3},{3,5},{5,7},{7,1},{8,10},{10,12},{12... | collective-permute-start | bytes 786440 | tf_op jit(solution)/shard_map/ppermute | solution.py:314
  105.1 10.4 %collective-permute-start.18 = (bf16[2,256,256]{2,1,0:T(8,128)(2,1)S(1)}, bf16[2,256,256]{2,1,0:T(8,128)(2,1)S(1)}, u32[]{:S(2)}, u32[]{:S(2)}) collective-permute-start(bf16[2,256,256]{2,1,0:T(8,128)(2,1)S(1)} %collective-permute-done.10.refs_3_), channel_id=1, source_target_pairs={{0,6},{2,0},{4,2},{6,4},{1,7},{3,1},{5,3},{7,5},{8,14},{10,8},{12,... | collective-permute-start | bytes 786440 | tf_op jit(solution)/shard_map/ppermute | solution.py:314
  107.9 6.4 %collective-permute-start.19 = (bf16[16,640]{1,0:T(8,128)(2,1)S(1)}, bf16[16,640]{1,0:T(8,128)(2,1)S(1)}, u32[]{:S(2)}, u32[]{:S(2)}) collective-permute-start(bf16[16,640]{1,0:T(8,128)(2,1)S(1)} %get-tuple-element.86), channel_id=1, source_target_pairs={{0,2},{2,4},{4,6},{6,0},{1,3},{3,5},{5,7},{7,1},{8,10},{10,12},{12... | collective-permute-start | bytes 61448 | tf_op jit(solution)/shard_map/ppermute | solution.py:314
  108.0 7.5 %collective-permute-start.20 = (bf16[16,640]{1,0:T(8,128)(2,1)S(1)}, bf16[16,640]{1,0:T(8,128)(2,1)S(1)}, u32[]{:S(2)}, u32[]{:S(2)}) collective-permute-start(bf16[16,640]{1,0:T(8,128)(2,1)S(1)} %get-tuple-element.85), channel_id=1, source_target_pairs={{0,4},{2,6},{4,0},{6,2},{1,5},{3,7},{5,1},{7,3},{8,12},{10,14},{12... | collective-permute-start | bytes 61448 | tf_op jit(solution)/shard_map/ppermute | solution.py:314
  110.5 4.9 %collective-permute-start.21 = (bf16[16,640]{1,0:T(8,128)(2,1)S(1)}, bf16[16,640]{1,0:T(8,128)(2,1)S(1)}, u32[]{:S(2)}, u32[]{:S(2)}) collective-permute-start(bf16[16,640]{1,0:T(8,128)(2,1)S(1)} %get-tuple-element.84), channel_id=1, source_target_pairs={{0,6},{2,0},{4,2},{6,4},{1,7},{3,1},{5,3},{7,5},{8,14},{10,8},{12,... | collective-permute-start | bytes 61448 | tf_op jit(solution)/shard_map/ppermute | solution.py:314
  115.5 2.9 %collective-permute-start.28 = (bf16[2,256,256]{2,1,0:T(8,128)(2,1)S(1)}, bf16[2,256,256]{2,1,0:T(8,128)(2,1)S(1)}, u32[]{:S(2)}, u32[]{:S(2)}) collective-permute-start(bf16[2,256,256]{2,1,0:T(8,128)(2,1)S(1)} %collective-permute-done.17.refs_0_), channel_id=1, source_target_pairs={{0,1},{1,0},{2,3},{3,2},{4,5},{5,4},{6,7},{7,6},{8,9},{9,8},{10,11... | collective-permute-start | bytes 786440 | tf_op jit(solution)/shard_map/ppermute | solution.py:309
  117.2 1.5 %collective-permute-start.29 = (bf16[2,256,256]{2,1,0:T(8,128)(2,1)S(1)}, bf16[2,256,256]{2,1,0:T(8,128)(2,1)S(1)}, u32[]{:S(2)}, u32[]{:S(2)}) collective-permute-start(bf16[2,256,256]{2,1,0:T(8,128)(2,1)S(1)} %collective-permute-done.18.refs_1_), channel_id=1, source_target_pairs={{0,1},{1,0},{2,3},{3,2},{4,5},{5,4},{6,7},{7,6},{8,9},{9,8},{10,11... | collective-permute-start | bytes 786440 | tf_op jit(solution)/shard_map/ppermute | solution.py:309

commit v6 on v5

--- a/solution.py
+++ b/solution.py
@@ -138,8 +138,8 @@
             pieces.append(jnp.transpose(turned_grad[:, at]))
         back_ref[slot(block), :, PAIR * VHEAD:] = jnp.concatenate(pieces, axis=1).astype(bf16)
 
-    for low_block in range(blocks // 2):
-        duo = (blocks - 1 - low_block, low_block)
+    for upper_block in range(blocks - 1, 0, -4):
+        duo = tuple(range(upper_block, upper_block - 4, -1))
         scores = [scores_of(block) for block in duo]
         soft = [softmax_of(score) for score in scores]
         done = [context_of(block, *soft[n]) for n, block in enumerate(duo)]

time: 121 us -> 119 us (0.983)
  Pallas kernels: 29.2 us -> 26.7 us
    pallas_call x1, Pallas kernels: 18.1 us -> 15.5 us  [attention(): pl.pallas_call(attention_kernel, grid_spec=pltpu.PrefetchScalarGridSpec(n...]
where the time goes in v6:
time: 119 us; the launch traced here: 118 us
  starting transfers between devices  50.7 us (43%)
  waiting for transfers between devices  34.5 us (29%)
  Pallas kernels  26.7 us (22%)
  local copies, waits for them, and re-layouts  4.09 us (3%)
  other arithmetic  1.28 us (1%)
    ppermute x21, starting transfers between devices, shifted(): lax.ppermute(value, axis, [(i, (i + steps) % count) for i in range(count)])  27.7 us
    ppermute x21, waiting for transfers between devices, shifted(): lax.ppermute(value, axis, [(i, (i + steps) % count) for i in range(count)])  17.3 us
    all_to_all x3, starting transfers between devices, exchanged(): return lax.all_to_all(value, axes, 0, 0, tiled=True)  17.1 us
    pallas_call x1, Pallas kernels, attention(): pl.pallas_call(attention_kernel, grid_spec=pltpu.PrefetchScalarGridSpec(n...  15.5 us
    all_to_all x3, waiting for transfers between devices, exchanged(): return lax.all_to_all(value, axes, 0, 0, tiled=True)  14.8 us
    pallas_call x3, Pallas kernels, unfold(): pl.pallas_call(kernel, grid_spec=pltpu.PrefetchScalarGridSpec(num_scalar_...  6.57 us
    ppermute x9, starting transfers between devices, swapped(): return lax.ppermute(value, 'core', [(0, 1), (1, 0)])  5.92 us
    pallas_call x1, Pallas kernels, join(): pl.pallas_call(kernel, out_shape=[jax.ShapeDtypeStruct((rows, slots * val...  2.5 us
  transfers between devices with their start and end apart: 33, of which 13 were waited for; matrix products, arithmetic and copies ran while one was open for 4% of the time, Pallas kernels for 8%

profile of v6, /device:TPU:1, one launch (start us, length us, event | category | flops | bytes accessed | tf_op | source)
XLA Modules:
  0.0 118.3 jit_solution(7534080341193028077)
XLA Ops:
  0.6 2.5 %collective-permute-start = (bf16[16,576]{1,0:T(8,128)(2,1)}, bf16[16,576]{1,0:T(8,128)(2,1)S(1)}, u32[]{:S(2)}, u32[]{:S(2)}) collective-permute-start(bf16[16,576]{1,0:T(8,128)(2,1)} %param.7), channel_id=1, source_target_pairs={{0,16},{16,32},{32,48},{48,0},{1,17},{17,33},{33,49},{49,1},{2,18}... | collective-permute-start | bytes 55304 | tf_op jit(solution)/shard_map/ppermute | solution.py:314
  3.2 3.3 %collective-permute-start.1 = (bf16[16,576]{1,0:T(8,128)(2,1)}, bf16[16,576]{1,0:T(8,128)(2,1)S(1)}, u32[]{:S(2)}, u32[]{:S(2)}) collective-permute-start(bf16[16,576]{1,0:T(8,128)(2,1)} %param.7), channel_id=1, source_target_pairs={{0,32},{16,48},{32,0},{48,16},{1,33},{17,49},{33,1},{49,17},{2,34}... | collective-permute-start | bytes 55304 | tf_op jit(solution)/shard_map/ppermute | solution.py:314
  6.5 0.7 collective-permute-start.2
  7.2 1.3 %copy.17 = bf16[128,2048]{0,1:T(8,128)(2,1)S(1)} copy(bf16[128,2048]{1,0:T(8,128)(2,1)} %param.10) | data formatting | bytes 1048576 | tf_op args[4]
  8.5 1.0 copy.18
  9.6 6.5 %all-to-all-start = ((bf16[8,128,256]{2,1,0:T(8,128)(2,1)}), bf16[8,128,256]{2,1,0:T(8,128)(2,1)S(1)}, u32[]{:S(2)}, u32[]{:S(2)}) async-start(bf16[8,128,256]{2,1,0:T(8,128)(2,1)} %bitcast.9), calls=%async_computation | async-start | bytes 1048576 | tf_op jit(solution)/shard_map/all_to_all | solution.py:318
  16.0 1.3 %collective-permute-start.3 = (bf16[4,16,576]{2,1,0:T(8,128)(2,1)S(1)}, bf16[4,16,576]{2,1,0:T(8,128)(2,1)S(1)}, u32[]{:S(2)}, u32[]{:S(2)}) collective-permute-start(bf16[4,16,576]{2,1,0:T(8,128)(2,1)S(1)} %pad_maximum_fusion.2), channel_id=1, source_target_pairs={{0,8},{8,0},{1,9},{9,1},{2,10},{10,2},{3,11},{11,3},{4,12},{12,4},... | collective-permute-start | bytes 221192 | tf_op jit(solution)/shard_map/ppermute | solution.py:314
  17.3 2.1 %pack.1 = bf16[64,16,384]{2,1,0:T(8,128)(2,1)} custom-call(bf16[16,24576]{1,0:T(8,128)(2,1)} %query_ref.1), custom_call_target="tpu_custom_call" | custom-call | tf_op jit(solution)/shard_map/pack/pallas_call | solution.py:301
  19.4 0.7 collective-permute-done.3
  20.2 1.0 collective-permute-start.4
  21.2 2.4 %collective-permute-start.5 = (bf16[128,576]{1,0:T(8,128)(2,1)S(1)}, bf16[128,576]{1,0:T(8,128)(2,1)S(1)}, u32[]{:S(2)}, u32[]{:S(2)}) collective-permute-start(bf16[128,576]{1,0:T(8,128)(2,1)S(1)} %bitcast.47), channel_id=1, source_target_pairs={{0,4},{2,6},{4,0},{6,2},{1,5},{3,7},{5,1},{7,3},{8,12},{10,14},{12... | collective-permute-start | bytes 442376 | tf_op jit(solution)/shard_map/ppermute | solution.py:314
  23.6 1.2 collective-permute-start.6
  24.8 1.0 all-to-all-done.grad_ref
  25.7 6.3 %all-to-all-start.1 = ((bf16[64,16,384]{2,1,0:T(8,128)(2,1)}), bf16[64,16,384]{2,1,0:T(8,128)(2,1)S(1)}, u32[]{:S(2)}, u32[]{:S(2)}) async-start(bf16[64,16,384]{2,1,0:T(8,128)(2,1)} %pack.1), calls=%async_computation.1 | async-start | bytes 1572864 | tf_op jit(solution)/shard_map/all_to_all | solution.py:318
  32.1 0.5 collective-permute-done.5
  33.1 1.1 collective-permute-start.7
  34.3 1.6 %collective-permute-done.7 = bf16[4,128,576]{1,2,0:T(8,128)(2,1)S(1)} collective-permute-done((bf16[4,128,576]{1,2,0:T(8,128)(2,1)S(1)}, bf16[4,128,576]{1,2,0:T(8,128)(2,1)S(1)}, u32[]{:S(2)}, u32[]{:S(2)}) %collective-permute-start.7) | collective-permute-done | bytes 589856 | tf_op jit(solution)/shard_map/ppermute | solution.py:309
  36.1 11.1 %all-to-all-done.1 = bf16[64,16,384]{2,1,0:T(8,128)(2,1)S(1)} async-done(((bf16[64,16,384]{2,1,0:T(8,128)(2,1)}), bf16[64,16,384]{2,1,0:T(8,128)(2,1)S(1)}, u32[]{:S(2)}, u32[]{:S(2)}) %all-to-all-start.1) | async-done | bytes 786464 | tf_op jit(solution)/shard_map/all_to_all | solution.py:318
  47.2 1.0 copy-done.1
  48.3 15.5 %attention.1 = (bf16[8,128,640]{2,1,0:T(8,128)(2,1)}, bf16[2,512,256]{2,1,0:T(8,128)(2,1)S(1)}, bf16[4,2,4,16,640]{4,3,2,1,0:T(8,128)(2,1)S(1)}, bf16[4,2,4,16,640]{4,3,2,1,0:T(8,128)(2,1)}) custom-call(s32[4]{0:T(128)S(1)} %pad_add_fusion.place, s32[1,8]{1,0:T(1,128)S(1)} %copy-done.2, bf16[1024,384]{1,0:T(8,128)(2,1)S(1)} %bitcast.44, ...), custom_call_target="tpu_custom_call" | custom-call | flops 8999999488 | bytes 15000000 | tf_op jit(solution)/shard_map/attention/pallas_call | solution.py:182
  63.8 0.4 collective-permute-start.11
  64.2 4.3 %all-to-all-start.2 = ((bf16[8,128,640]{2,1,0:T(8,128)(2,1)}), bf16[8,128,640]{2,1,0:T(8,128)(2,1)}, u32[]{:S(2)}, u32[]{:S(2)}) async-start(bf16[8,128,640]{2,1,0:T(8,128)(2,1)} %get-tuple-element.49), calls=%async_computation.2 | async-start | bytes 2621440 | tf_op jit(solution)/shard_map/all_to_all | solution.py:318
  68.5 2.6 %collective-permute-start.8 = (bf16[2,512,256]{2,1,0:T(8,128)(2,1)S(1)}, bf16[2,512,256]{2,1,0:T(8,128)(2,1)S(1)}, u32[]{:S(2)}, u32[]{:S(2)}) collective-permute-start(bf16[2,512,256]{2,1,0:T(8,128)(2,1)S(1)} %get-tuple-element.48), channel_id=1, source_target_pairs={{0,64},{64,0},{1,65},{65,1},{2,66},{66,2},{3,67},{67,3},{4,68},{68... | collective-permute-start | bytes 1572872 | tf_op jit(solution)/shard_map/ppermute | solution.py:314
  71.7 1.8 %collective-permute-start.13 = (bf16[2,4,16,640]{3,2,1,0:T(8,128)(2,1)S(1)}, bf16[2,4,16,640]{3,2,1,0:T(8,128)(2,1)S(1)}, u32[]{:S(2)}, u32[]{:S(2)}) collective-permute-start(bf16[2,4,16,640]{3,2,1,0:T(8,128)(2,1)S(1)} %get-tuple-element.81), channel_id=1, source_target_pairs={{0,32},{16,48},{32,0},{48,16},{1,33},{17,49},{33,1},{49,17},{2,34}... | collective-permute-start | bytes 491528 | tf_op jit(solution)/shard_map/ppermute | solution.py:314
  73.5 0.7 collective-permute-start.14
  74.2 9.2 %collective-permute-done.8 = bf16[2,512,256]{2,1,0:T(8,128)(2,1)S(1)} collective-permute-done((bf16[2,512,256]{2,1,0:T(8,128)(2,1)S(1)}, bf16[2,512,256]{2,1,0:T(8,128)(2,1)S(1)}, u32[]{:S(2)}, u32[]{:S(2)}) %collective-permute-start.8) | collective-permute-done | bytes 524320 | tf_op jit(solution)/shard_map/ppermute | solution.py:314
  83.7 2.7 %all-to-all-done.2.back_ref = bf16[8,128,640]{2,1,0:T(8,128)(2,1)} async-done(((bf16[8,128,640]{2,1,0:T(8,128)(2,1)}), bf16[8,128,640]{2,1,0:T(8,128)(2,1)}, u32[]{:S(2)}, u32[]{:S(2)}) %all-to-all-start.2) | async-done | bytes 1310752 | tf_op jit(solution)/shard_map/all_to_all | solution.py:318
  86.4 0.4 collective-permute-start.16
  86.8 0.5 collective-permute-start.22
  87.4 2.3 %collective-permute-start.23 = (bf16[2,256,256]{2,1,0:T(8,128)(2,1)S(1)}, bf16[2,256,256]{2,1,0:T(8,128)(2,1)S(1)}, u32[]{:S(2)}, u32[]{:S(2)}) collective-permute-start(bf16[2,256,256]{2,1,0:T(8,128)(2,1)S(1)} %get-tuple-element.83), channel_id=1, source_target_pairs={{0,6},{2,0},{4,2},{6,4},{1,7},{3,1},{5,3},{7,5},{8,14},{10,8},{12,... | collective-permute-start | bytes 786440 | tf_op jit(solution)/shard_map/ppermute | solution.py:314
  90.0 0.7 collective-permute-done.15
  90.7 0.5 collective-permute-start.9
  91.2 4.7 %collective-permute-done.22.refs_1_ = bf16[2,256,256]{2,1,0:T(8,128)(2,1)S(1)} collective-permute-done((bf16[2,256,256]{2,1,0:T(8,128)(2,1)S(1)}, bf16[2,256,256]{2,1,0:T(8,128)(2,1)S(1)}, u32[]{:S(2)}, u32[]{:S(2)}) %collective-permute-start.22) | collective-permute-done | bytes 262176 | tf_op jit(solution)/shard_map/ppermute | solution.py:314
  95.8 1.5 %collective-permute-start.25 = (bf16[2,256,256]{2,1,0:T(8,128)(2,1)S(1)}, bf16[2,256,256]{2,1,0:T(8,128)(2,1)S(1)}, u32[]{:S(2)}, u32[]{:S(2)}) collective-permute-start(bf16[2,256,256]{2,1,0:T(8,128)(2,1)S(1)} %collective-permute-done.22.refs_1_), channel_id=1, source_target_pairs={{0,1},{1,0},{2,3},{3,2},{4,5},{5,4},{6,7},{7,6},{8,9},{9,8},{10,11... | collective-permute-start | bytes 786440 | tf_op jit(solution)/shard_map/ppermute | solution.py:309
  97.4 2.5 %join.1 = (bf16[128,2048]{1,0:T(8,128)(2,1)}, bf16[128,3072]{1,0:T(8,128)(2,1)}) custom-call(bf16[8,128,640]{2,1,0:T(8,128)(2,1)} %all-to-all-done.2.back_ref), custom_call_target="tpu_custom_call" | custom-call | tf_op jit(solution)/shard_map/join/pallas_call | solution.py:227
  99.9 1.9 %unfold.3 = (f32[16,512,128]{2,1,0:T(8,128)}, f32[16,512,128]{2,1,0:T(8,128)}) custom-call(s32[4]{0:T(128)S(1)} %pad_add_fusion.place, bf16[2,512,256]{2,1,0:T(8,128)(2,1)S(1)} %add_convert_fusion.1.refs_0_, bf16[2,512,256]{2,1,0:T(8,128)(2,1)S(1)} %collective-permute-done.16.refs_1_), custom_call_target="tpu_custom_call" | custom-call | bytes 4000000 | tf_op jit(solution)/shard_map/unfold/pallas_call | solution.py:271
  101.9 0.6 collective-permute-start.24
  102.5 2.8 %collective-permute-start.18 = (bf16[2,256,256]{2,1,0:T(8,128)(2,1)S(1)}, bf16[2,256,256]{2,1,0:T(8,128)(2,1)S(1)}, u32[]{:S(2)}, u32[]{:S(2)}) collective-permute-start(bf16[2,256,256]{2,1,0:T(8,128)(2,1)S(1)} %collective-permute-done.10.refs_3_), channel_id=1, source_target_pairs={{0,6},{2,0},{4,2},{6,4},{1,7},{3,1},{5,3},{7,5},{8,14},{10,8},{12,... | collective-permute-start | bytes 786440 | tf_op jit(solution)/shard_map/ppermute | solution.py:314
  105.5 2.6 %collective-permute-start.20 = (bf16[16,640]{1,0:T(8,128)(2,1)S(1)}, bf16[16,640]{1,0:T(8,128)(2,1)S(1)}, u32[]{:S(2)}, u32[]{:S(2)}) collective-permute-start(bf16[16,640]{1,0:T(8,128)(2,1)S(1)} %get-tuple-element.85), channel_id=1, source_target_pairs={{0,4},{2,6},{4,0},{6,2},{1,5},{3,7},{5,1},{7,3},{8,12},{10,14},{12... | collective-permute-start | bytes 61448 | tf_op jit(solution)/shard_map/ppermute | solution.py:314
  108.0 0.6 collective-permute-start.21
  108.6 2.7 %unfold.4 = (f32[16,512,128]{2,1,0:T(8,128)}, f32[16,512,128]{2,1,0:T(8,128)}) custom-call(s32[4]{0:T(128)S(1)} %pad_add_fusion.place, bf16[2,256,256]{2,1,0:T(8,128)(2,1)S(1)} %collective-permute-done.9.refs_0_, bf16[2,256,256]{2,1,0:T(8,128)(2,1)S(1)} %collective-permute-done.22.refs_1_, ...), custom_call_target="tpu_custom_call", output_to_operand_aliasing={{0}: (9, {}), {1}: (10, {})} | custom-call | bytes 4000000 | tf_op jit(solution)/shard_map/unfold/pallas_call | solution.py:271
  111.3 0.4 collective-permute-done.19
  111.8 1.1 collective-permute-done.20
  113.0 1.7 %collective-permute-start.28 = (bf16[2,256,256]{2,1,0:T(8,128)(2,1)S(1)}, bf16[2,256,256]{2,1,0:T(8,128)(2,1)S(1)}, u32[]{:S(2)}, u32[]{:S(2)}) collective-permute-start(bf16[2,256,256]{2,1,0:T(8,128)(2,1)S(1)} %collective-permute-done.17.refs_0_), channel_id=1, source_target_pairs={{0,1},{1,0},{2,3},{3,2},{4,5},{5,4},{6,7},{7,6},{8,9},{9,8},{10,11... | collective-permute-start | bytes 786440 | tf_op jit(solution)/shard_map/ppermute | solution.py:309
  114.8 0.6 convert_add_fusion.2
  115.4 0.4 collective-permute-done.28.refs_2_
  115.8 0.4 collective-permute-done.29.refs_3_
  116.2 1.9 %unfold.5 = (f32[16,512,128]{2,1,0:T(8,128)}, f32[16,512,128]{2,1,0:T(8,128)}) custom-call(s32[4]{0:T(128)S(1)} %pad_add_fusion.place, bf16[2,256,256]{2,1,0:T(8,128)(2,1)S(1)} %collective-permute-done.17.refs_0_, bf16[2,256,256]{2,1,0:T(8,128)(2,1)S(1)} %collective-permute-done.18.refs_1_, ...), custom_call_target="tpu_custom_call", output_to_operand_aliasing={{0}: (5, {}), {1}: (6, {})} | custom-call | bytes 4000000 | tf_op jit(solution)/shard_map/unfold/pallas_call | solution.py:271
  (49 shorter events, 2.4 us)
Async XLA Ops:
  0.6 8.9 %copy-start.3 = (bf16[16,576]{1,0:T(8,128)(2,1)S(1)}, bf16[16,576]{1,0:T(8,128)(2,1)}, u32[]{:S(2)}) copy-start(bf16[16,576]{1,0:T(8,128)(2,1)} %param.7) | copy-start | bytes 55300
  0.6 8.9 %collective-permute-start = (bf16[16,576]{1,0:T(8,128)(2,1)}, bf16[16,576]{1,0:T(8,128)(2,1)S(1)}, u32[]{:S(2)}, u32[]{:S(2)}) collective-permute-start(bf16[16,576]{1,0:T(8,128)(2,1)} %param.7), channel_id=1, source_target_pairs={{0,16},{16,32},{32,48},{48,0},{1,17},{17,33},{33,49},{49,1},{2,18}... | collective-permute-start | bytes 55304 | tf_op jit(solution)/shard_map/ppermute | solution.py:314
  3.2 6.4 %collective-permute-start.1 = (bf16[16,576]{1,0:T(8,128)(2,1)}, bf16[16,576]{1,0:T(8,128)(2,1)S(1)}, u32[]{:S(2)}, u32[]{:S(2)}) collective-permute-start(bf16[16,576]{1,0:T(8,128)(2,1)} %param.7), channel_id=1, source_target_pairs={{0,32},{16,48},{32,0},{48,16},{1,33},{17,49},{33,1},{49,17},{2,34}... | collective-permute-start | bytes 55304 | tf_op jit(solution)/shard_map/ppermute | solution.py:314
  6.5 3.1 %collective-permute-start.2 = (bf16[16,576]{1,0:T(8,128)(2,1)}, bf16[16,576]{1,0:T(8,128)(2,1)S(1)}, u32[]{:S(2)}, u32[]{:S(2)}) collective-permute-start(bf16[16,576]{1,0:T(8,128)(2,1)} %param.7), channel_id=1, source_target_pairs={{0,48},{16,0},{32,16},{48,32},{1,49},{17,1},{33,17},{49,33},{2,50}... | collective-permute-start | bytes 55304 | tf_op jit(solution)/shard_map/ppermute | solution.py:314
  9.6 16.1 %all-to-all-start = ((bf16[8,128,256]{2,1,0:T(8,128)(2,1)}), bf16[8,128,256]{2,1,0:T(8,128)(2,1)S(1)}, u32[]{:S(2)}, u32[]{:S(2)}) async-start(bf16[8,128,256]{2,1,0:T(8,128)(2,1)} %bitcast.9), calls=%async_computation | async-start | bytes 1048576 | tf_op jit(solution)/shard_map/all_to_all | solution.py:318
  16.0 4.1 %collective-permute-start.3 = (bf16[4,16,576]{2,1,0:T(8,128)(2,1)S(1)}, bf16[4,16,576]{2,1,0:T(8,128)(2,1)S(1)}, u32[]{:S(2)}, u32[]{:S(2)}) collective-permute-start(bf16[4,16,576]{2,1,0:T(8,128)(2,1)S(1)} %pad_maximum_fusion.2), channel_id=1, source_target_pairs={{0,8},{8,0},{1,9},{9,1},{2,10},{10,2},{3,11},{11,3},{4,12},{12,4},... | collective-permute-start | bytes 221192 | tf_op jit(solution)/shard_map/ppermute | solution.py:314
  20.2 11.9 %collective-permute-start.4 = (bf16[128,576]{1,0:T(8,128)(2,1)S(1)}, bf16[128,576]{1,0:T(8,128)(2,1)S(1)}, u32[]{:S(2)}, u32[]{:S(2)}) collective-permute-start(bf16[128,576]{1,0:T(8,128)(2,1)S(1)} %bitcast.46), channel_id=1, source_target_pairs={{0,2},{2,4},{4,6},{6,0},{1,3},{3,5},{5,7},{7,1},{8,10},{10,12},{12... | collective-permute-start | bytes 442376 | tf_op jit(solution)/shard_map/ppermute | solution.py:314
  21.2 11.4 %collective-permute-start.5 = (bf16[128,576]{1,0:T(8,128)(2,1)S(1)}, bf16[128,576]{1,0:T(8,128)(2,1)S(1)}, u32[]{:S(2)}, u32[]{:S(2)}) collective-permute-start(bf16[128,576]{1,0:T(8,128)(2,1)S(1)} %bitcast.47), channel_id=1, source_target_pairs={{0,4},{2,6},{4,0},{6,2},{1,5},{3,7},{5,1},{7,3},{8,12},{10,14},{12... | collective-permute-start | bytes 442376 | tf_op jit(solution)/shard_map/ppermute | solution.py:314
  23.6 9.0 %collective-permute-start.6 = (bf16[128,576]{1,0:T(8,128)(2,1)S(1)}, bf16[128,576]{1,0:T(8,128)(2,1)S(1)}, u32[]{:S(2)}, u32[]{:S(2)}) collective-permute-start(bf16[128,576]{1,0:T(8,128)(2,1)S(1)} %bitcast.48), channel_id=1, source_target_pairs={{0,6},{2,0},{4,2},{6,4},{1,7},{3,1},{5,3},{7,5},{8,14},{10,8},{12,... | collective-permute-start | bytes 442376 | tf_op jit(solution)/shard_map/ppermute | solution.py:314
  25.7 6.9 %copy-start = (bf16[8,128,256]{2,1,0:T(8,128)(2,1)}, bf16[8,128,256]{2,1,0:T(8,128)(2,1)S(1)}, u32[]{:S(2)}) copy-start(bf16[8,128,256]{2,1,0:T(8,128)(2,1)S(1)} %all-to-all-done.grad_ref) | copy-start | bytes 1572868
  25.7 21.5 %all-to-all-start.1 = ((bf16[64,16,384]{2,1,0:T(8,128)(2,1)}), bf16[64,16,384]{2,1,0:T(8,128)(2,1)S(1)}, u32[]{:S(2)}, u32[]{:S(2)}) async-start(bf16[64,16,384]{2,1,0:T(8,128)(2,1)} %pack.1), calls=%async_computation.1 | async-start | bytes 1572864 | tf_op jit(solution)/shard_map/all_to_all | solution.py:318
  32.1 15.1 %copy-start.2 = (s32[1,8]{1,0:T(1,128)S(1)}, s32[1,8]{1,0:T(1,128)}, u32[]{:S(2)}) copy-start(s32[1,8]{1,0:T(1,128)} %docs.1) | copy-start | bytes 100
  33.1 2.8 %collective-permute-start.7 = (bf16[4,128,576]{1,2,0:T(8,128)(2,1)S(1)}, bf16[4,128,576]{1,2,0:T(8,128)(2,1)S(1)}, u32[]{:S(2)}, u32[]{:S(2)}) collective-permute-start(bf16[4,128,576]{1,2,0:T(8,128)(2,1)S(1)} %copy.19), channel_id=1, source_target_pairs={{0,1},{1,0},{2,3},{3,2},{4,5},{5,4},{6,7},{7,6},{8,9},{9,8},{10,11... | collective-permute-start | bytes 1769480 | tf_op jit(solution)/shard_map/ppermute | solution.py:309
  47.2 1.0 copy-start.1
  63.8 7.3 %collective-permute-start.11 = (bf16[4,2,4,16,640]{4,3,2,1,0:T(8,128)(2,1)}, bf16[4,2,4,16,640]{4,3,2,1,0:T(8,128)(2,1)S(1)}, u32[]{:S(2)}, u32[]{:S(2)}) collective-permute-start(bf16[4,2,4,16,640]{4,3,2,1,0:T(8,128)(2,1)} %get-tuple-element.52), channel_id=1, source_target_pairs={{0,1},{1,0},{2,3},{3,2},{4,5},{5,4},{6,7},{7,6},{8,9},{9,8},{10,11... | collective-permute-start | bytes 1966088 | tf_op jit(solution)/shard_map/ppermute | solution.py:309
  64.2 22.2 %all-to-all-start.2 = ((bf16[8,128,640]{2,1,0:T(8,128)(2,1)}), bf16[8,128,640]{2,1,0:T(8,128)(2,1)}, u32[]{:S(2)}, u32[]{:S(2)}) async-start(bf16[8,128,640]{2,1,0:T(8,128)(2,1)} %get-tuple-element.49), calls=%async_computation.2 | async-start | bytes 2621440 | tf_op jit(solution)/shard_map/all_to_all | solution.py:318
  68.5 14.9 %collective-permute-start.8 = (bf16[2,512,256]{2,1,0:T(8,128)(2,1)S(1)}, bf16[2,512,256]{2,1,0:T(8,128)(2,1)S(1)}, u32[]{:S(2)}, u32[]{:S(2)}) collective-permute-start(bf16[2,512,256]{2,1,0:T(8,128)(2,1)S(1)} %get-tuple-element.48), channel_id=1, source_target_pairs={{0,64},{64,0},{1,65},{65,1},{2,66},{66,2},{3,67},{67,3},{4,68},{68... | collective-permute-start | bytes 1572872 | tf_op jit(solution)/shard_map/ppermute | solution.py:314
  71.4 12.2 %collective-permute-start.12 = (bf16[2,4,16,640]{3,2,1,0:T(8,128)(2,1)S(1)}, bf16[2,4,16,640]{3,2,1,0:T(8,128)(2,1)S(1)}, u32[]{:S(2)}, u32[]{:S(2)}) collective-permute-start(bf16[2,4,16,640]{3,2,1,0:T(8,128)(2,1)S(1)} %get-tuple-element.79), channel_id=1, source_target_pairs={{0,16},{16,32},{32,48},{48,0},{1,17},{17,33},{33,49},{49,1},{2,18}... | collective-permute-start | bytes 491528 | tf_op jit(solution)/shard_map/ppermute | solution.py:314
  71.7 11.8 %collective-permute-start.13 = (bf16[2,4,16,640]{3,2,1,0:T(8,128)(2,1)S(1)}, bf16[2,4,16,640]{3,2,1,0:T(8,128)(2,1)S(1)}, u32[]{:S(2)}, u32[]{:S(2)}) collective-permute-start(bf16[2,4,16,640]{3,2,1,0:T(8,128)(2,1)S(1)} %get-tuple-element.81), channel_id=1, source_target_pairs={{0,32},{16,48},{32,0},{48,16},{1,33},{17,49},{33,1},{49,17},{2,34}... | collective-permute-start | bytes 491528 | tf_op jit(solution)/shard_map/ppermute | solution.py:314
  73.5 10.1 %collective-permute-start.14 = (bf16[2,4,16,640]{3,2,1,0:T(8,128)(2,1)S(1)}, bf16[2,4,16,640]{3,2,1,0:T(8,128)(2,1)S(1)}, u32[]{:S(2)}, u32[]{:S(2)}) collective-permute-start(bf16[2,4,16,640]{3,2,1,0:T(8,128)(2,1)S(1)} %get-tuple-element.80), channel_id=1, source_target_pairs={{0,48},{16,0},{32,16},{48,32},{1,49},{17,1},{33,17},{49,33},{2,50}... | collective-permute-start | bytes 491528 | tf_op jit(solution)/shard_map/ppermute | solution.py:314
  86.4 13.5 %collective-permute-start.16 = (bf16[2,512,256]{2,1,0:T(8,128)(2,1)S(1)}, bf16[2,512,256]{2,1,0:T(8,128)(2,1)S(1)}, u32[]{:S(2)}, u32[]{:S(2)}) collective-permute-start(bf16[2,512,256]{2,1,0:T(8,128)(2,1)S(1)} %add_convert_fusion.1.refs_0_), channel_id=1, source_target_pairs={{0,1},{1,0},{2,3},{3,2},{4,5},{5,4},{6,7},{7,6},{8,9},{9,8},{10,11... | collective-permute-start | bytes 1572872 | tf_op jit(solution)/shard_map/ppermute | solution.py:309
  86.8 9.0 %collective-permute-start.22 = (bf16[2,256,256]{2,1,0:T(8,128)(2,1)S(1)}, bf16[2,256,256]{2,1,0:T(8,128)(2,1)S(1)}, u32[]{:S(2)}, u32[]{:S(2)}) collective-permute-start(bf16[2,256,256]{2,1,0:T(8,128)(2,1)S(1)} %get-tuple-element.82), channel_id=1, source_target_pairs={{0,2},{2,4},{4,6},{6,0},{1,3},{3,5},{5,7},{7,1},{8,10},{10,12},{12... | collective-permute-start | bytes 786440 | tf_op jit(solution)/shard_map/ppermute | solution.py:314
  87.3 3.4 %collective-permute-start.15 = (bf16[4,16,640]{2,1,0:T(8,128)(2,1)S(1)}, bf16[4,16,640]{2,1,0:T(8,128)(2,1)S(1)}, u32[]{:S(2)}, u32[]{:S(2)}) collective-permute-start(bf16[4,16,640]{2,1,0:T(8,128)(2,1)S(1)} %slice_bitcast_fusion.4), channel_id=1, source_target_pairs={{0,8},{8,0},{1,9},{9,1},{2,10},{10,2},{3,11},{11,3},{4,12},{12,4},... | collective-permute-start | bytes 245768 | tf_op jit(solution)/shard_map/ppermute | solution.py:314
  87.4 12.5 %collective-permute-start.23 = (bf16[2,256,256]{2,1,0:T(8,128)(2,1)S(1)}, bf16[2,256,256]{2,1,0:T(8,128)(2,1)S(1)}, u32[]{:S(2)}, u32[]{:S(2)}) collective-permute-start(bf16[2,256,256]{2,1,0:T(8,128)(2,1)S(1)} %get-tuple-element.83), channel_id=1, source_target_pairs={{0,6},{2,0},{4,2},{6,4},{1,7},{3,1},{5,3},{7,5},{8,14},{10,8},{12,... | collective-permute-start | bytes 786440 | tf_op jit(solution)/shard_map/ppermute | solution.py:314
  89.7 12.1 %collective-permute-start.10 = (bf16[2,256,256]{2,1,0:T(8,128)(2,1)S(1)}, bf16[2,256,256]{2,1,0:T(8,128)(2,1)S(1)}, u32[]{:S(2)}, u32[]{:S(2)}) collective-permute-start(bf16[2,256,256]{2,1,0:T(8,128)(2,1)S(1)} %get-tuple-element.82), channel_id=1, source_target_pairs={{0,6},{2,0},{4,2},{6,4},{1,7},{3,1},{5,3},{7,5},{8,14},{10,8},{12,... | collective-permute-start | bytes 786440 | tf_op jit(solution)/shard_map/ppermute | solution.py:314
  90.7 11.2 %collective-permute-start.9 = (bf16[2,256,256]{2,1,0:T(8,128)(2,1)S(1)}, bf16[2,256,256]{2,1,0:T(8,128)(2,1)S(1)}, u32[]{:S(2)}, u32[]{:S(2)}) collective-permute-start(bf16[2,256,256]{2,1,0:T(8,128)(2,1)S(1)} %get-tuple-element.83), channel_id=1, source_target_pairs={{0,2},{2,4},{4,6},{6,0},{1,3},{3,5},{5,7},{7,1},{8,10},{10,12},{12... | collective-permute-start | bytes 786440 | tf_op jit(solution)/shard_map/ppermute | solution.py:314
  95.8 6.7 %collective-permute-start.25 = (bf16[2,256,256]{2,1,0:T(8,128)(2,1)S(1)}, bf16[2,256,256]{2,1,0:T(8,128)(2,1)S(1)}, u32[]{:S(2)}, u32[]{:S(2)}) collective-permute-start(bf16[2,256,256]{2,1,0:T(8,128)(2,1)S(1)} %collective-permute-done.22.refs_1_), channel_id=1, source_target_pairs={{0,1},{1,0},{2,3},{3,2},{4,5},{5,4},{6,7},{7,6},{8,9},{9,8},{10,11... | collective-permute-start | bytes 786440 | tf_op jit(solution)/shard_map/ppermute | solution.py:309
  99.9 5.5 %collective-permute-start.26 = (bf16[2,256,256]{2,1,0:T(8,128)(2,1)S(1)}, bf16[2,256,256]{2,1,0:T(8,128)(2,1)S(1)}, u32[]{:S(2)}, u32[]{:S(2)}) collective-permute-start(bf16[2,256,256]{2,1,0:T(8,128)(2,1)S(1)} %collective-permute-done.23.refs_2_), channel_id=1, source_target_pairs={{0,1},{1,0},{2,3},{3,2},{4,5},{5,4},{6,7},{7,6},{8,9},{9,8},{10,11... | collective-permute-start | bytes 786440 | tf_op jit(solution)/shard_map/ppermute | solution.py:309
  101.9 3.6 %collective-permute-start.24 = (bf16[2,256,256]{2,1,0:T(8,128)(2,1)S(1)}, bf16[2,256,256]{2,1,0:T(8,128)(2,1)S(1)}, u32[]{:S(2)}, u32[]{:S(2)}) collective-permute-start(bf16[2,256,256]{2,1,0:T(8,128)(2,1)S(1)} %collective-permute-done.9.refs_0_), channel_id=1, source_target_pairs={{0,1},{1,0},{2,3},{3,2},{4,5},{5,4},{6,7},{7,6},{8,9},{9,8},{10,11... | collective-permute-start | bytes 786440 | tf_op jit(solution)/shard_map/ppermute | solution.py:309
  102.4 5.6 %collective-permute-start.27 = (bf16[2,256,256]{2,1,0:T(8,128)(2,1)S(1)}, bf16[2,256,256]{2,1,0:T(8,128)(2,1)S(1)}, u32[]{:S(2)}, u32[]{:S(2)}) collective-permute-start(bf16[2,256,256]{2,1,0:T(8,128)(2,1)S(1)} %collective-permute-done.10.refs_3_), channel_id=1, source_target_pairs={{0,1},{1,0},{2,3},{3,2},{4,5},{5,4},{6,7},{7,6},{8,9},{9,8},{10,11... | collective-permute-start | bytes 786440 | tf_op jit(solution)/shard_map/ppermute | solution.py:309
  102.5 10.4 %collective-permute-start.17 = (bf16[2,256,256]{2,1,0:T(8,128)(2,1)S(1)}, bf16[2,256,256]{2,1,0:T(8,128)(2,1)S(1)}, u32[]{:S(2)}, u32[]{:S(2)}) collective-permute-start(bf16[2,256,256]{2,1,0:T(8,128)(2,1)S(1)} %collective-permute-done.9.refs_0_), channel_id=1, source_target_pairs={{0,2},{2,4},{4,6},{6,0},{1,3},{3,5},{5,7},{7,1},{8,10},{10,12},{12... | collective-permute-start | bytes 786440 | tf_op jit(solution)/shard_map/ppermute | solution.py:314
  102.5 10.4 %collective-permute-start.18 = (bf16[2,256,256]{2,1,0:T(8,128)(2,1)S(1)}, bf16[2,256,256]{2,1,0:T(8,128)(2,1)S(1)}, u32[]{:S(2)}, u32[]{:S(2)}) collective-permute-start(bf16[2,256,256]{2,1,0:T(8,128)(2,1)S(1)} %collective-permute-done.10.refs_3_), channel_id=1, source_target_pairs={{0,6},{2,0},{4,2},{6,4},{1,7},{3,1},{5,3},{7,5},{8,14},{10,8},{12,... | collective-permute-start | bytes 786440 | tf_op jit(solution)/shard_map/ppermute | solution.py:314
  105.4 6.4 %collective-permute-start.19 = (bf16[16,640]{1,0:T(8,128)(2,1)S(1)}, bf16[16,640]{1,0:T(8,128)(2,1)S(1)}, u32[]{:S(2)}, u32[]{:S(2)}) collective-permute-start(bf16[16,640]{1,0:T(8,128)(2,1)S(1)} %get-tuple-element.86), channel_id=1, source_target_pairs={{0,2},{2,4},{4,6},{6,0},{1,3},{3,5},{5,7},{7,1},{8,10},{10,12},{12... | collective-permute-start | bytes 61448 | tf_op jit(solution)/shard_map/ppermute | solution.py:314
  105.5 7.5 %collective-permute-start.20 = (bf16[16,640]{1,0:T(8,128)(2,1)S(1)}, bf16[16,640]{1,0:T(8,128)(2,1)S(1)}, u32[]{:S(2)}, u32[]{:S(2)}) collective-permute-start(bf16[16,640]{1,0:T(8,128)(2,1)S(1)} %get-tuple-element.85), channel_id=1, source_target_pairs={{0,4},{2,6},{4,0},{6,2},{1,5},{3,7},{5,1},{7,3},{8,12},{10,14},{12... | collective-permute-start | bytes 61448 | tf_op jit(solution)/shard_map/ppermute | solution.py:314
  108.0 4.9 %collective-permute-start.21 = (bf16[16,640]{1,0:T(8,128)(2,1)S(1)}, bf16[16,640]{1,0:T(8,128)(2,1)S(1)}, u32[]{:S(2)}, u32[]{:S(2)}) collective-permute-start(bf16[16,640]{1,0:T(8,128)(2,1)S(1)} %get-tuple-element.84), channel_id=1, source_target_pairs={{0,6},{2,0},{4,2},{6,4},{1,7},{3,1},{5,3},{7,5},{8,14},{10,8},{12,... | collective-permute-start | bytes 61448 | tf_op jit(solution)/shard_map/ppermute | solution.py:314
  113.0 2.9 %collective-permute-start.28 = (bf16[2,256,256]{2,1,0:T(8,128)(2,1)S(1)}, bf16[2,256,256]{2,1,0:T(8,128)(2,1)S(1)}, u32[]{:S(2)}, u32[]{:S(2)}) collective-permute-start(bf16[2,256,256]{2,1,0:T(8,128)(2,1)S(1)} %collective-permute-done.17.refs_0_), channel_id=1, source_target_pairs={{0,1},{1,0},{2,3},{3,2},{4,5},{5,4},{6,7},{7,6},{8,9},{9,8},{10,11... | collective-permute-start | bytes 786440 | tf_op jit(solution)/shard_map/ppermute | solution.py:309
  114.7 1.5 %collective-permute-start.29 = (bf16[2,256,256]{2,1,0:T(8,128)(2,1)S(1)}, bf16[2,256,256]{2,1,0:T(8,128)(2,1)S(1)}, u32[]{:S(2)}, u32[]{:S(2)}) collective-permute-start(bf16[2,256,256]{2,1,0:T(8,128)(2,1)S(1)} %collective-permute-done.18.refs_1_), channel_id=1, source_target_pairs={{0,1},{1,0},{2,3},{3,2},{4,5},{5,4},{6,7},{7,6},{8,9},{9,8},{10,11... | collective-permute-start | bytes 786440 | tf_op jit(solution)/shard_map/ppermute | solution.py:309

commit v7 on v6

--- a/solution.py
+++ b/solution.py
@@ -138,8 +138,8 @@
             pieces.append(jnp.transpose(turned_grad[:, at]))
         back_ref[slot(block), :, PAIR * VHEAD:] = jnp.concatenate(pieces, axis=1).astype(bf16)
 
-    for upper_block in range(blocks - 1, 0, -4):
-        duo = tuple(range(upper_block, upper_block - 4, -1))
+    for upper_block in range(blocks - 1, 0, -8):
+        duo = tuple(range(upper_block, upper_block - 8, -1))
         scores = [scores_of(block) for block in duo]
         soft = [softmax_of(score) for score in scores]
         done = [context_of(block, *soft[n]) for n, block in enumerate(duo)]

time: 119 us -> 119 us (level)
  no operation moved by 1% of the time
where the time goes in v7:
time: 119 us; the launch traced here: 118 us
  starting transfers between devices  50.7 us (43%)
  waiting for transfers between devices  34.5 us (29%)
  Pallas kernels  26.7 us (22%)
  local copies, waits for them, and re-layouts  4.09 us (3%)
  other arithmetic  1.28 us (1%)
    ppermute x21, starting transfers between devices, shifted(): lax.ppermute(value, axis, [(i, (i + steps) % count) for i in range(count)])  27.7 us
    ppermute x21, waiting for transfers between devices, shifted(): lax.ppermute(value, axis, [(i, (i + steps) % count) for i in range(count)])  17.3 us
    all_to_all x3, starting transfers between devices, exchanged(): return lax.all_to_all(value, axes, 0, 0, tiled=True)  17.1 us
    pallas_call x1, Pallas kernels, attention(): pl.pallas_call(attention_kernel, grid_spec=pltpu.PrefetchScalarGridSpec(n...  15.5 us
    all_to_all x3, waiting for transfers between devices, exchanged(): return lax.all_to_all(value, axes, 0, 0, tiled=True)  14.8 us
    pallas_call x3, Pallas kernels, unfold(): pl.pallas_call(kernel, grid_spec=pltpu.PrefetchScalarGridSpec(num_scalar_...  6.57 us
    ppermute x9, starting transfers between devices, swapped(): return lax.ppermute(value, 'core', [(0, 1), (1, 0)])  5.92 us
    pallas_call x1, Pallas kernels, join(): pl.pallas_call(kernel, out_shape=[jax.ShapeDtypeStruct((rows, slots * val...  2.5 us
  transfers between devices with their start and end apart: 33, of which 13 were waited for; matrix products, arithmetic and copies ran while one was open for 4% of the time, Pallas kernels for 8%

profile of v7, /device:TPU:1, one launch (start us, length us, event | category | flops | bytes accessed | tf_op | source)
XLA Modules:
  0.0 118.3 jit_solution(8289814429076489423)
XLA Ops:
  0.6 2.5 %collective-permute-start = (bf16[16,576]{1,0:T(8,128)(2,1)}, bf16[16,576]{1,0:T(8,128)(2,1)S(1)}, u32[]{:S(2)}, u32[]{:S(2)}) collective-permute-start(bf16[16,576]{1,0:T(8,128)(2,1)} %param.7), channel_id=1, source_target_pairs={{0,16},{16,32},{32,48},{48,0},{1,17},{17,33},{33,49},{49,1},{2,18}... | collective-permute-start | bytes 55304 | tf_op jit(solution)/shard_map/ppermute | solution.py:314
  3.2 3.3 %collective-permute-start.1 = (bf16[16,576]{1,0:T(8,128)(2,1)}, bf16[16,576]{1,0:T(8,128)(2,1)S(1)}, u32[]{:S(2)}, u32[]{:S(2)}) collective-permute-start(bf16[16,576]{1,0:T(8,128)(2,1)} %param.7), channel_id=1, source_target_pairs={{0,32},{16,48},{32,0},{48,16},{1,33},{17,49},{33,1},{49,17},{2,34}... | collective-permute-start | bytes 55304 | tf_op jit(solution)/shard_map/ppermute | solution.py:314
  6.5 0.7 collective-permute-start.2
  7.2 1.3 %copy.17 = bf16[128,2048]{0,1:T(8,128)(2,1)S(1)} copy(bf16[128,2048]{1,0:T(8,128)(2,1)} %param.10) | data formatting | bytes 1048576 | tf_op args[4]
  8.5 1.0 copy.18
  9.6 6.5 %all-to-all-start = ((bf16[8,128,256]{2,1,0:T(8,128)(2,1)}), bf16[8,128,256]{2,1,0:T(8,128)(2,1)S(1)}, u32[]{:S(2)}, u32[]{:S(2)}) async-start(bf16[8,128,256]{2,1,0:T(8,128)(2,1)} %bitcast.9), calls=%async_computation | async-start | bytes 1048576 | tf_op jit(solution)/shard_map/all_to_all | solution.py:318
  16.0 1.3 %collective-permute-start.3 = (bf16[4,16,576]{2,1,0:T(8,128)(2,1)S(1)}, bf16[4,16,576]{2,1,0:T(8,128)(2,1)S(1)}, u32[]{:S(2)}, u32[]{:S(2)}) collective-permute-start(bf16[4,16,576]{2,1,0:T(8,128)(2,1)S(1)} %pad_maximum_fusion.2), channel_id=1, source_target_pairs={{0,8},{8,0},{1,9},{9,1},{2,10},{10,2},{3,11},{11,3},{4,12},{12,4},... | collective-permute-start | bytes 221192 | tf_op jit(solution)/shard_map/ppermute | solution.py:314
  17.3 2.1 %pack.1 = bf16[64,16,384]{2,1,0:T(8,128)(2,1)} custom-call(bf16[16,24576]{1,0:T(8,128)(2,1)} %query_ref.1), custom_call_target="tpu_custom_call" | custom-call | tf_op jit(solution)/shard_map/pack/pallas_call | solution.py:301
  19.4 0.7 collective-permute-done.3
  20.2 1.0 collective-permute-start.4
  21.2 2.4 %collective-permute-start.5 = (bf16[128,576]{1,0:T(8,128)(2,1)S(1)}, bf16[128,576]{1,0:T(8,128)(2,1)S(1)}, u32[]{:S(2)}, u32[]{:S(2)}) collective-permute-start(bf16[128,576]{1,0:T(8,128)(2,1)S(1)} %bitcast.47), channel_id=1, source_target_pairs={{0,4},{2,6},{4,0},{6,2},{1,5},{3,7},{5,1},{7,3},{8,12},{10,14},{12... | collective-permute-start | bytes 442376 | tf_op jit(solution)/shard_map/ppermute | solution.py:314
  23.6 1.2 collective-permute-start.6
  24.8 1.0 all-to-all-done.grad_ref
  25.7 6.3 %all-to-all-start.1 = ((bf16[64,16,384]{2,1,0:T(8,128)(2,1)}), bf16[64,16,384]{2,1,0:T(8,128)(2,1)S(1)}, u32[]{:S(2)}, u32[]{:S(2)}) async-start(bf16[64,16,384]{2,1,0:T(8,128)(2,1)} %pack.1), calls=%async_computation.1 | async-start | bytes 1572864 | tf_op jit(solution)/shard_map/all_to_all | solution.py:318
  32.1 0.5 collective-permute-done.5
  33.1 1.1 collective-permute-start.7
  34.3 1.6 %collective-permute-done.7 = bf16[4,128,576]{1,2,0:T(8,128)(2,1)S(1)} collective-permute-done((bf16[4,128,576]{1,2,0:T(8,128)(2,1)S(1)}, bf16[4,128,576]{1,2,0:T(8,128)(2,1)S(1)}, u32[]{:S(2)}, u32[]{:S(2)}) %collective-permute-start.7) | collective-permute-done | bytes 589856 | tf_op jit(solution)/shard_map/ppermute | solution.py:309
  36.1 11.1 %all-to-all-done.1 = bf16[64,16,384]{2,1,0:T(8,128)(2,1)S(1)} async-done(((bf16[64,16,384]{2,1,0:T(8,128)(2,1)}), bf16[64,16,384]{2,1,0:T(8,128)(2,1)S(1)}, u32[]{:S(2)}, u32[]{:S(2)}) %all-to-all-start.1) | async-done | bytes 786464 | tf_op jit(solution)/shard_map/all_to_all | solution.py:318
  47.2 1.0 copy-done.1
  48.3 15.5 %attention.1 = (bf16[8,128,640]{2,1,0:T(8,128)(2,1)}, bf16[2,512,256]{2,1,0:T(8,128)(2,1)S(1)}, bf16[4,2,4,16,640]{4,3,2,1,0:T(8,128)(2,1)S(1)}, bf16[4,2,4,16,640]{4,3,2,1,0:T(8,128)(2,1)}) custom-call(s32[4]{0:T(128)S(1)} %pad_add_fusion.place, s32[1,8]{1,0:T(1,128)S(1)} %copy-done.2, bf16[1024,384]{1,0:T(8,128)(2,1)S(1)} %bitcast.44, ...), custom_call_target="tpu_custom_call" | custom-call | flops 8999999488 | bytes 15000000 | tf_op jit(solution)/shard_map/attention/pallas_call | solution.py:182
  63.8 0.4 collective-permute-start.11
  64.2 4.3 %all-to-all-start.2 = ((bf16[8,128,640]{2,1,0:T(8,128)(2,1)}), bf16[8,128,640]{2,1,0:T(8,128)(2,1)}, u32[]{:S(2)}, u32[]{:S(2)}) async-start(bf16[8,128,640]{2,1,0:T(8,128)(2,1)} %get-tuple-element.49), calls=%async_computation.2 | async-start | bytes 2621440 | tf_op jit(solution)/shard_map/all_to_all | solution.py:318
  68.5 2.6 %collective-permute-start.8 = (bf16[2,512,256]{2,1,0:T(8,128)(2,1)S(1)}, bf16[2,512,256]{2,1,0:T(8,128)(2,1)S(1)}, u32[]{:S(2)}, u32[]{:S(2)}) collective-permute-start(bf16[2,512,256]{2,1,0:T(8,128)(2,1)S(1)} %get-tuple-element.48), channel_id=1, source_target_pairs={{0,64},{64,0},{1,65},{65,1},{2,66},{66,2},{3,67},{67,3},{4,68},{68... | collective-permute-start | bytes 1572872 | tf_op jit(solution)/shard_map/ppermute | solution.py:314
  71.3 0.4 collective-permute-start.12
  71.7 1.8 %collective-permute-start.13 = (bf16[2,4,16,640]{3,2,1,0:T(8,128)(2,1)S(1)}, bf16[2,4,16,640]{3,2,1,0:T(8,128)(2,1)S(1)}, u32[]{:S(2)}, u32[]{:S(2)}) collective-permute-start(bf16[2,4,16,640]{3,2,1,0:T(8,128)(2,1)S(1)} %get-tuple-element.81), channel_id=1, source_target_pairs={{0,32},{16,48},{32,0},{48,16},{1,33},{17,49},{33,1},{49,17},{2,34}... | collective-permute-start | bytes 491528 | tf_op jit(solution)/shard_map/ppermute | solution.py:314
  73.5 0.7 collective-permute-start.14
  74.2 9.2 %collective-permute-done.8 = bf16[2,512,256]{2,1,0:T(8,128)(2,1)S(1)} collective-permute-done((bf16[2,512,256]{2,1,0:T(8,128)(2,1)S(1)}, bf16[2,512,256]{2,1,0:T(8,128)(2,1)S(1)}, u32[]{:S(2)}, u32[]{:S(2)}) %collective-permute-start.8) | collective-permute-done | bytes 524320 | tf_op jit(solution)/shard_map/ppermute | solution.py:314
  83.6 2.8 %all-to-all-done.2.back_ref = bf16[8,128,640]{2,1,0:T(8,128)(2,1)} async-done(((bf16[8,128,640]{2,1,0:T(8,128)(2,1)}), bf16[8,128,640]{2,1,0:T(8,128)(2,1)}, u32[]{:S(2)}, u32[]{:S(2)}) %all-to-all-start.2) | async-done | bytes 1310752 | tf_op jit(solution)/shard_map/all_to_all | solution.py:318
  86.8 0.5 collective-permute-start.22
  87.4 2.3 %collective-permute-start.23 = (bf16[2,256,256]{2,1,0:T(8,128)(2,1)S(1)}, bf16[2,256,256]{2,1,0:T(8,128)(2,1)S(1)}, u32[]{:S(2)}, u32[]{:S(2)}) collective-permute-start(bf16[2,256,256]{2,1,0:T(8,128)(2,1)S(1)} %get-tuple-element.83), channel_id=1, source_target_pairs={{0,6},{2,0},{4,2},{6,4},{1,7},{3,1},{5,3},{7,5},{8,14},{10,8},{12,... | collective-permute-start | bytes 786440 | tf_op jit(solution)/shard_map/ppermute | solution.py:314
  90.0 0.7 collective-permute-done.15
  90.7 0.5 collective-permute-start.9
  91.2 4.7 %collective-permute-done.22.refs_1_ = bf16[2,256,256]{2,1,0:T(8,128)(2,1)S(1)} collective-permute-done((bf16[2,256,256]{2,1,0:T(8,128)(2,1)S(1)}, bf16[2,256,256]{2,1,0:T(8,128)(2,1)S(1)}, u32[]{:S(2)}, u32[]{:S(2)}) %collective-permute-start.22) | collective-permute-done | bytes 262176 | tf_op jit(solution)/shard_map/ppermute | solution.py:314
  95.8 1.5 %collective-permute-start.25 = (bf16[2,256,256]{2,1,0:T(8,128)(2,1)S(1)}, bf16[2,256,256]{2,1,0:T(8,128)(2,1)S(1)}, u32[]{:S(2)}, u32[]{:S(2)}) collective-permute-start(bf16[2,256,256]{2,1,0:T(8,128)(2,1)S(1)} %collective-permute-done.22.refs_1_), channel_id=1, source_target_pairs={{0,1},{1,0},{2,3},{3,2},{4,5},{5,4},{6,7},{7,6},{8,9},{9,8},{10,11... | collective-permute-start | bytes 786440 | tf_op jit(solution)/shard_map/ppermute | solution.py:309
  97.4 2.5 %join.1 = (bf16[128,2048]{1,0:T(8,128)(2,1)}, bf16[128,3072]{1,0:T(8,128)(2,1)}) custom-call(bf16[8,128,640]{2,1,0:T(8,128)(2,1)} %all-to-all-done.2.back_ref), custom_call_target="tpu_custom_call" | custom-call | tf_op jit(solution)/shard_map/join/pallas_call | solution.py:227
  99.9 1.9 %unfold.3 = (f32[16,512,128]{2,1,0:T(8,128)}, f32[16,512,128]{2,1,0:T(8,128)}) custom-call(s32[4]{0:T(128)S(1)} %pad_add_fusion.place, bf16[2,512,256]{2,1,0:T(8,128)(2,1)S(1)} %add_convert_fusion.1.refs_0_, bf16[2,512,256]{2,1,0:T(8,128)(2,1)S(1)} %collective-permute-done.16.refs_1_), custom_call_target="tpu_custom_call" | custom-call | bytes 4000000 | tf_op jit(solution)/shard_map/unfold/pallas_call | solution.py:271
  101.9 0.6 collective-permute-start.24
  102.5 2.8 %collective-permute-start.18 = (bf16[2,256,256]{2,1,0:T(8,128)(2,1)S(1)}, bf16[2,256,256]{2,1,0:T(8,128)(2,1)S(1)}, u32[]{:S(2)}, u32[]{:S(2)}) collective-permute-start(bf16[2,256,256]{2,1,0:T(8,128)(2,1)S(1)} %collective-permute-done.10.refs_3_), channel_id=1, source_target_pairs={{0,6},{2,0},{4,2},{6,4},{1,7},{3,1},{5,3},{7,5},{8,14},{10,8},{12,... | collective-permute-start | bytes 786440 | tf_op jit(solution)/shard_map/ppermute | solution.py:314
  105.5 2.6 %collective-permute-start.20 = (bf16[16,640]{1,0:T(8,128)(2,1)S(1)}, bf16[16,640]{1,0:T(8,128)(2,1)S(1)}, u32[]{:S(2)}, u32[]{:S(2)}) collective-permute-start(bf16[16,640]{1,0:T(8,128)(2,1)S(1)} %get-tuple-element.85), channel_id=1, source_target_pairs={{0,4},{2,6},{4,0},{6,2},{1,5},{3,7},{5,1},{7,3},{8,12},{10,14},{12... | collective-permute-start | bytes 61448 | tf_op jit(solution)/shard_map/ppermute | solution.py:314
  108.0 0.6 collective-permute-start.21
  108.6 2.7 %unfold.4 = (f32[16,512,128]{2,1,0:T(8,128)}, f32[16,512,128]{2,1,0:T(8,128)}) custom-call(s32[4]{0:T(128)S(1)} %pad_add_fusion.place, bf16[2,256,256]{2,1,0:T(8,128)(2,1)S(1)} %collective-permute-done.9.refs_0_, bf16[2,256,256]{2,1,0:T(8,128)(2,1)S(1)} %collective-permute-done.22.refs_1_, ...), custom_call_target="tpu_custom_call", output_to_operand_aliasing={{0}: (9, {}), {1}: (10, {})} | custom-call | bytes 4000000 | tf_op jit(solution)/shard_map/unfold/pallas_call | solution.py:271
  111.3 0.4 collective-permute-done.19
  111.8 1.1 collective-permute-done.20
  112.9 1.7 %collective-permute-start.28 = (bf16[2,256,256]{2,1,0:T(8,128)(2,1)S(1)}, bf16[2,256,256]{2,1,0:T(8,128)(2,1)S(1)}, u32[]{:S(2)}, u32[]{:S(2)}) collective-permute-start(bf16[2,256,256]{2,1,0:T(8,128)(2,1)S(1)} %collective-permute-done.17.refs_0_), channel_id=1, source_target_pairs={{0,1},{1,0},{2,3},{3,2},{4,5},{5,4},{6,7},{7,6},{8,9},{9,8},{10,11... | collective-permute-start | bytes 786440 | tf_op jit(solution)/shard_map/ppermute | solution.py:309
  114.8 0.6 convert_add_fusion.2
  115.4 0.4 collective-permute-done.28.refs_2_
  115.8 0.4 collective-permute-done.29.refs_3_
  116.2 1.9 %unfold.5 = (f32[16,512,128]{2,1,0:T(8,128)}, f32[16,512,128]{2,1,0:T(8,128)}) custom-call(s32[4]{0:T(128)S(1)} %pad_add_fusion.place, bf16[2,256,256]{2,1,0:T(8,128)(2,1)S(1)} %collective-permute-done.17.refs_0_, bf16[2,256,256]{2,1,0:T(8,128)(2,1)S(1)} %collective-permute-done.18.refs_1_, ...), custom_call_target="tpu_custom_call", output_to_operand_aliasing={{0}: (5, {}), {1}: (6, {})} | custom-call | bytes 4000000 | tf_op jit(solution)/shard_map/unfold/pallas_call | solution.py:271
  (49 shorter events, 2.4 us)
Async XLA Ops:
  0.6 8.9 %copy-start.3 = (bf16[16,576]{1,0:T(8,128)(2,1)S(1)}, bf16[16,576]{1,0:T(8,128)(2,1)}, u32[]{:S(2)}) copy-start(bf16[16,576]{1,0:T(8,128)(2,1)} %param.7) | copy-start | bytes 55300
  0.6 8.9 %collective-permute-start = (bf16[16,576]{1,0:T(8,128)(2,1)}, bf16[16,576]{1,0:T(8,128)(2,1)S(1)}, u32[]{:S(2)}, u32[]{:S(2)}) collective-permute-start(bf16[16,576]{1,0:T(8,128)(2,1)} %param.7), channel_id=1, source_target_pairs={{0,16},{16,32},{32,48},{48,0},{1,17},{17,33},{33,49},{49,1},{2,18}... | collective-permute-start | bytes 55304 | tf_op jit(solution)/shard_map/ppermute | solution.py:314
  3.2 6.4 %collective-permute-start.1 = (bf16[16,576]{1,0:T(8,128)(2,1)}, bf16[16,576]{1,0:T(8,128)(2,1)S(1)}, u32[]{:S(2)}, u32[]{:S(2)}) collective-permute-start(bf16[16,576]{1,0:T(8,128)(2,1)} %param.7), channel_id=1, source_target_pairs={{0,32},{16,48},{32,0},{48,16},{1,33},{17,49},{33,1},{49,17},{2,34}... | collective-permute-start | bytes 55304 | tf_op jit(solution)/shard_map/ppermute | solution.py:314
  6.5 3.1 %collective-permute-start.2 = (bf16[16,576]{1,0:T(8,128)(2,1)}, bf16[16,576]{1,0:T(8,128)(2,1)S(1)}, u32[]{:S(2)}, u32[]{:S(2)}) collective-permute-start(bf16[16,576]{1,0:T(8,128)(2,1)} %param.7), channel_id=1, source_target_pairs={{0,48},{16,0},{32,16},{48,32},{1,49},{17,1},{33,17},{49,33},{2,50}... | collective-permute-start | bytes 55304 | tf_op jit(solution)/shard_map/ppermute | solution.py:314
  9.6 16.1 %all-to-all-start = ((bf16[8,128,256]{2,1,0:T(8,128)(2,1)}), bf16[8,128,256]{2,1,0:T(8,128)(2,1)S(1)}, u32[]{:S(2)}, u32[]{:S(2)}) async-start(bf16[8,128,256]{2,1,0:T(8,128)(2,1)} %bitcast.9), calls=%async_computation | async-start | bytes 1048576 | tf_op jit(solution)/shard_map/all_to_all | solution.py:318
  16.0 4.1 %collective-permute-start.3 = (bf16[4,16,576]{2,1,0:T(8,128)(2,1)S(1)}, bf16[4,16,576]{2,1,0:T(8,128)(2,1)S(1)}, u32[]{:S(2)}, u32[]{:S(2)}) collective-permute-start(bf16[4,16,576]{2,1,0:T(8,128)(2,1)S(1)} %pad_maximum_fusion.2), channel_id=1, source_target_pairs={{0,8},{8,0},{1,9},{9,1},{2,10},{10,2},{3,11},{11,3},{4,12},{12,4},... | collective-permute-start | bytes 221192 | tf_op jit(solution)/shard_map/ppermute | solution.py:314
  20.2 11.9 %collective-permute-start.4 = (bf16[128,576]{1,0:T(8,128)(2,1)S(1)}, bf16[128,576]{1,0:T(8,128)(2,1)S(1)}, u32[]{:S(2)}, u32[]{:S(2)}) collective-permute-start(bf16[128,576]{1,0:T(8,128)(2,1)S(1)} %bitcast.46), channel_id=1, source_target_pairs={{0,2},{2,4},{4,6},{6,0},{1,3},{3,5},{5,7},{7,1},{8,10},{10,12},{12... | collective-permute-start | bytes 442376 | tf_op jit(solution)/shard_map/ppermute | solution.py:314
  21.2 11.4 %collective-permute-start.5 = (bf16[128,576]{1,0:T(8,128)(2,1)S(1)}, bf16[128,576]{1,0:T(8,128)(2,1)S(1)}, u32[]{:S(2)}, u32[]{:S(2)}) collective-permute-start(bf16[128,576]{1,0:T(8,128)(2,1)S(1)} %bitcast.47), channel_id=1, source_target_pairs={{0,4},{2,6},{4,0},{6,2},{1,5},{3,7},{5,1},{7,3},{8,12},{10,14},{12... | collective-permute-start | bytes 442376 | tf_op jit(solution)/shard_map/ppermute | solution.py:314
  23.6 9.0 %collective-permute-start.6 = (bf16[128,576]{1,0:T(8,128)(2,1)S(1)}, bf16[128,576]{1,0:T(8,128)(2,1)S(1)}, u32[]{:S(2)}, u32[]{:S(2)}) collective-permute-start(bf16[128,576]{1,0:T(8,128)(2,1)S(1)} %bitcast.48), channel_id=1, source_target_pairs={{0,6},{2,0},{4,2},{6,4},{1,7},{3,1},{5,3},{7,5},{8,14},{10,8},{12,... | collective-permute-start | bytes 442376 | tf_op jit(solution)/shard_map/ppermute | solution.py:314
  25.7 6.9 %copy-start = (bf16[8,128,256]{2,1,0:T(8,128)(2,1)}, bf16[8,128,256]{2,1,0:T(8,128)(2,1)S(1)}, u32[]{:S(2)}) copy-start(bf16[8,128,256]{2,1,0:T(8,128)(2,1)S(1)} %all-to-all-done.grad_ref) | copy-start | bytes 1572868
  25.7 21.5 %all-to-all-start.1 = ((bf16[64,16,384]{2,1,0:T(8,128)(2,1)}), bf16[64,16,384]{2,1,0:T(8,128)(2,1)S(1)}, u32[]{:S(2)}, u32[]{:S(2)}) async-start(bf16[64,16,384]{2,1,0:T(8,128)(2,1)} %pack.1), calls=%async_computation.1 | async-start | bytes 1572864 | tf_op jit(solution)/shard_map/all_to_all | solution.py:318
  32.1 15.1 %copy-start.2 = (s32[1,8]{1,0:T(1,128)S(1)}, s32[1,8]{1,0:T(1,128)}, u32[]{:S(2)}) copy-start(s32[1,8]{1,0:T(1,128)} %docs.1) | copy-start | bytes 100
  33.1 2.8 %collective-permute-start.7 = (bf16[4,128,576]{1,2,0:T(8,128)(2,1)S(1)}, bf16[4,128,576]{1,2,0:T(8,128)(2,1)S(1)}, u32[]{:S(2)}, u32[]{:S(2)}) collective-permute-start(bf16[4,128,576]{1,2,0:T(8,128)(2,1)S(1)} %copy.19), channel_id=1, source_target_pairs={{0,1},{1,0},{2,3},{3,2},{4,5},{5,4},{6,7},{7,6},{8,9},{9,8},{10,11... | collective-permute-start | bytes 1769480 | tf_op jit(solution)/shard_map/ppermute | solution.py:309
  47.2 1.0 copy-start.1
  63.8 7.3 %collective-permute-start.11 = (bf16[4,2,4,16,640]{4,3,2,1,0:T(8,128)(2,1)}, bf16[4,2,4,16,640]{4,3,2,1,0:T(8,128)(2,1)S(1)}, u32[]{:S(2)}, u32[]{:S(2)}) collective-permute-start(bf16[4,2,4,16,640]{4,3,2,1,0:T(8,128)(2,1)} %get-tuple-element.52), channel_id=1, source_target_pairs={{0,1},{1,0},{2,3},{3,2},{4,5},{5,4},{6,7},{7,6},{8,9},{9,8},{10,11... | collective-permute-start | bytes 1966088 | tf_op jit(solution)/shard_map/ppermute | solution.py:309
  64.2 22.2 %all-to-all-start.2 = ((bf16[8,128,640]{2,1,0:T(8,128)(2,1)}), bf16[8,128,640]{2,1,0:T(8,128)(2,1)}, u32[]{:S(2)}, u32[]{:S(2)}) async-start(bf16[8,128,640]{2,1,0:T(8,128)(2,1)} %get-tuple-element.49), calls=%async_computation.2 | async-start | bytes 2621440 | tf_op jit(solution)/shard_map/all_to_all | solution.py:318
  68.5 14.9 %collective-permute-start.8 = (bf16[2,512,256]{2,1,0:T(8,128)(2,1)S(1)}, bf16[2,512,256]{2,1,0:T(8,128)(2,1)S(1)}, u32[]{:S(2)}, u32[]{:S(2)}) collective-permute-start(bf16[2,512,256]{2,1,0:T(8,128)(2,1)S(1)} %get-tuple-element.48), channel_id=1, source_target_pairs={{0,64},{64,0},{1,65},{65,1},{2,66},{66,2},{3,67},{67,3},{4,68},{68... | collective-permute-start | bytes 1572872 | tf_op jit(solution)/shard_map/ppermute | solution.py:314
  71.3 12.2 %collective-permute-start.12 = (bf16[2,4,16,640]{3,2,1,0:T(8,128)(2,1)S(1)}, bf16[2,4,16,640]{3,2,1,0:T(8,128)(2,1)S(1)}, u32[]{:S(2)}, u32[]{:S(2)}) collective-permute-start(bf16[2,4,16,640]{3,2,1,0:T(8,128)(2,1)S(1)} %get-tuple-element.79), channel_id=1, source_target_pairs={{0,16},{16,32},{32,48},{48,0},{1,17},{17,33},{33,49},{49,1},{2,18}... | collective-permute-start | bytes 491528 | tf_op jit(solution)/shard_map/ppermute | solution.py:314
  71.7 11.8 %collective-permute-start.13 = (bf16[2,4,16,640]{3,2,1,0:T(8,128)(2,1)S(1)}, bf16[2,4,16,640]{3,2,1,0:T(8,128)(2,1)S(1)}, u32[]{:S(2)}, u32[]{:S(2)}) collective-permute-start(bf16[2,4,16,640]{3,2,1,0:T(8,128)(2,1)S(1)} %get-tuple-element.81), channel_id=1, source_target_pairs={{0,32},{16,48},{32,0},{48,16},{1,33},{17,49},{33,1},{49,17},{2,34}... | collective-permute-start | bytes 491528 | tf_op jit(solution)/shard_map/ppermute | solution.py:314
  73.5 10.1 %collective-permute-start.14 = (bf16[2,4,16,640]{3,2,1,0:T(8,128)(2,1)S(1)}, bf16[2,4,16,640]{3,2,1,0:T(8,128)(2,1)S(1)}, u32[]{:S(2)}, u32[]{:S(2)}) collective-permute-start(bf16[2,4,16,640]{3,2,1,0:T(8,128)(2,1)S(1)} %get-tuple-element.80), channel_id=1, source_target_pairs={{0,48},{16,0},{32,16},{48,32},{1,49},{17,1},{33,17},{49,33},{2,50}... | collective-permute-start | bytes 491528 | tf_op jit(solution)/shard_map/ppermute | solution.py:314
  86.4 13.5 %collective-permute-start.16 = (bf16[2,512,256]{2,1,0:T(8,128)(2,1)S(1)}, bf16[2,512,256]{2,1,0:T(8,128)(2,1)S(1)}, u32[]{:S(2)}, u32[]{:S(2)}) collective-permute-start(bf16[2,512,256]{2,1,0:T(8,128)(2,1)S(1)} %add_convert_fusion.1.refs_0_), channel_id=1, source_target_pairs={{0,1},{1,0},{2,3},{3,2},{4,5},{5,4},{6,7},{7,6},{8,9},{9,8},{10,11... | collective-permute-start | bytes 1572872 | tf_op jit(solution)/shard_map/ppermute | solution.py:309
  86.8 9.0 %collective-permute-start.22 = (bf16[2,256,256]{2,1,0:T(8,128)(2,1)S(1)}, bf16[2,256,256]{2,1,0:T(8,128)(2,1)S(1)}, u32[]{:S(2)}, u32[]{:S(2)}) collective-permute-start(bf16[2,256,256]{2,1,0:T(8,128)(2,1)S(1)} %get-tuple-element.82), channel_id=1, source_target_pairs={{0,2},{2,4},{4,6},{6,0},{1,3},{3,5},{5,7},{7,1},{8,10},{10,12},{12... | collective-permute-start | bytes 786440 | tf_op jit(solution)/shard_map/ppermute | solution.py:314
  87.3 3.4 %collective-permute-start.15 = (bf16[4,16,640]{2,1,0:T(8,128)(2,1)S(1)}, bf16[4,16,640]{2,1,0:T(8,128)(2,1)S(1)}, u32[]{:S(2)}, u32[]{:S(2)}) collective-permute-start(bf16[4,16,640]{2,1,0:T(8,128)(2,1)S(1)} %slice_bitcast_fusion.4), channel_id=1, source_target_pairs={{0,8},{8,0},{1,9},{9,1},{2,10},{10,2},{3,11},{11,3},{4,12},{12,4},... | collective-permute-start | bytes 245768 | tf_op jit(solution)/shard_map/ppermute | solution.py:314
  87.4 12.5 %collective-permute-start.23 = (bf16[2,256,256]{2,1,0:T(8,128)(2,1)S(1)}, bf16[2,256,256]{2,1,0:T(8,128)(2,1)S(1)}, u32[]{:S(2)}, u32[]{:S(2)}) collective-permute-start(bf16[2,256,256]{2,1,0:T(8,128)(2,1)S(1)} %get-tuple-element.83), channel_id=1, source_target_pairs={{0,6},{2,0},{4,2},{6,4},{1,7},{3,1},{5,3},{7,5},{8,14},{10,8},{12,... | collective-permute-start | bytes 786440 | tf_op jit(solution)/shard_map/ppermute | solution.py:314
  89.7 12.1 %collective-permute-start.10 = (bf16[2,256,256]{2,1,0:T(8,128)(2,1)S(1)}, bf16[2,256,256]{2,1,0:T(8,128)(2,1)S(1)}, u32[]{:S(2)}, u32[]{:S(2)}) collective-permute-start(bf16[2,256,256]{2,1,0:T(8,128)(2,1)S(1)} %get-tuple-element.82), channel_id=1, source_target_pairs={{0,6},{2,0},{4,2},{6,4},{1,7},{3,1},{5,3},{7,5},{8,14},{10,8},{12,... | collective-permute-start | bytes 786440 | tf_op jit(solution)/shard_map/ppermute | solution.py:314
  90.7 11.2 %collective-permute-start.9 = (bf16[2,256,256]{2,1,0:T(8,128)(2,1)S(1)}, bf16[2,256,256]{2,1,0:T(8,128)(2,1)S(1)}, u32[]{:S(2)}, u32[]{:S(2)}) collective-permute-start(bf16[2,256,256]{2,1,0:T(8,128)(2,1)S(1)} %get-tuple-element.83), channel_id=1, source_target_pairs={{0,2},{2,4},{4,6},{6,0},{1,3},{3,5},{5,7},{7,1},{8,10},{10,12},{12... | collective-permute-start | bytes 786440 | tf_op jit(solution)/shard_map/ppermute | solution.py:314
  95.8 6.7 %collective-permute-start.25 = (bf16[2,256,256]{2,1,0:T(8,128)(2,1)S(1)}, bf16[2,256,256]{2,1,0:T(8,128)(2,1)S(1)}, u32[]{:S(2)}, u32[]{:S(2)}) collective-permute-start(bf16[2,256,256]{2,1,0:T(8,128)(2,1)S(1)} %collective-permute-done.22.refs_1_), channel_id=1, source_target_pairs={{0,1},{1,0},{2,3},{3,2},{4,5},{5,4},{6,7},{7,6},{8,9},{9,8},{10,11... | collective-permute-start | bytes 786440 | tf_op jit(solution)/shard_map/ppermute | solution.py:309
  99.9 5.5 %collective-permute-start.26 = (bf16[2,256,256]{2,1,0:T(8,128)(2,1)S(1)}, bf16[2,256,256]{2,1,0:T(8,128)(2,1)S(1)}, u32[]{:S(2)}, u32[]{:S(2)}) collective-permute-start(bf16[2,256,256]{2,1,0:T(8,128)(2,1)S(1)} %collective-permute-done.23.refs_2_), channel_id=1, source_target_pairs={{0,1},{1,0},{2,3},{3,2},{4,5},{5,4},{6,7},{7,6},{8,9},{9,8},{10,11... | collective-permute-start | bytes 786440 | tf_op jit(solution)/shard_map/ppermute | solution.py:309
  101.9 3.6 %collective-permute-start.24 = (bf16[2,256,256]{2,1,0:T(8,128)(2,1)S(1)}, bf16[2,256,256]{2,1,0:T(8,128)(2,1)S(1)}, u32[]{:S(2)}, u32[]{:S(2)}) collective-permute-start(bf16[2,256,256]{2,1,0:T(8,128)(2,1)S(1)} %collective-permute-done.9.refs_0_), channel_id=1, source_target_pairs={{0,1},{1,0},{2,3},{3,2},{4,5},{5,4},{6,7},{7,6},{8,9},{9,8},{10,11... | collective-permute-start | bytes 786440 | tf_op jit(solution)/shard_map/ppermute | solution.py:309
  102.4 5.6 %collective-permute-start.27 = (bf16[2,256,256]{2,1,0:T(8,128)(2,1)S(1)}, bf16[2,256,256]{2,1,0:T(8,128)(2,1)S(1)}, u32[]{:S(2)}, u32[]{:S(2)}) collective-permute-start(bf16[2,256,256]{2,1,0:T(8,128)(2,1)S(1)} %collective-permute-done.10.refs_3_), channel_id=1, source_target_pairs={{0,1},{1,0},{2,3},{3,2},{4,5},{5,4},{6,7},{7,6},{8,9},{9,8},{10,11... | collective-permute-start | bytes 786440 | tf_op jit(solution)/shard_map/ppermute | solution.py:309
  102.5 10.4 %collective-permute-start.17 = (bf16[2,256,256]{2,1,0:T(8,128)(2,1)S(1)}, bf16[2,256,256]{2,1,0:T(8,128)(2,1)S(1)}, u32[]{:S(2)}, u32[]{:S(2)}) collective-permute-start(bf16[2,256,256]{2,1,0:T(8,128)(2,1)S(1)} %collective-permute-done.9.refs_0_), channel_id=1, source_target_pairs={{0,2},{2,4},{4,6},{6,0},{1,3},{3,5},{5,7},{7,1},{8,10},{10,12},{12... | collective-permute-start | bytes 786440 | tf_op jit(solution)/shard_map/ppermute | solution.py:314
  102.5 10.4 %collective-permute-start.18 = (bf16[2,256,256]{2,1,0:T(8,128)(2,1)S(1)}, bf16[2,256,256]{2,1,0:T(8,128)(2,1)S(1)}, u32[]{:S(2)}, u32[]{:S(2)}) collective-permute-start(bf16[2,256,256]{2,1,0:T(8,128)(2,1)S(1)} %collective-permute-done.10.refs_3_), channel_id=1, source_target_pairs={{0,6},{2,0},{4,2},{6,4},{1,7},{3,1},{5,3},{7,5},{8,14},{10,8},{12,... | collective-permute-start | bytes 786440 | tf_op jit(solution)/shard_map/ppermute | solution.py:314
  105.4 6.4 %collective-permute-start.19 = (bf16[16,640]{1,0:T(8,128)(2,1)S(1)}, bf16[16,640]{1,0:T(8,128)(2,1)S(1)}, u32[]{:S(2)}, u32[]{:S(2)}) collective-permute-start(bf16[16,640]{1,0:T(8,128)(2,1)S(1)} %get-tuple-element.86), channel_id=1, source_target_pairs={{0,2},{2,4},{4,6},{6,0},{1,3},{3,5},{5,7},{7,1},{8,10},{10,12},{12... | collective-permute-start | bytes 61448 | tf_op jit(solution)/shard_map/ppermute | solution.py:314
  105.5 7.5 %collective-permute-start.20 = (bf16[16,640]{1,0:T(8,128)(2,1)S(1)}, bf16[16,640]{1,0:T(8,128)(2,1)S(1)}, u32[]{:S(2)}, u32[]{:S(2)}) collective-permute-start(bf16[16,640]{1,0:T(8,128)(2,1)S(1)} %get-tuple-element.85), channel_id=1, source_target_pairs={{0,4},{2,6},{4,0},{6,2},{1,5},{3,7},{5,1},{7,3},{8,12},{10,14},{12... | collective-permute-start | bytes 61448 | tf_op jit(solution)/shard_map/ppermute | solution.py:314
  108.0 4.9 %collective-permute-start.21 = (bf16[16,640]{1,0:T(8,128)(2,1)S(1)}, bf16[16,640]{1,0:T(8,128)(2,1)S(1)}, u32[]{:S(2)}, u32[]{:S(2)}) collective-permute-start(bf16[16,640]{1,0:T(8,128)(2,1)S(1)} %get-tuple-element.84), channel_id=1, source_target_pairs={{0,6},{2,0},{4,2},{6,4},{1,7},{3,1},{5,3},{7,5},{8,14},{10,8},{12,... | collective-permute-start | bytes 61448 | tf_op jit(solution)/shard_map/ppermute | solution.py:314
  112.9 2.9 %collective-permute-start.28 = (bf16[2,256,256]{2,1,0:T(8,128)(2,1)S(1)}, bf16[2,256,256]{2,1,0:T(8,128)(2,1)S(1)}, u32[]{:S(2)}, u32[]{:S(2)}) collective-permute-start(bf16[2,256,256]{2,1,0:T(8,128)(2,1)S(1)} %collective-permute-done.17.refs_0_), channel_id=1, source_target_pairs={{0,1},{1,0},{2,3},{3,2},{4,5},{5,4},{6,7},{7,6},{8,9},{9,8},{10,11... | collective-permute-start | bytes 786440 | tf_op jit(solution)/shard_map/ppermute | solution.py:309
  114.7 1.5 %collective-permute-start.29 = (bf16[2,256,256]{2,1,0:T(8,128)(2,1)S(1)}, bf16[2,256,256]{2,1,0:T(8,128)(2,1)S(1)}, u32[]{:S(2)}, u32[]{:S(2)}) collective-permute-start(bf16[2,256,256]{2,1,0:T(8,128)(2,1)S(1)} %collective-permute-done.18.refs_1_), channel_id=1, source_target_pairs={{0,1},{1,0},{2,3},{3,2},{4,5},{5,4},{6,7},{7,6},{8,9},{9,8},{10,11... | collective-permute-start | bytes 786440 | tf_op jit(solution)/shard_map/ppermute | solution.py:309
